TPU v7x, 32 devices: a whole 2x2x4 slice. The times are simulated.
32 devices in a mesh: groups: 2 (over y), expert: 4 (over z), dp: 4 (over x, core).
Axes of the slice: x: 2, y: 2, z: 4, core: 2. Of those that a mesh axis runs over, the one named last changes fastest.
Arguments:
- tokens: bfloat16 [4096, 3584], P(('groups', 'expert', 'dp')), parts along dimension 0, may hold values from -6 to 6
- w_gate: bfloat16 [3584, 8192], P(None, 'expert'), may hold values from -0.09375 to 0.09375
- w_up: bfloat16 [3584, 8192], P(None, 'expert'), may hold values from -0.09375 to 0.09375
- w_down: bfloat16 [8192, 3584], P('expert'), may hold values from -0.125 to 0.125
- w_latent: bfloat16 [3584, 576], P('expert'), may hold values from -0.09375 to 0.09375
- latent_gain: float32 [512], replicated, may hold values from 0.1 to 1.9
- route_ids: int32 [4096, 8], P(('groups', 'expert', 'dp')), parts along dimension 0, may hold values from 0 to 255, all different within a row; in each aligned block of 128 rows (0 to 127, 128 to 255, ...) at most 8 rows name the same one
- route_weight: float32 [4096, 8], P(('groups', 'expert', 'dp')), parts along dimension 0, may hold values from 0.5 to 2
- old_latents: bfloat16 [256, 9216], P(('groups', 'expert', 'dp')), parts along dimension 0, may hold values from -6 to 6
- survive: int32 [256], P(('groups', 'expert', 'dp')), parts along dimension 0, may hold values from 0 to 1, as said below
- old_target: int32 [256], P(('groups', 'expert', 'dp')), parts along dimension 0, may hold values from -1 to 127, as said below
Outputs:
- moe_out: bfloat16 [4096, 3584], P(('groups', 'expert', 'dp')), parts along dimension 0
- latents: bfloat16 [256, 9216], P(('groups', 'expert', 'dp')), parts along dimension 0
There are 2 independent parts, one for each index of `groups`. A program takes and returns all parts, laid end to end along the dimension named above; an argument that names none is the same for every part. Nothing has to cross between parts.
Inputs may be any that keep to these rules, and one draw needn't show every extreme that they name: `route_ids`: in each aligned block of 128 rows (the rows of one device) no expert is named more than 8 times. survive[j] = 1 exactly where some entry of old_target equals j. `old_target`: entries other than -1 are distinct; the new page of an old page lies on a device with the same dp index; of one device's pages, at most 2 go to any one device.
All inputs are finite; a program needn't handle non-finite values.
Results may differ from a plain program's by a relative error of at most 0.0085.
Values may be sent and summed in bfloat16 or wider, within the bound.
No kernel may reach another device: no remote copies, remote signals or barrier semaphores. Data moves between devices by JAX's collectives and lax.ppermute only.
A program may use at most 128 MiB of HBM per device.

v0:
```python
import jax
import jax.numpy as jnp
from jax import lax
from jax.sharding import PartitionSpec as P

FF = 2048
EXPERTS = 4
KV = 512
CAP = 8


EPS = 1e-06


def rebuild_latents(tokens, w_latent, latent_gain):
    projected = jnp.dot(
        tokens,
        lax.all_gather(w_latent, "expert", axis=0, tiled=True),
        preferred_element_type=jnp.float32,
    )
    nope_part = projected[:, :KV]
    inv_rms = lax.rsqrt(jnp.mean(nope_part * nope_part, axis=1, keepdims=True) + EPS)
    return jnp.concatenate([nope_part * inv_rms * latent_gain, projected[:, KV:]], axis=1).astype(
        jnp.bfloat16
    )


def moved_pages(old_latents, survive, old_target, rebuilt):
    peer_count = lax.axis_size("expert")
    dp_count = lax.axis_size("dp")
    page_count = old_latents.shape[0]
    per_pair = max(1, page_count // peer_count)
    slot_ids = jnp.arange(page_count, dtype=jnp.int32)
    peer_ids = jnp.arange(peer_count, dtype=jnp.int32)
    rank_ids = jnp.arange(per_pair, dtype=jnp.int32)
    valid_out = old_target >= 0
    target_peer = old_target // page_count // dp_count
    target_slot = jnp.where(valid_out, old_target % page_count + 1, 0).astype(jnp.float32)
    same_peer = (target_peer[:, None] == target_peer[None, :]) & valid_out[None, :]
    earlier = slot_ids[None, :] < slot_ids[:, None]
    out_rank = jnp.sum((same_peer & earlier).astype(jnp.int32), axis=1)
    select = (
        valid_out[None, None, :]
        & (target_peer[None, None, :] == peer_ids[:, None, None])
        & (out_rank[None, None, :] == rank_ids[None, :, None])
    )
    select = select.reshape(peer_count * per_pair, page_count)
    outgoing = jnp.dot(
        select.astype(jnp.bfloat16), old_latents, preferred_element_type=jnp.float32
    ).astype(jnp.bfloat16)
    slot_tags = jnp.dot(
        select.astype(jnp.float32), target_slot, precision=lax.Precision.HIGHEST
    ).astype(jnp.bfloat16)
    arrived, arrived_tags = (
        lax.all_to_all(
            outgoing.reshape(peer_count, per_pair, -1),
            "expert",
            split_axis=0,
            concat_axis=0,
            tiled=True,
        ),
        lax.all_to_all(
            slot_tags.reshape(peer_count, per_pair),
            "expert",
            split_axis=0,
            concat_axis=0,
            tiled=True,
        ),
    )
    tag_values = arrived_tags.reshape(peer_count * per_pair).astype(jnp.float32)
    chooser = (tag_values[None, :] == (slot_ids + 1).astype(jnp.float32)[:, None]).astype(
        jnp.bfloat16
    )
    carried = jnp.dot(
        chooser, arrived.reshape(peer_count * per_pair, -1), preferred_element_type=jnp.float32
    ).astype(jnp.bfloat16)
    return jnp.where((survive > 0)[:, None], carried, rebuilt)


def route_tables(route_ids, route_weight):
    token_count, top_count = route_ids.shape
    flat_ids = route_ids.reshape(-1)
    onehot = (flat_ids[:, None] == jnp.arange(EXPERTS, dtype=jnp.int32)[None, :]).astype(jnp.int32)
    slot_rank = jnp.sum((jnp.cumsum(onehot, axis=0) - onehot) * onehot, axis=1)
    slot_index = jnp.where(flat_ids < EXPERTS, flat_ids * CAP + slot_rank, -1)
    matches = slot_index[:, None] == jnp.arange(EXPERTS * CAP, dtype=jnp.int32)[None, :]
    matches = matches.reshape(token_count, top_count, EXPERTS * CAP)
    placing = jnp.sum(matches.astype(jnp.float32), axis=1).astype(jnp.bfloat16)
    mixing = jnp.sum(matches.astype(jnp.float32) * route_weight[:, :, None], axis=1)
    return (placing, mixing)


def expert_rows(received, w_gate, w_up, w_down, per_dev):
    unit_count = w_gate.shape[1] // per_dev
    gate_w = w_gate.reshape(w_gate.shape[0], per_dev, unit_count)
    up_w = w_up.reshape(w_up.shape[0], per_dev, unit_count)
    down_w = w_down.reshape(per_dev, unit_count, w_down.shape[1])
    gate_value = jnp.einsum("spkd,dpf->spkf", received, gate_w, preferred_element_type=jnp.float32)
    up_value = jnp.einsum("spkd,dpf->spkf", received, up_w, preferred_element_type=jnp.float32)
    hidden = (jax.nn.silu(gate_value) * up_value).astype(jnp.bfloat16)
    return jnp.einsum("spkf,pfd->spkd", hidden, down_w, preferred_element_type=jnp.float32)


def shards(
    tokens,
    w_gate,
    w_up,
    w_down,
    w_latent,
    latent_gain,
    route_ids,
    route_weight,
    old_latents,
    survive,
    old_target,
):
    rebuilt = rebuild_latents(tokens, w_latent, latent_gain).reshape(old_latents.shape[0], -1)
    latents = moved_pages(old_latents, survive, old_target, rebuilt)
    column_count = w_gate.shape[1]
    per_dev = max(1, column_count // FF)
    span_size = max(1, FF // column_count)
    group_count = EXPERTS // per_dev
    model_width = tokens.shape[1]
    placing, mixing = route_tables(route_ids, route_weight)
    outgoing = jnp.einsum("te,td->ed", placing, tokens, preferred_element_type=jnp.float32).astype(
        jnp.bfloat16
    )
    grouped = outgoing.reshape(group_count, per_dev, CAP, model_width)
    sent_rows = jnp.repeat(grouped, span_size, axis=0)
    partial_value = expert_rows(
        lax.all_to_all(sent_rows, "expert", split_axis=0, concat_axis=0, tiled=True),
        w_gate,
        w_up,
        w_down,
        per_dev,
    )
    returned = lax.all_to_all(
        partial_value.astype(jnp.bfloat16), "expert", split_axis=0, concat_axis=0, tiled=True
    ).astype(partial_value.dtype)
    summed = jnp.sum(returned.reshape(group_count, span_size, per_dev, CAP, model_width), axis=1)
    expert_out = summed.reshape(EXPERTS * CAP, model_width)
    moe_out = jnp.dot(mixing, expert_out, precision=lax.Precision.HIGHEST).astype(jnp.bfloat16)
    return (moe_out, latents)


def solution(mesh):
    in_specs = (
        P(("groups", "expert", "dp"), None),
        P(None, "expert"),
        P(None, "expert"),
        P("expert", None),
        P("expert", None),
        P(),
        P(("groups", "expert", "dp"), None),
        P(("groups", "expert", "dp"), None),
        P(("groups", "expert", "dp"), None),
        P(("groups", "expert", "dp")),
        P(("groups", "expert", "dp")),
    )
    out_specs = (P(("groups", "expert", "dp"), None), P(("groups", "expert", "dp"), None))
    return jax.shard_map(shards, mesh=mesh, in_specs=in_specs, out_specs=out_specs, check_vma=False)
```

profile of v0, /device:TPU:0, one launch (start us, length us, event | category | flops | bytes accessed | tf_op | source)
XLA Modules:
  0.0 114.4 jit_solution(4820817702562104234)
XLA Ops:
  7.2 0.0 copy-start
  7.2 0.0 all-gather.2.cloned.1.call-start
  7.2 0.7 all-gather.2.cloned.1.call-update
  7.9 0.8 copy.46
  8.7 0.1 eq.107
  8.8 0.1 eq.103
  8.9 1.1 %reduce-window.6 = s32[4,8,128]{2,1,0:T(8,128)S(1)} reduce-window(s32[4,8,128]{2,1,0:T(8,128)S(1)} %fusion.45, s32[]{:T(128)} %constant.50.clone.1), window={size=1x1x128 pad=0_0x0_0x127_0}, to_apply=%region_0.0 | reduce-window | flops 520192 | bytes 32772 | tf_op jit(solution)/shard_map/reduce-window
  10.0 0.2 slice_reduce_fusion
  10.3 0.2 reduce-window.9
  10.4 0.1 add_bitcast_fusion
  10.6 0.1 reduce_sum.52
  10.7 0.7 add_select_fusion
  11.4 0.7 convert_reduce_fusion
  12.1 0.0 copy-done
  12.1 1.0 fusion.10
  13.1 6.3 %all-to-all-start = ((bf16[4,1,8,3584]{3,2,1,0:T(8,128)(2,1)}), bf16[4,1,8,3584]{3,2,1,0:T(8,128)(2,1)S(1)}, u32[]{:S(2)}, u32[]{:S(2)}) async-start(bf16[4,1,8,3584]{3,2,1,0:T(8,128)(2,1)} %fusion.10), calls=%async_computation | async-start | bytes 458752 | tf_op jit(solution)/shard_map/all_to_all | solution.py:131
  19.4 0.7 broadcast_compare_fusion
  20.1 0.7 and_select_fusion.1
  20.7 0.2 convert_reduce_fusion.1
  21.0 0.8 fusion.31
  21.8 0.7 all_to_all.20
  22.5 1.1 convolution_convert_fusion.1
  23.5 0.7 reshape.180
  24.3 8.4 %all-to-all-done = bf16[4,1,8,3584]{3,2,1,0:T(8,128)(2,1)S(1)} async-done(((bf16[4,1,8,3584]{3,2,1,0:T(8,128)(2,1)}), bf16[4,1,8,3584]{3,2,1,0:T(8,128)(2,1)S(1)}, u32[]{:S(2)}, u32[]{:S(2)}) %all-to-all-start) | async-done | bytes 229408 | tf_op jit(solution)/shard_map/all_to_all | solution.py:131
  32.6 6.4 %all-to-all-start.2 = ((bf16[4,1,2]{2,1,0:T(2,128)(2,1)}), bf16[4,1,2]{2,1,0:T(2,128)(2,1)S(1)}, u32[]{:S(2)}, u32[]{:S(2)}) async-start(bf16[4,1,2]{2,1,0:T(2,128)(2,1)} %all_to_all.20), calls=%async_computation.2 | async-start | bytes 4096 | tf_op jit(solution)/shard_map/all_to_all | solution.py:62
  39.0 7.7 %fusion.14 = f32[4,1,8,2048]{3,2,0,1:T(8,128)S(1)} fusion(bf16[3584,2048]{1,0:T(8,128)(2,1)} %param.12, bf16[4,1,8,3584]{3,2,1,0:T(8,128)(2,1)S(1)} %all-to-all-done), kind=kOutput, calls=%fused_computation.14 | convolution fusion | flops 469762048 | bytes 15171584 | tf_op jit(solution)/shard_map/spkd,dpf->spkf/dot_general | solution.py:98
  46.7 0.0 all-to-all-done.2
  46.8 5.2 %all-to-all-start.3 = ((bf16[4,2,9216]{2,1,0:T(2,128)(2,1)}), bf16[4,2,9216]{2,1,0:T(2,128)(2,1)S(1)}, u32[]{:S(2)}, u32[]{:S(2)}) async-start(bf16[4,2,9216]{2,1,0:T(2,128)(2,1)} %reshape.180), calls=%async_computation.3 | async-start | bytes 294912 | tf_op jit(solution)/shard_map/all_to_all | solution.py:55
  51.9 0.0 copy-start.2
  51.9 0.0 copy-start.1
  51.9 15.1 %fusion.11 = bf16[4,1,8,3584]{3,2,1,0:T(8,128)(2,1)} fusion(bf16[2048,3584]{1,0:T(8,128)(2,1)} %param.14, bf16[3584,2048]{1,0:T(8,128)(2,1)} %param.13, f32[4,1,8,2048]{3,2,0,1:T(8,128)S(1)} %fusion.14, bf16[4,1,8,3584]{3,2,1,0:T(8,128)(2,1)S(1)} %all-to-all-done), kind=kOutput, calls=%fused_computation.13 | convolution fusion | flops 940032000 | bytes 30081024 | tf_op jit(solution)/shard_map/spkf,pfd->spkd/dot_general | solution.py:101
  67.1 0.0 all-to-all-done.3
  67.1 5.1 %all-to-all-start.1 = ((bf16[4,1,8,3584]{3,2,1,0:T(8,128)(2,1)}), bf16[4,1,8,3584]{3,2,1,0:T(8,128)(2,1)S(1)}, u32[]{:S(2)}, u32[]{:S(2)}) async-start(bf16[4,1,8,3584]{3,2,1,0:T(8,128)(2,1)} %fusion.11), calls=%async_computation.1 | async-start | bytes 458752 | tf_op jit(solution)/shard_map/all_to_all | solution.py:137
  72.2 0.0 copy-done.2
  72.2 0.1 reshape.182
  72.3 0.1 reshape.181
  72.3 15.3 %all-to-all-done.1 = bf16[4,1,8,3584]{3,2,1,0:T(8,128)(2,1)S(1)} async-done(((bf16[4,1,8,3584]{3,2,1,0:T(8,128)(2,1)}), bf16[4,1,8,3584]{3,2,1,0:T(8,128)(2,1)S(1)}, u32[]{:S(2)}, u32[]{:S(2)}) %all-to-all-start.1) | async-done | bytes 229408 | tf_op jit(solution)/shard_map/all_to_all | solution.py:137
  87.7 1.8 %convolution_convert_fusion.2 = bf16[128,3584]{1,0:T(8,128)(2,1)} fusion(f32[128,32]{0,1:T(8,128)S(1)} %get-tuple-element.3, bf16[4,1,8,3584]{3,2,1,0:T(8,128)(2,1)S(1)} %all-to-all-done.1), kind=kOutput, calls=%fused_computation.9 | convolution fusion | flops 176619520 | bytes 1163264 | tf_op jit(solution)/shard_map/dot_general | solution.py:142
  89.5 13.1 %all-gather.2.cloned.1.call-done = bf16[3584,576]{0,1:T(8,128)(2,1)} async-done(((bf16[896,576]{0,1:T(8,128)(2,1)}), bf16[3584,576]{0,1:T(8,128)(2,1)}) %all-gather.2.cloned.1.call-update) | async-done | bytes 4128784 | tf_op jit(solution)/shard_map/all_gather | solution.py:18
  102.7 3.4 %fusion.62 = f32[128,576]{0,1:T(8,128)S(1)} fusion(bf16[128,3584]{1,0:T(8,128)(2,1)S(1)} %copy-done, bf16[3584,576]{0,1:T(8,128)(2,1)} %all-gather.2.cloned.1.call-done), kind=kOutput, calls=%fused_computation.82 | convolution fusion | flops 528482304 | bytes 5341184 | tf_op jit(solution)/shard_map/dot_general | solution.py:16
  106.0 0.1 multiply_reduce_fusion
  106.1 0.0 copy-done.1
  106.2 0.1 multiply_convert_fusion
  106.3 0.2 copy.52
  106.5 0.2 convert_element_type.95
  106.6 0.9 fusion.6
  (13 shorter events, 0.2 us)
Async XLA Ops:
  7.2 5.0 %copy-start = (bf16[128,3584]{1,0:T(8,128)(2,1)S(1)}, bf16[128,3584]{1,0:T(8,128)(2,1)}, u32[]{:S(2)}) copy-start(bf16[128,3584]{1,0:T(8,128)(2,1)} %param.11) | copy-start | bytes 2752516
  7.2 95.5 %all-gather.2.cloned.1.call-start = ((), (), s32[]{:S(2)}) async-start(), calls=%async_computation.4 | async-start | bytes 5160960 | tf_op jit(solution)/shard_map/all_gather | solution.py:18
  13.1 19.5 %all-to-all-start = ((bf16[4,1,8,3584]{3,2,1,0:T(8,128)(2,1)}), bf16[4,1,8,3584]{3,2,1,0:T(8,128)(2,1)S(1)}, u32[]{:S(2)}, u32[]{:S(2)}) async-start(bf16[4,1,8,3584]{3,2,1,0:T(8,128)(2,1)} %fusion.10), calls=%async_computation | async-start | bytes 458752 | tf_op jit(solution)/shard_map/all_to_all | solution.py:131
  32.6 14.1 %all-to-all-start.2 = ((bf16[4,1,2]{2,1,0:T(2,128)(2,1)}), bf16[4,1,2]{2,1,0:T(2,128)(2,1)S(1)}, u32[]{:S(2)}, u32[]{:S(2)}) async-start(bf16[4,1,2]{2,1,0:T(2,128)(2,1)} %all_to_all.20), calls=%async_computation.2 | async-start | bytes 4096 | tf_op jit(solution)/shard_map/all_to_all | solution.py:62
  46.8 20.3 %all-to-all-start.3 = ((bf16[4,2,9216]{2,1,0:T(2,128)(2,1)}), bf16[4,2,9216]{2,1,0:T(2,128)(2,1)S(1)}, u32[]{:S(2)}, u32[]{:S(2)}) async-start(bf16[4,2,9216]{2,1,0:T(2,128)(2,1)} %reshape.180), calls=%async_computation.3 | async-start | bytes 294912 | tf_op jit(solution)/shard_map/all_to_all | solution.py:55
  51.9 20.2 %copy-start.2 = (s32[8]{0:T(128)S(1)}, s32[8]{0:T(128)}, u32[]{:S(2)}) copy-start(s32[8]{0:T(128)} %param.20) | copy-start | bytes 100
  51.9 54.2 %copy-start.1 = (f32[512]{0:T(512)S(1)}, f32[512]{0:T(512)}, u32[]{:S(2)}) copy-start(f32[512]{0:T(512)} %param.16) | copy-start | bytes 6148
  67.1 20.6 %all-to-all-start.1 = ((bf16[4,1,8,3584]{3,2,1,0:T(8,128)(2,1)}), bf16[4,1,8,3584]{3,2,1,0:T(8,128)(2,1)S(1)}, u32[]{:S(2)}, u32[]{:S(2)}) async-start(bf16[4,1,8,3584]{3,2,1,0:T(8,128)(2,1)} %fusion.11), calls=%async_computation.1 | async-start | bytes 458752 | tf_op jit(solution)/shard_map/all_to_all | solution.py:137
Sparse Core Ops, SparseCore 0:
  9.6 92.9 all-gather.1
where the time goes:
time: 115 us; the launch traced here: 114 us
  waiting for transfers between devices  37.5 us (33%)
  matrix products  31.7 us (28%)
  starting transfers between devices  23.1 us (20%)
  between operations  14.2 us (12%)
  other arithmetic  4.68 us (4%)
  local copies, waits for them, and re-layouts  3.24 us (3%)
    all_to_all x1, waiting for transfers between devices, shards(): lax.all_to_all(partial_value.astype(jnp.bfloat16), 'expert', split_axis=0...  15.3 us
    dot_general x1, matrix products, expert_rows(): jnp.einsum('spkf,pfd->spkd', hidden, down_w, preferred_element_type=jnp.f...  15.1 us
    all_gather x1, waiting for transfers between devices, rebuild_latents(): lax.all_gather(w_latent, 'expert', axis=0, tiled=True)  13.1 us
    all_to_all x1, waiting for transfers between devices, shards(): lax.all_to_all(sent_rows, 'expert', split_axis=0, concat_axis=0, tiled=True)  8.36 us
    dot_general x1, matrix products, expert_rows(): jnp.einsum('spkd,dpf->spkf', received, gate_w, preferred_element_type=jnp...  7.7 us
    all_to_all x1, starting transfers between devices, moved_pages(): lax.all_to_all(slot_tags.reshape(peer_count, per_pair), 'expert', split_a...  6.43 us
    all_to_all x1, starting transfers between devices, shards(): lax.all_to_all(sent_rows, 'expert', split_axis=0, concat_axis=0, tiled=True)  6.31 us
    all_to_all x1, starting transfers between devices, moved_pages(): lax.all_to_all(outgoing.reshape(peer_count, per_pair, -1), 'expert', spli...  5.18 us
  transfers between devices with their start and end apart: 5, of which 3 were waited for; matrix products, arithmetic and copies ran while one was open for 30% of the time, Pallas kernels for 0%

commit v1 on v0

--- a/solution.py
+++ b/solution.py
@@ -1,15 +1,455 @@
+import functools
+
 import jax
 import jax.numpy as jnp
 from jax import lax
+from jax.experimental import pallas as pl
+from jax.experimental.pallas import tpu as pltpu
 from jax.sharding import PartitionSpec as P
 
 FF = 2048
 EXPERTS = 4
 KV = 512
 CAP = 8
+PER_PAIR = 2
+SPLIT = 4
+LANES = 128
+ROWS = 16
 
 
 EPS = 1e-06
+VMEM = pltpu.VMEM
+SMEM = pltpu.SMEM
+CHUNK = 512
+NT = (((1,), (1,)), ((), ()))
+TN = (((0,), (0,)), ((), ()))
+
+
+def xor_pairs(count, bit):
+    return [(at, at ^ bit) for at in range(count)]
+
+
+def plane_pairs(group_count, dp_count, core_zero_along_x):
+    pairs = []
+    for group in range(group_count):
+        for dp in range(dp_count):
+            along_x = (dp % 2 == 0) == core_zero_along_x
+            to_group, to_dp = (group, dp ^ 2) if along_x else (group ^ 1, dp)
+            pairs.append((group * dp_count + dp, to_group * dp_count + to_dp))
+    return pairs
+
+
+def piece_rows(width):
+    chip = width // 4
+    core = -(-(chip // 2) // ROWS) * ROWS
+    return chip, core
+
+
+def open_kernel(page_span, *refs):
+    sources, latent_ref, outs = refs[:5], refs[5], refs[6:]
+    sends, mixing_ref, pages = outs[:EXPERTS], outs[EXPERTS], outs[EXPERTS + 1 : 2 * EXPERTS + 1]
+    piece_ref, across_ref = outs[2 * EXPERTS + 1 : 2 * EXPERTS + 3]
+    *held, sem, sems = outs[2 * EXPERTS + 3 :]
+    ids_ref, weight_ref, tokens_ref, old_ref, target_ref = held
+    copies = [
+        pltpu.make_async_copy(source, target, sems.at[at])
+        for at, (source, target) in enumerate(zip(sources, held))
+    ]
+    for copy in copies:
+        copy.start()
+    group, me, dp = (lax.axis_index(axis) for axis in ("groups", "expert", "dp"))
+    chip_rows, core_rows = piece_rows(latent_ref.shape[0])
+    start = (group * 2 + dp // 2) * chip_rows + (dp % 2) * (chip_rows - core_rows)
+    piece = pltpu.make_async_copy(
+        latent_ref.at[pl.ds(pl.multiple_of(start, ROWS), core_rows)], piece_ref, sem
+    )
+    piece.start()
+    for copy in copies:
+        copy.wait()
+    shard = latent_ref.shape[1]
+    for half, bit in enumerate((1, 3)):
+        columns = pl.ds(pl.multiple_of((me ^ bit) * shard, LANES), shard)
+        across_ref[:, half * shard : (half + 1) * shard] = tokens_ref[:, columns]
+    top_count, token_count = ids_ref.shape
+    slot_count = EXPERTS * CAP
+    row = lax.broadcasted_iota(jnp.int32, (slot_count, token_count), 0)
+    expert_of = (row >> 3) ^ me
+    chosen = jnp.zeros((slot_count, token_count), jnp.float32)
+    weight = jnp.zeros((slot_count, token_count), jnp.float32)
+    for at in range(top_count):
+        named = ids_ref[at : at + 1, :] == expert_of
+        chosen = jnp.where(named, 1.0, chosen)
+        weight = jnp.where(named, weight_ref[at : at + 1, :], weight)
+    before = lax.broadcasted_iota(jnp.int32, (token_count, token_count), 0)
+    token = lax.broadcasted_iota(jnp.int32, (token_count, token_count), 1)
+    earlier = jnp.where(before < token, 1.0, 0.0).astype(jnp.bfloat16)
+    rank = jnp.dot(chosen.astype(jnp.bfloat16), earlier, preferred_element_type=jnp.float32)
+    placed = jnp.where(rank == (row & 7).astype(jnp.float32), chosen, 0.0)
+    mixing_ref[...] = placed * weight
+    outgoing = jnp.dot(
+        placed.astype(jnp.bfloat16), tokens_ref[...], preferred_element_type=jnp.float32
+    )
+    for at in range(EXPERTS):
+        sends[at][...] = outgoing[at * CAP : (at + 1) * CAP].astype(jnp.bfloat16)
+    page_count, width = old_ref.shape
+    row_count = EXPERTS * PER_PAIR * SPLIT
+    out_row = lax.broadcasted_iota(jnp.int32, (row_count, page_count), 0)
+    old_page = lax.broadcasted_iota(jnp.int32, (row_count, page_count), 1)
+    tag_row = lax.broadcasted_iota(jnp.int32, (row_count, LANES), 0)
+    select = [jnp.zeros((row_count, page_count), jnp.float32) for _ in range(SPLIT)]
+    tags = jnp.zeros((row_count, LANES), jnp.float32)
+    targets = [target_ref[at] for at in range(page_count)]
+    peers = [jnp.where(target >= 0, target // page_span, -1) for target in targets]
+    for at in range(page_count):
+        rank_at = jnp.int32(0)
+        for first in range(at):
+            rank_at = rank_at + jnp.where(peers[first] == peers[at], 1, 0)
+        row_at = ((peers[at] ^ me) * PER_PAIR + rank_at) * SPLIT
+        row_at = jnp.where(peers[at] >= 0, row_at, -SPLIT)
+        for part in range(SPLIT):
+            here = (out_row == row_at + part) & (old_page == at)
+            select[part] = jnp.where(here, 1.0, select[part])
+        slot_tag = (targets[at] % page_count + 1).astype(jnp.float32)
+        tags = jnp.where((tag_row >= row_at) & (tag_row < row_at + SPLIT), slot_tag, tags)
+    width = width // SPLIT
+    moved = jnp.zeros((row_count, width), jnp.float32)
+    for part in range(SPLIT):
+        columns = slice(part * width, (part + 1) * width)
+        moved = moved + jnp.dot(
+            select[part].astype(jnp.bfloat16),
+            old_ref[:, columns],
+            preferred_element_type=jnp.float32,
+        )
+    for at in range(EXPERTS):
+        rows = slice(at * PER_PAIR * SPLIT, (at + 1) * PER_PAIR * SPLIT)
+        pages[at][:, :width] = moved[rows].astype(jnp.bfloat16)
+        pages[at][:, width:] = tags[rows].astype(jnp.bfloat16)
+    piece.wait()
+
+
+def open_work(ids, weights, tokens, old_latents, latent, old_target):
+    token_count, model_width = tokens.shape
+    page_count, page_width = old_latents.shape
+    send = jax.ShapeDtypeStruct((CAP, model_width), jnp.bfloat16)
+    mixing = jax.ShapeDtypeStruct((EXPERTS * CAP, token_count), jnp.float32)
+    page = jax.ShapeDtypeStruct((PER_PAIR * SPLIT, page_width // SPLIT + LANES), jnp.bfloat16)
+    piece = jax.ShapeDtypeStruct((piece_rows(latent.shape[0])[1], latent.shape[1]), jnp.bfloat16)
+    across = jax.ShapeDtypeStruct((token_count, 2 * latent.shape[1]), jnp.bfloat16)
+    spec = pl.BlockSpec(memory_space=VMEM)
+    inputs = [
+        pltpu.with_memory_space_constraint(value, pltpu.HBM)
+        for value in (ids, weights, tokens, old_latents, old_target, latent)
+    ]
+    results = pl.pallas_call(
+        functools.partial(open_kernel, page_count * lax.axis_size("dp")),
+        out_shape=(send,) * EXPERTS + (mixing,) + (page,) * EXPERTS + (piece, across),
+        in_specs=[pl.BlockSpec(memory_space=pltpu.HBM)] * 6,
+        out_specs=(spec,) * (2 * EXPERTS + 3),
+        scratch_shapes=[VMEM(value.shape, value.dtype) for value in inputs[:4]]
+        + [
+            SMEM(old_target.shape, old_target.dtype),
+            pltpu.SemaphoreType.DMA,
+            pltpu.SemaphoreType.DMA((5,)),
+        ],
+        compiler_params=pltpu.CompilerParams(vmem_limit_bytes=8 << 20),
+        cost_estimate=pl.CostEstimate(
+            flops=20_000_000_000, bytes_accessed=2 << 20, transcendentals=0
+        ),
+        name="open",
+    )(*inputs)
+    sends, mixing, rest = results[:EXPERTS], results[EXPERTS], results[EXPERTS + 1 :]
+    return sends, mixing, rest[:EXPERTS], rest[EXPERTS], rest[EXPERTS + 1]
+
+
+def stacked_rows(refs):
+    return jnp.concatenate([ref[...].astype(jnp.float32) for ref in refs], axis=0).astype(
+        jnp.bfloat16
+    )
+
+
+def gate_up_kernel(*refs):
+    rows, (gate_ref, up_ref) = refs[:EXPERTS], refs[EXPERTS : EXPERTS + 2]
+    hidden_ref = refs[-1]
+    block = stacked_rows(rows)
+    step = CHUNK // 2
+    for at in range(0, gate_ref.shape[1], step):
+        columns = slice(at, at + step)
+        gate = jnp.dot(block, gate_ref[:, columns], preferred_element_type=jnp.float32)
+        up = jnp.dot(block, up_ref[:, columns], preferred_element_type=jnp.float32)
+        hidden_ref[:, columns] = (gate / (1.0 + jnp.exp(-gate)) * up).astype(jnp.bfloat16)
+
+
+def gate_up(rows, w_gate, w_up, after):
+    spec, unread = pl.BlockSpec(memory_space=VMEM), pl.BlockSpec(memory_space=pl.ANY)
+    held = [pltpu.with_memory_space_constraint(w, VMEM) for w in (w_gate, w_up)]
+    model_width, unit_count = w_gate.shape
+    row_count = EXPERTS * CAP
+    return pl.pallas_call(
+        gate_up_kernel,
+        out_shape=jax.ShapeDtypeStruct((row_count, unit_count), jnp.bfloat16),
+        in_specs=[spec] * (EXPERTS + 2) + [unread] * len(after),
+        out_specs=spec,
+        compiler_params=pltpu.CompilerParams(vmem_limit_bytes=4 << 20),
+        cost_estimate=pl.CostEstimate(
+            flops=4 * row_count * model_width * unit_count,
+            bytes_accessed=4 * model_width * unit_count,
+            transcendentals=row_count * unit_count,
+        ),
+        name="gate_up",
+    )(*rows, *held, *after)
+
+
+def down_kernel(hidden_ref, down_ref, *refs):
+    pages, outs = refs[:EXPERTS], refs[-EXPERTS:]
+    model_width = down_ref.shape[1]
+    for peer in range(EXPERTS):
+        outs[peer][:, model_width:] = pages[peer][...]
+    for at in range(0, down_ref.shape[1], CHUNK):
+        columns = slice(at, at + CHUNK)
+        result = jnp.dot(
+            hidden_ref[...], down_ref[:, columns], preferred_element_type=jnp.float32
+        )
+        for peer in range(EXPERTS):
+            part = result[peer * CAP : (peer + 1) * CAP]
+            outs[peer][:, columns] = part.astype(jnp.bfloat16)
+
+
+def down(hidden, w_down, pages, after):
+    spec, unread = pl.BlockSpec(memory_space=VMEM), pl.BlockSpec(memory_space=pl.ANY)
+    unit_count, model_width = w_down.shape
+    return pl.pallas_call(
+        down_kernel,
+        out_shape=(jax.ShapeDtypeStruct((CAP, model_width + pages[0].shape[1]), jnp.bfloat16),)
+        * EXPERTS,
+        in_specs=[spec] * (2 + EXPERTS) + [unread] * len(after),
+        out_specs=(spec,) * EXPERTS,
+        compiler_params=pltpu.CompilerParams(vmem_limit_bytes=4 << 20),
+        cost_estimate=pl.CostEstimate(
+            flops=2 * EXPERTS * CAP * model_width * unit_count,
+            bytes_accessed=2 * model_width * unit_count,
+            transcendentals=0,
+        ),
+        name="down",
+    )(hidden, pltpu.with_memory_space_constraint(w_down, VMEM), *pages, *after)
+
+
+def combine_kernel(mixing_ref, *refs):
+    rows, out_ref = refs[:EXPERTS], refs[EXPERTS]
+    block = stacked_rows(rows)
+    mixing = mixing_ref[...]
+    high = mixing.astype(jnp.bfloat16).astype(jnp.float32)
+    mixing = jnp.concatenate([high, mixing - high], axis=0).astype(jnp.bfloat16)
+    block = jnp.concatenate([block, block], axis=0)
+    total = lax.dot_general(mixing, block, TN, preferred_element_type=jnp.float32)
+    out_ref[...] = total.astype(jnp.bfloat16)
+
+
+def combine(mixing, rows, model_width):
+    slot_count, token_count = mixing.shape
+    width = model_width // 2
+    columns = pl.BlockSpec((CAP, width), lambda at: (0, at))
+    return pl.pallas_call(
+        combine_kernel,
+        grid=(model_width // width,),
+        out_shape=jax.ShapeDtypeStruct((token_count, model_width), jnp.bfloat16),
+        in_specs=[pl.BlockSpec((slot_count, token_count), lambda at: (0, 0))] + [columns] * EXPERTS,
+        out_specs=pl.BlockSpec((token_count, width), lambda at: (0, at)),
+        compiler_params=pltpu.CompilerParams(vmem_limit_bytes=8 << 20),
+        cost_estimate=pl.CostEstimate(
+            flops=4 * token_count * slot_count * model_width,
+            bytes_accessed=3 * token_count * model_width,
+            transcendentals=0,
+        ),
+        name="combine",
+    )(mixing, *rows)
+
+
+def project_kernel(tokens_ref, theirs_ref, own_ref, *refs):
+    held, (mine_out, theirs_out), (far_ref, sems) = refs[:4], refs[-4:-2], refs[-2:]
+    group, me, dp = (lax.axis_index(axis) for axis in ("groups", "expert", "dp"))
+    shard = own_ref.shape[1]
+    chip_rows, core_rows = piece_rows(own_ref.shape[0])
+    chip, core = group * 2 + dp // 2, dp % 2
+
+    def copies_of(my_core):
+        copies = []
+        for which in range(2):
+            core_at = my_core if which == 0 else 1 - my_core
+            near_xor = 1 if core_at == 0 else 2
+            for at, chip_xor in enumerate((0, near_xor, 3 - near_xor, 3)):
+                buffer = held[2 * which + at // 2].at[at % 2]
+                skip = 0 if core_at == 0 else 2 * core_rows - chip_rows
+                start = (chip ^ chip_xor) * chip_rows + (0 if core_at == 0 else core_rows)
+                count = core_rows - skip
+                copies.append(
+                    pltpu.make_async_copy(
+                        buffer.at[pl.ds(skip, count)],
+                        far_ref.at[pl.ds(pl.multiple_of(start, ROWS), count)],
+                        sems.at[len(copies)],
+                    )
+                )
+        return copies
+
+    def on_each_core(act):
+        for my_core in range(2):
+
+            @pl.when(core == my_core)
+            def _(my_core=my_core):
+                for copy in copies_of(my_core):
+                    act(copy)
+
+    def part(left, weights_ref):
+        return lax.dot_general(left, weights_ref[...], NT, preferred_element_type=jnp.float32)
+
+    on_each_core(lambda copy: copy.start())
+    theirs_near = part(theirs_ref[:, :shard], own_ref)
+    mine_near = part(tokens_ref[:, pl.ds(pl.multiple_of(me * shard, LANES), shard)], own_ref)
+    on_each_core(lambda copy: copy.wait())
+    theirs_far = part(theirs_ref[:, shard:], far_ref)
+    theirs_out[...] = (theirs_near + theirs_far).astype(jnp.bfloat16)
+    far_columns = pl.ds(pl.multiple_of((me ^ 2) * shard, LANES), shard)
+    mine_out[...] = mine_near + part(tokens_ref[:, far_columns], far_ref)
+
+
+def project(tokens, theirs, own, held, after):
+    vmem, hbm = pl.BlockSpec(memory_space=VMEM), pl.BlockSpec(memory_space=pl.ANY)
+    token_count = tokens.shape[0]
+    width, shard = own.shape
+    return pl.pallas_call(
+        project_kernel,
+        out_shape=(
+            jax.ShapeDtypeStruct((token_count, width), jnp.float32),
+            jax.ShapeDtypeStruct((token_count, width), jnp.bfloat16),
+        ),
+        in_specs=[vmem] * 3 + [hbm] * (4 + len(after)),
+        out_specs=(vmem, vmem),
+        scratch_shapes=[VMEM((width, shard), jnp.bfloat16), pltpu.SemaphoreType.DMA((8,))],
+        compiler_params=pltpu.CompilerParams(vmem_limit_bytes=8 << 20),
+        cost_estimate=pl.CostEstimate(
+            flops=8 * token_count * shard * width, bytes_accessed=4 << 20, transcendentals=0
+        ),
+        name="project",
+    )(tokens, theirs, own, *held, *after)
+
+
+def finish_kernel(mine_ref, theirs_ref, gain_ref, survive_ref, *refs):
+    arrived, out_ref = refs[:EXPERTS], refs[EXPERTS]
+    page_count, page_width = out_ref.shape
+    projected = mine_ref[...] + theirs_ref[...].astype(jnp.float32)
+    nope_part = projected[:, :KV]
+    inv_rms = lax.rsqrt(jnp.mean(nope_part * nope_part, axis=1, keepdims=True) + EPS)
+    rebuilt = jnp.concatenate([nope_part * inv_rms * gain_ref[...], projected[:, KV:]], axis=1)
+    rebuilt = rebuilt.astype(jnp.bfloat16)
+    token_count, width = rebuilt.shape
+    page_tokens = token_count // page_count
+    row = lax.broadcasted_iota(jnp.int32, (token_count, token_count), 0)
+    source = lax.broadcasted_iota(jnp.int32, (token_count, token_count), 1)
+    moves = source == (row % page_count) * page_tokens + row // page_count
+    ordered = jnp.dot(
+        jnp.where(moves, 1.0, 0.0).astype(jnp.bfloat16),
+        rebuilt,
+        preferred_element_type=jnp.float32,
+    )
+    columns = slice(arrived[0].shape[1] - LANES - page_width // SPLIT, None)
+    arrivals = jnp.concatenate([ref[:, columns].astype(jnp.float32) for ref in arrived], axis=0)
+    part_width = page_width // SPLIT
+    row_count = arrivals.shape[0]
+    slot = lax.broadcasted_iota(jnp.int32, (row_count, page_count), 1).astype(jnp.float32)
+    part_of = lax.broadcasted_iota(jnp.int32, (row_count, page_count), 0) % SPLIT
+    meant = arrivals[:, part_width : part_width + 1] == slot + 1.0
+    arrivals = arrivals[:, :part_width].astype(jnp.bfloat16)
+    carried = [
+        lax.dot_general(
+            jnp.where(meant & (part_of == part), 1.0, 0.0).astype(jnp.bfloat16),
+            arrivals,
+            TN,
+            preferred_element_type=jnp.float32,
+        )
+        for part in range(SPLIT)
+    ]
+    page_row = lax.broadcasted_iota(jnp.int32, (page_count, 2 * width), 0)
+    survives = jnp.zeros((page_count, 2 * width), jnp.int32)
+    for at in range(page_count):
+        survives = jnp.where(page_row == at, survive_ref[at], survives)
+    for at in range(0, page_tokens, 2):
+        fresh = jnp.concatenate(
+            [ordered[(at + half) * page_count : (at + half + 1) * page_count] for half in range(2)],
+            axis=1,
+        )
+        columns = slice(at * width, (at + 2) * width)
+        start = at * width % part_width
+        kept = carried[at * width // part_width][:, start : start + 2 * width]
+        chosen = jnp.where(survives > 0, kept, fresh)
+        out_ref[:, columns] = chosen.astype(jnp.bfloat16)
+
+
+def finish(mine, theirs, latent_gain, survive, arrived, page_count, page_width):
+    vmem = pl.BlockSpec(memory_space=VMEM)
+    return pl.pallas_call(
+        finish_kernel,
+        out_shape=jax.ShapeDtypeStruct((page_count, page_width), jnp.bfloat16),
+        in_specs=[vmem] * 3 + [pl.BlockSpec(memory_space=SMEM)] + [vmem] * EXPERTS,
+        out_specs=vmem,
+        compiler_params=pltpu.CompilerParams(vmem_limit_bytes=6 << 20),
+        cost_estimate=pl.CostEstimate(
+            flops=4 * mine.shape[0] ** 2 * mine.shape[1],
+            bytes_accessed=1 << 20,
+            transcendentals=mine.shape[0],
+        ),
+        name="finish",
+    )(mine, theirs, latent_gain.reshape(1, -1), survive, *arrived)
+
+
+def swap(value, axis, bit):
+    return lax.ppermute(value, axis, xor_pairs(lax.axis_size(axis), bit))
+
+
+def tied(value, *after):
+    return lax.optimization_barrier((value, *after))[0]
+
+
+def exchanged(values, axis="expert"):
+    return [values[0]] + [swap(values[bit], axis, bit) for bit in range(1, len(values))]
+
+
+def block_shards(
+    tokens,
+    w_gate,
+    w_up,
+    w_down,
+    w_latent,
+    latent_gain,
+    route_ids,
+    route_weight,
+    old_latents,
+    survive,
+    old_target,
+):
+    group_count, dp_count = lax.axis_size("groups"), lax.axis_size("dp")
+    plane = ("groups", "dp")
+    latent = w_latent.T
+    sends, mixing, pages, piece, across = open_work(
+        route_ids.T, route_weight.T, tokens, old_latents, latent, old_target
+    )
+    far_piece = swap(piece, "expert", 2)
+    received = exchanged(sends)
+    far_piece = tied(far_piece, received[1])
+    first = lax.ppermute(far_piece, plane, plane_pairs(group_count, dp_count, True))
+    theirs = swap(tied(across, *received[1:]), "expert", 1)
+    hidden = gate_up(received, w_gate, w_up, (far_piece,))
+    near = tied(jnp.stack([far_piece, first]), hidden)
+    far = lax.ppermute(near, plane, plane_pairs(group_count, dp_count, False))
+    near_other = swap(near, "dp", 1)
+    results = down(hidden, w_down, pages, (near,))
+    returned = exchanged(results)
+    far_other = swap(far, "dp", 1)
+    mine, across_sums = project(
+        tokens, theirs, latent, (near, far, near_other, far_other), (results[0],)
+    )
+    their_sums = swap(across_sums, "expert", 1)
+    moe_out = combine(mixing, returned, tokens.shape[1])
+    latents = finish(mine, their_sums, latent_gain, survive, returned, *old_latents.shape)
+    return (moe_out, latents)
 
 
 def rebuild_latents(tokens, w_latent, latent_gain):
@@ -143,6 +583,11 @@
     return (moe_out, latents)
 
 
+def small_block(mesh):
+    sizes = (mesh.shape["groups"], mesh.shape["expert"], mesh.shape["dp"])
+    return sizes == (2, EXPERTS, 4)
+
+
 def solution(mesh):
     in_specs = (
         P(("groups", "expert", "dp"), None),
@@ -158,4 +603,5 @@
         P(("groups", "expert", "dp")),
     )
     out_specs = (P(("groups", "expert", "dp"), None), P(("groups", "expert", "dp"), None))
-    return jax.shard_map(shards, mesh=mesh, in_specs=in_specs, out_specs=out_specs, check_vma=False)
+    body = block_shards if small_block(mesh) else shards
+    return jax.shard_map(body, mesh=mesh, in_specs=in_specs, out_specs=out_specs, check_vma=False)

time: 115 us -> 57.2 us (0.50)
  matrix products: 31.7 us -> 0 us
  Pallas kernels: 0 us -> 16 us
  waiting for transfers between devices: 37.5 us -> 21.5 us
  between operations: 14.2 us -> 0.82 us
  other arithmetic: 4.68 us -> 0.03 us
  starting transfers between devices: 23.1 us -> 18.6 us
  local copies, waits for them, and re-layouts: 3.24 us -> 0.06 us
    dot_general x8 -> x0, matrix products: 31.7 us -> none  [the longest x1 15.1 us: expert_rows(): jnp.einsum('spkf,pfd->spkd', hidden, down_w, preferred_element_type=jnp.f...]
    all_to_all x4 -> x0, waiting for transfers between devices: 23.7 us -> none  [the longest x1 15.3 us: shards(): lax.all_to_all(partial_value.astype(jnp.bfloat16), 'expert', split_axis=0...]
    all_to_all x4 -> x0, starting transfers between devices: 23 us -> none  [the longest x1 6.43 us: moved_pages(): lax.all_to_all(slot_tags.reshape(peer_count, per_pair), 'expert', split_a...]
    ppermute x0 -> x13, waiting for transfers between devices: none -> 21.5 us  [the longest x11 16.9 us: swap(): return lax.ppermute(value, axis, xor_pairs(lax.axis_size(axis), bit))]
    ppermute x0 -> x13, starting transfers between devices: none -> 18.6 us  [the longest x11 15.2 us: swap(): return lax.ppermute(value, axis, xor_pairs(lax.axis_size(axis), bit))]
    pallas_call x0 -> x6, Pallas kernels: none -> 16 us  [the longest x1 5.26 us: gate_up(): pl.pallas_call(gate_up_kernel, out_shape=jax.ShapeDtypeStruct((row_count,...]
    all_gather x1 -> x0, waiting for transfers between devices: 13.1 us -> none  [rebuild_latents(): lax.all_gather(w_latent, 'expert', axis=0, tiled=True)]
    another operation x3 -> x1, other arithmetic: 1.46 us -> 0.03 us  [block_shards(): near = tied(jnp.stack([far_piece, first]), hidden)]
  transfers between devices with their start and end apart: 5 -> 13, of which waited for: 3 -> 7; matrix products, arithmetic and copies ran while one was open for 30% -> 0% of each run, Pallas kernels for 0% -> 16%
where the time goes in v1:
time: 57.2 us; the launch traced here: 57.1 us
  waiting for transfers between devices  21.5 us (38%)
  starting transfers between devices  18.6 us (33%)
  Pallas kernels  16 us (28%)
  between operations  0.82 us (1%)
    ppermute x11, waiting for transfers between devices, swap(): return lax.ppermute(value, axis, xor_pairs(lax.axis_size(axis), bit))  16.9 us
    ppermute x11, starting transfers between devices, swap(): return lax.ppermute(value, axis, xor_pairs(lax.axis_size(axis), bit))  15.2 us
    pallas_call x1, Pallas kernels, gate_up(): pl.pallas_call(gate_up_kernel, out_shape=jax.ShapeDtypeStruct((row_count,...  5.26 us
    ppermute x1, waiting for transfers between devices, block_shards(): far = lax.ppermute(near, plane, plane_pairs(group_count, dp_count, False))  4.63 us
    pallas_call x1, Pallas kernels, project(): pl.pallas_call(project_kernel, out_shape=(jax.ShapeDtypeStruct((token_cou...  3.11 us
    pallas_call x1, Pallas kernels, down(): pl.pallas_call(down_kernel, out_shape=(jax.ShapeDtypeStruct((CAP, model_w...  2.61 us
    pallas_call x1, Pallas kernels, open_work(): pl.pallas_call(functools.partial(open_kernel, page_count * lax.axis_size(...  2.02 us
    ppermute x1, starting transfers between devices, block_shards(): lax.ppermute(far_piece, plane, plane_pairs(group_count, dp_count, True))  1.84 us
  transfers between devices with their start and end apart: 13, of which 7 were waited for; matrix products, arithmetic and copies ran while one was open for 0% of the time, Pallas kernels for 16%

profile of v1, /device:TPU:0, one launch (start us, length us, event | category | flops | bytes accessed | tf_op | source)
XLA Modules:
  0.0 57.1 jit_solution(14348102563617419053)
XLA Ops:
  0.6 0.0 copy-start
  0.6 0.0 copy-start.1
  0.7 0.0 slice-start
  0.7 0.0 slice-start.1
  0.7 0.0 slice-start.2
  0.7 2.0 %open.1 = (bf16[8,3584]{1,0:T(8,128)(2,1)S(1)}, bf16[8,3584]{1,0:T(8,128)(2,1)S(1)}, bf16[8,3584]{1,0:T(8,128)(2,1)S(1)}, bf16[8,3584]{1,0:T(8,128)(2,1)S(1)}, f...) custom-call(s32[8,128]{1,0:T(8,128)} %bitcast.13, ...), custom_call_target="tpu_custom_call" | custom-call | flops 20000000000 | bytes 2097152 | tf_op jit(solution)/shard_map/open/pallas_call | solution.py:143
  2.7 4.1 %collective-permute-start.3 = (bf16[80,896]{1,0:T(8,128)(2,1)S(1)}, bf16[80,896]{1,0:T(8,128)(2,1)S(1)}, u32[]{:S(2)}, u32[]{:S(2)}) collective-permute-start(bf16[80,896]{1,0:T(8,128)(2,1)S(1)} %get-tuple-element.27), channel_id=1, source_target_pairs={{0,8},{4,12},{8,0},{12,4},{1,9},{5,13},{9,1},{13,5},{2,10},{6,14},... | collective-permute-start | bytes 430088 | tf_op jit(solution)/shard_map/ppermute | solution.py:404
  6.8 1.6 %collective-permute-start = (bf16[8,3584]{1,0:T(8,128)(2,1)S(1)}, bf16[8,3584]{1,0:T(8,128)(2,1)S(1)}, u32[]{:S(2)}, u32[]{:S(2)}) collective-permute-start(bf16[8,3584]{1,0:T(8,128)(2,1)S(1)} %get-tuple-element.24), channel_id=1, source_target_pairs={{0,4},{4,0},{8,12},{12,8},{1,5},{5,1},{9,13},{13,9},{2,6},{6,2},{1... | collective-permute-start | bytes 172040 | tf_op jit(solution)/shard_map/ppermute | solution.py:404
  8.4 0.3 collective-permute-start.1
  8.7 2.5 %collective-permute-start.2 = (bf16[8,3584]{1,0:T(8,128)(2,1)S(1)}, bf16[8,3584]{1,0:T(8,128)(2,1)S(1)}, u32[]{:S(2)}, u32[]{:S(2)}) collective-permute-start(bf16[8,3584]{1,0:T(8,128)(2,1)S(1)} %get-tuple-element.26), channel_id=1, source_target_pairs={{0,12},{4,8},{8,4},{12,0},{1,13},{5,9},{9,5},{13,1},{2,14},{6,10},... | collective-permute-start | bytes 172040 | tf_op jit(solution)/shard_map/ppermute | solution.py:404
  11.2 1.0 %collective-permute-done.refs_1_ = bf16[8,3584]{1,0:T(8,128)(2,1)S(1)} collective-permute-done((bf16[8,3584]{1,0:T(8,128)(2,1)S(1)}, bf16[8,3584]{1,0:T(8,128)(2,1)S(1)}, u32[]{:S(2)}, u32[]{:S(2)}) %collective-permute-start) | collective-permute-done | bytes 57376 | tf_op jit(solution)/shard_map/ppermute | solution.py:404
  12.2 4.7 %collective-permute-done.3.refs_6_ = bf16[80,896]{1,0:T(8,128)(2,1)S(1)} collective-permute-done((bf16[80,896]{1,0:T(8,128)(2,1)S(1)}, bf16[80,896]{1,0:T(8,128)(2,1)S(1)}, u32[]{:S(2)}, u32[]{:S(2)}) %collective-permute-start.3) | collective-permute-done | bytes 143392 | tf_op jit(solution)/shard_map/ppermute | solution.py:404
  16.9 1.8 %collective-permute-start.4 = (bf16[80,896]{1,0:T(8,128)(2,1)S(1)}, bf16[80,896]{1,0:T(8,128)(2,1)S(1)}, u32[]{:S(2)}, u32[]{:S(2)}) collective-permute-start(bf16[80,896]{1,0:T(8,128)(2,1)S(1)} %collective-permute-done.3.refs_6_), channel_id=1, source_target_pairs={{0,2},{1,17},{2,0},{3,19},{16,18},{17,1},{18,16},{19,3},{4,6},{5,2... | collective-permute-start | bytes 430088 | tf_op jit(solution)/shard_map/ppermute | solution.py:437
  18.8 0.0 collective-permute-done.1.refs_2_
  18.8 0.0 collective-permute-done.2.refs_3_
  18.8 0.0 copy-done
  18.8 0.0 copy-done.1
  18.8 0.0 slice-start.3
  18.8 5.3 %gate_up.1.hidden_ref = bf16[32,2048]{1,0:T(8,128)(2,1)S(1)} custom-call(bf16[8,3584]{1,0:T(8,128)(2,1)S(1)} %get-tuple-element.23.refs_0_, bf16[8,3584]{1,0:T(8,128)(2,1)S(1)} %collective-permute-done.refs_1_, bf16[8,3584]{1,0:T(8,128)(2,1)S(1)} %collective-permute-done.1.refs_2_, bf16[8,3584]{1,0:T(8,128)(2,1)S(1)} %collective-permute-done.2.refs_3_, ...), custom_call_target="tpu_custom_call" | custom-call | flops 939524096 | bytes 29360128 | tf_op jit(solution)/shard_map/gate_up/pallas_call | solution.py:187
  24.1 0.0 copy-start.2
  24.1 0.0 copy-start.3
  24.1 0.0 copy-start.4
  24.1 0.0 copy-start.5
  24.1 0.0 collective-permute-done.4
  24.2 1.6 %collective-permute-start.9 = (bf16[2,80,896]{2,1,0:T(8,128)(2,1)S(1)}, bf16[2,80,896]{2,1,0:T(8,128)(2,1)S(1)}, u32[]{:S(2)}, u32[]{:S(2)}) collective-permute-start(bf16[2,80,896]{2,1,0:T(8,128)(2,1)S(1)} %pad_maximum_fusion.refs_4_.refs_0_), channel_id=1, source_target_pairs={{0,16},{1,3},{2,18},{3,1},{16,0},{17,19},{18,2},{19,17},{4,20},{5,... | collective-permute-start | bytes 860168 | tf_op jit(solution)/shard_map/ppermute | solution.py:441
  25.8 0.5 collective-permute-start.8
  26.2 0.0 collective-permute-start.10
  26.2 4.6 %collective-permute-done.9.refs_1_ = bf16[2,80,896]{2,1,0:T(8,128)(2,1)S(1)} collective-permute-done((bf16[2,80,896]{2,1,0:T(8,128)(2,1)S(1)}, bf16[2,80,896]{2,1,0:T(8,128)(2,1)S(1)}, u32[]{:S(2)}, u32[]{:S(2)}) %collective-permute-start.9) | collective-permute-done | bytes 286752 | tf_op jit(solution)/shard_map/ppermute | solution.py:441
  30.9 0.0 collective-permute-start.11
  30.9 0.0 slice-done
  30.9 0.0 slice-done.1
  30.9 0.0 slice-done.2
  30.9 0.0 slice-done.3
  30.9 2.6 %down.1 = (bf16[8,6016]{1,0:T(8,128)(2,1)S(1)}, bf16[8,6016]{1,0:T(8,128)(2,1)S(1)}, bf16[8,6016]{1,0:T(8,128)(2,1)S(1)}, bf16[8,6016]{1,0:T(8,128)(2,1)S(1)}) custom-call(bf16[32,2048]{1,0:T(8,128)(2,1)S(1)} %gate_up.1.hidden_ref, bf16[2048,3584]{1,0:T(8,128)(2,1)S(1)} %bitcast.7, bf16[8,2432]{1,0:T(8,128)(2,1)S(1)} %get-tuple-element.29.refs_0_, ...), custom_call_target="tpu_custom_call" | custom-call | flops 469762048 | bytes 14680064 | tf_op jit(solution)/shard_map/down/pallas_call | solution.py:220
  33.5 3.1 %collective-permute-done.8.theirs_ref = bf16[128,1792]{1,0:T(8,128)(2,1)S(1)} collective-permute-done((bf16[128,1792]{1,0:T(8,128)(2,1)S(1)}, bf16[128,1792]{1,0:T(8,128)(2,1)S(1)}, u32[]{:S(2)}, u32[]{:S(2)}) %collective-permute-start.8) | collective-permute-done | bytes 458784 | tf_op jit(solution)/shard_map/ppermute | solution.py:404
  36.6 0.0 collective-permute-done.10.refs_2_
  36.6 0.0 collective-permute-done.11.refs_3_
  36.6 0.0 copy-done.2
  36.6 0.0 copy-done.3
  36.7 3.1 %project.1 = (f32[128,576]{1,0:T(8,128)S(1)}, bf16[128,576]{1,0:T(8,128)(2,1)S(1)}) custom-call(bf16[128,3584]{1,0:T(8,128)(2,1)S(1)} %copy-done.3, bf16[128,1792]{1,0:T(8,128)(2,1)S(1)} %collective-permute-done.8.theirs_ref, bf16[576,896]{1,0:T(8,128)(2,1)S(1)} %bitcast.9, bf16[2,80,896]{2,1,0:T(8,128)(2,1)S(1)} %pad_maximum_fusion.refs_4_.refs_0_, ...), custom_call_target="tpu_custom_call" | custom-call | flops 528482304 | bytes 4194304 | tf_op jit(solution)/shard_map/project/pallas_call | solution.py:318
  39.8 1.8 %collective-permute-start.12 = (bf16[128,576]{1,0:T(8,128)(2,1)S(1)}, bf16[128,576]{1,0:T(8,128)(2,1)S(1)}, u32[]{:S(2)}, u32[]{:S(2)}) collective-permute-start(bf16[128,576]{1,0:T(8,128)(2,1)S(1)} %get-tuple-element.41), channel_id=1, source_target_pairs={{0,4},{4,0},{8,12},{12,8},{1,5},{5,1},{9,13},{13,9},{2,6},{6,2},{1... | collective-permute-start | bytes 442376 | tf_op jit(solution)/shard_map/ppermute | solution.py:404
  41.6 0.3 collective-permute-start.5
  41.9 3.7 %collective-permute-start.6 = (bf16[8,6016]{1,0:T(8,128)(2,1)S(1)}, bf16[8,6016]{1,0:T(8,128)(2,1)S(1)}, u32[]{:S(2)}, u32[]{:S(2)}) collective-permute-start(bf16[8,6016]{1,0:T(8,128)(2,1)S(1)} %get-tuple-element.36), channel_id=1, source_target_pairs={{0,8},{4,12},{8,0},{12,4},{1,9},{5,13},{9,1},{13,5},{2,10},{6,14},... | collective-permute-start | bytes 288776 | tf_op jit(solution)/shard_map/ppermute | solution.py:404
  45.5 0.4 collective-permute-start.7
  46.0 2.9 %collective-permute-done.5.refs_1_ = bf16[8,6016]{1,0:T(8,128)(2,1)S(1)} collective-permute-done((bf16[8,6016]{1,0:T(8,128)(2,1)S(1)}, bf16[8,6016]{1,0:T(8,128)(2,1)S(1)}, u32[]{:S(2)}, u32[]{:S(2)}) %collective-permute-start.5) | collective-permute-done | bytes 96288 | tf_op jit(solution)/shard_map/ppermute | solution.py:404
  48.9 0.3 collective-permute-done.6.refs_2_
  49.2 4.9 %collective-permute-done.7.refs_3_ = bf16[8,6016]{1,0:T(8,128)(2,1)S(1)} collective-permute-done((bf16[8,6016]{1,0:T(8,128)(2,1)S(1)}, bf16[8,6016]{1,0:T(8,128)(2,1)S(1)}, u32[]{:S(2)}, u32[]{:S(2)}) %collective-permute-start.7) | collective-permute-done | bytes 96288 | tf_op jit(solution)/shard_map/ppermute | solution.py:404
  54.0 1.4 %combine.1 = bf16[128,3584]{1,0:T(8,128)(2,1)} custom-call(f32[32,128]{1,0:T(8,128)S(1)} %get-tuple-element.22.mixing_ref, bf16[8,6016]{1,0:T(8,128)(2,1)S(1)} %get-tuple-element.34.refs_0_.refs_4_, bf16[8,6016]{1,0:T(8,128)(2,1)S(1)} %collective-permute-done.5.refs_1_, bf16[8,6016]{1,0:T(8,128)(2,1)S(1)} %collective-permute-done.6.refs_2_, ...), custom_call_target="tpu_custom_call" | custom-call | flops 58720256 | bytes 1376256 | tf_op jit(solution)/shard_map/combine/pallas_call | solution.py:251
  55.4 0.0 collective-permute-done.12.theirs_ref
  55.5 0.0 copy-done.4
  55.5 0.0 copy-done.5
  55.5 1.6 %finish.1 = bf16[8,9216]{1,0:T(8,128)(2,1)} custom-call(f32[128,576]{1,0:T(8,128)S(1)} %get-tuple-element.40.mine_ref, bf16[128,576]{1,0:T(8,128)(2,1)S(1)} %collective-permute-done.12.theirs_ref, f32[1,512]{1,0:T(1,128)S(1)} %bitcast.11, s32[8]{0:T(128)S(1)} %copy-done.5, bf16[8,6016]{1,0:T(8,128)(2,1)S(1)} %get-tuple-element.34.refs_0_.refs_4_, ...), custom_call_target="tpu_custom_call" | custom-call | flops 37748736 | bytes 1048576 | tf_op jit(solution)/shard_map/finish/pallas_call | solution.py:388
  (2 shorter events, 0.0 us)
Async XLA Ops:
  0.6 18.1 %copy-start = (bf16[3584,2048]{1,0:T(8,128)(2,1)S(1)}, bf16[3584,2048]{1,0:T(8,128)(2,1)}, u32[]{:S(2)}) copy-start(bf16[3584,2048]{1,0:T(8,128)(2,1)} %refs_4_.3) | copy-start | bytes 44040196
  0.6 18.1 %copy-start.1 = (bf16[3584,2048]{1,0:T(8,128)(2,1)S(1)}, bf16[3584,2048]{1,0:T(8,128)(2,1)}, u32[]{:S(2)}) copy-start(bf16[3584,2048]{1,0:T(8,128)(2,1)} %refs_5_.1) | copy-start | bytes 44040196
  0.7 30.2 %slice-start = ((s8[14680064]{0:T(1024)(128)(4,1)}), s8[4194304]{0:T(1024)(128)(4,1)S(1)}, s32[]{:S(2)}) async-start(s8[14680064]{0:T(1024)(128)(4,1)} %bitcast.6), calls=%async_computation | async-start | bytes 8388608
  0.7 30.2 %slice-start.1 = ((s8[14680064]{0:T(1024)(128)(4,1)}), s8[4194304]{0:T(1024)(128)(4,1)S(1)}, s32[]{:S(2)}) async-start(s8[14680064]{0:T(1024)(128)(4,1)} %bitcast.6), calls=%async_computation.1 | async-start | bytes 8388608
  0.7 30.2 %slice-start.2 = ((s8[14680064]{0:T(1024)(128)(4,1)}), s8[4194304]{0:T(1024)(128)(4,1)S(1)}, s32[]{:S(2)}) async-start(s8[14680064]{0:T(1024)(128)(4,1)} %bitcast.6), calls=%async_computation.2 | async-start | bytes 8388608
  2.7 14.2 %collective-permute-start.3 = (bf16[80,896]{1,0:T(8,128)(2,1)S(1)}, bf16[80,896]{1,0:T(8,128)(2,1)S(1)}, u32[]{:S(2)}, u32[]{:S(2)}) collective-permute-start(bf16[80,896]{1,0:T(8,128)(2,1)S(1)} %get-tuple-element.27), channel_id=1, source_target_pairs={{0,8},{4,12},{8,0},{12,4},{1,9},{5,13},{9,1},{13,5},{2,10},{6,14},... | collective-permute-start | bytes 430088 | tf_op jit(solution)/shard_map/ppermute | solution.py:404
  6.8 5.4 %collective-permute-start = (bf16[8,3584]{1,0:T(8,128)(2,1)S(1)}, bf16[8,3584]{1,0:T(8,128)(2,1)S(1)}, u32[]{:S(2)}, u32[]{:S(2)}) collective-permute-start(bf16[8,3584]{1,0:T(8,128)(2,1)S(1)} %get-tuple-element.24), channel_id=1, source_target_pairs={{0,4},{4,0},{8,12},{12,8},{1,5},{5,1},{9,13},{13,9},{2,6},{6,2},{1... | collective-permute-start | bytes 172040 | tf_op jit(solution)/shard_map/ppermute | solution.py:404
  8.4 10.4 %collective-permute-start.1 = (bf16[8,3584]{1,0:T(8,128)(2,1)S(1)}, bf16[8,3584]{1,0:T(8,128)(2,1)S(1)}, u32[]{:S(2)}, u32[]{:S(2)}) collective-permute-start(bf16[8,3584]{1,0:T(8,128)(2,1)S(1)} %get-tuple-element.25), channel_id=1, source_target_pairs={{0,8},{4,12},{8,0},{12,4},{1,9},{5,13},{9,1},{13,5},{2,10},{6,14},... | collective-permute-start | bytes 172040 | tf_op jit(solution)/shard_map/ppermute | solution.py:404
  8.7 10.0 %collective-permute-start.2 = (bf16[8,3584]{1,0:T(8,128)(2,1)S(1)}, bf16[8,3584]{1,0:T(8,128)(2,1)S(1)}, u32[]{:S(2)}, u32[]{:S(2)}) collective-permute-start(bf16[8,3584]{1,0:T(8,128)(2,1)S(1)} %get-tuple-element.26), channel_id=1, source_target_pairs={{0,12},{4,8},{8,4},{12,0},{1,13},{5,9},{9,5},{13,1},{2,14},{6,10},... | collective-permute-start | bytes 172040 | tf_op jit(solution)/shard_map/ppermute | solution.py:404
  16.9 7.2 %collective-permute-start.4 = (bf16[80,896]{1,0:T(8,128)(2,1)S(1)}, bf16[80,896]{1,0:T(8,128)(2,1)S(1)}, u32[]{:S(2)}, u32[]{:S(2)}) collective-permute-start(bf16[80,896]{1,0:T(8,128)(2,1)S(1)} %collective-permute-done.3.refs_6_), channel_id=1, source_target_pairs={{0,2},{1,17},{2,0},{3,19},{16,18},{17,1},{18,16},{19,3},{4,6},{5,2... | collective-permute-start | bytes 430088 | tf_op jit(solution)/shard_map/ppermute | solution.py:437
  18.8 12.1 %slice-start.3 = ((s8[14680064]{0:T(1024)(128)(4,1)}), s8[2097152]{0:T(1024)(128)(4,1)S(1)}, s32[]{:S(2)}) async-start(s8[14680064]{0:T(1024)(128)(4,1)} %bitcast.6), calls=%async_computation.3 | async-start | bytes 4194304
  24.1 12.6 %copy-start.2 = (bf16[896,576]{0,1:T(8,128)(2,1)S(1)}, bf16[896,576]{0,1:T(8,128)(2,1)}, u32[]{:S(2)}) copy-start(bf16[896,576]{0,1:T(8,128)(2,1)} %param.15) | copy-start | bytes 3096580
  24.1 12.6 %copy-start.3 = (bf16[128,3584]{1,0:T(8,128)(2,1)S(1)}, bf16[128,3584]{1,0:T(8,128)(2,1)}, u32[]{:S(2)}) copy-start(bf16[128,3584]{1,0:T(8,128)(2,1)} %tokens_ref.1) | copy-start | bytes 2752516
  24.1 31.4 %copy-start.4 = (f32[512]{0:T(512)S(1)}, f32[512]{0:T(512)}, u32[]{:S(2)}) copy-start(f32[512]{0:T(512)} %param.16) | copy-start | bytes 6148
  24.1 31.3 %copy-start.5 = (s32[8]{0:T(128)S(1)}, s32[8]{0:T(128)}, u32[]{:S(2)}) copy-start(s32[8]{0:T(128)} %survive_ref.1) | copy-start | bytes 100
  24.2 6.7 %collective-permute-start.9 = (bf16[2,80,896]{2,1,0:T(8,128)(2,1)S(1)}, bf16[2,80,896]{2,1,0:T(8,128)(2,1)S(1)}, u32[]{:S(2)}, u32[]{:S(2)}) collective-permute-start(bf16[2,80,896]{2,1,0:T(8,128)(2,1)S(1)} %pad_maximum_fusion.refs_4_.refs_0_), channel_id=1, source_target_pairs={{0,16},{1,3},{2,18},{3,1},{16,0},{17,19},{18,2},{19,17},{4,20},{5,... | collective-permute-start | bytes 860168 | tf_op jit(solution)/shard_map/ppermute | solution.py:441
  25.8 10.9 %collective-permute-start.8 = (bf16[128,1792]{1,0:T(8,128)(2,1)S(1)}, bf16[128,1792]{1,0:T(8,128)(2,1)S(1)}, u32[]{:S(2)}, u32[]{:S(2)}) collective-permute-start(bf16[128,1792]{1,0:T(8,128)(2,1)S(1)} %get-tuple-element.39), channel_id=1, source_target_pairs={{0,4},{4,0},{8,12},{12,8},{1,5},{5,1},{9,13},{13,9},{2,6},{6,2},{1... | collective-permute-start | bytes 1376264 | tf_op jit(solution)/shard_map/ppermute | solution.py:404
  26.2 10.4 %collective-permute-start.10 = (bf16[2,80,896]{2,1,0:T(8,128)(2,1)S(1)}, bf16[2,80,896]{2,1,0:T(8,128)(2,1)S(1)}, u32[]{:S(2)}, u32[]{:S(2)}) collective-permute-start(bf16[2,80,896]{2,1,0:T(8,128)(2,1)S(1)} %pad_maximum_fusion.refs_4_.refs_0_), channel_id=1, source_target_pairs={{0,1},{1,0},{2,3},{3,2},{4,5},{5,4},{6,7},{7,6},{8,9},{9,8},{10,11... | collective-permute-start | bytes 860168 | tf_op jit(solution)/shard_map/ppermute | solution.py:404
  30.9 5.8 %collective-permute-start.11 = (bf16[2,80,896]{2,1,0:T(8,128)(2,1)S(1)}, bf16[2,80,896]{2,1,0:T(8,128)(2,1)S(1)}, u32[]{:S(2)}, u32[]{:S(2)}) collective-permute-start(bf16[2,80,896]{2,1,0:T(8,128)(2,1)S(1)} %collective-permute-done.9.refs_1_), channel_id=1, source_target_pairs={{0,1},{1,0},{2,3},{3,2},{4,5},{5,4},{6,7},{7,6},{8,9},{9,8},{10,11... | collective-permute-start | bytes 860168 | tf_op jit(solution)/shard_map/ppermute | solution.py:404
  39.8 15.7 %collective-permute-start.12 = (bf16[128,576]{1,0:T(8,128)(2,1)S(1)}, bf16[128,576]{1,0:T(8,128)(2,1)S(1)}, u32[]{:S(2)}, u32[]{:S(2)}) collective-permute-start(bf16[128,576]{1,0:T(8,128)(2,1)S(1)} %get-tuple-element.41), channel_id=1, source_target_pairs={{0,4},{4,0},{8,12},{12,8},{1,5},{5,1},{9,13},{13,9},{2,6},{6,2},{1... | collective-permute-start | bytes 442376 | tf_op jit(solution)/shard_map/ppermute | solution.py:404
  41.6 7.3 %collective-permute-start.5 = (bf16[8,6016]{1,0:T(8,128)(2,1)S(1)}, bf16[8,6016]{1,0:T(8,128)(2,1)S(1)}, u32[]{:S(2)}, u32[]{:S(2)}) collective-permute-start(bf16[8,6016]{1,0:T(8,128)(2,1)S(1)} %get-tuple-element.35), channel_id=1, source_target_pairs={{0,4},{4,0},{8,12},{12,8},{1,5},{5,1},{9,13},{13,9},{2,6},{6,2},{1... | collective-permute-start | bytes 288776 | tf_op jit(solution)/shard_map/ppermute | solution.py:404
  41.9 7.3 %collective-permute-start.6 = (bf16[8,6016]{1,0:T(8,128)(2,1)S(1)}, bf16[8,6016]{1,0:T(8,128)(2,1)S(1)}, u32[]{:S(2)}, u32[]{:S(2)}) collective-permute-start(bf16[8,6016]{1,0:T(8,128)(2,1)S(1)} %get-tuple-element.36), channel_id=1, source_target_pairs={{0,8},{4,12},{8,0},{12,4},{1,9},{5,13},{9,1},{13,5},{2,10},{6,14},... | collective-permute-start | bytes 288776 | tf_op jit(solution)/shard_map/ppermute | solution.py:404
  45.5 8.5 %collective-permute-start.7 = (bf16[8,6016]{1,0:T(8,128)(2,1)S(1)}, bf16[8,6016]{1,0:T(8,128)(2,1)S(1)}, u32[]{:S(2)}, u32[]{:S(2)}) collective-permute-start(bf16[8,6016]{1,0:T(8,128)(2,1)S(1)} %get-tuple-element.37), channel_id=1, source_target_pairs={{0,12},{4,8},{8,4},{12,0},{1,13},{5,9},{9,5},{13,1},{2,14},{6,10},... | collective-permute-start | bytes 288776 | tf_op jit(solution)/shard_map/ppermute | solution.py:404

commit v2 on v1

--- a/solution.py
+++ b/solution.py
@@ -45,11 +45,35 @@
     return chip, core
 
 
+def cut_kernel(latent_ref, piece_ref, sem):
+    group, dp = lax.axis_index("groups"), lax.axis_index("dp")
+    chip_rows, core_rows = piece_rows(latent_ref.shape[0])
+    start = (group * 2 + dp // 2) * chip_rows + (dp % 2) * (chip_rows - core_rows)
+    piece = pltpu.make_async_copy(
+        latent_ref.at[pl.ds(pl.multiple_of(start, ROWS), core_rows)], piece_ref, sem
+    )
+    piece.start()
+    piece.wait()
+
+
+def cut(latent):
+    width, shard = latent.shape
+    return pl.pallas_call(
+        cut_kernel,
+        out_shape=jax.ShapeDtypeStruct((piece_rows(width)[1], shard), jnp.bfloat16),
+        in_specs=[pl.BlockSpec(memory_space=pltpu.HBM)],
+        out_specs=pl.BlockSpec(memory_space=VMEM),
+        scratch_shapes=[pltpu.SemaphoreType.DMA],
+        compiler_params=pltpu.CompilerParams(vmem_limit_bytes=1 << 20),
+        name="cut",
+    )(pltpu.with_memory_space_constraint(latent, pltpu.HBM))
+
+
 def open_kernel(page_span, *refs):
-    sources, latent_ref, outs = refs[:5], refs[5], refs[6:]
+    sources, outs = refs[:5], refs[5:]
     sends, mixing_ref, pages = outs[:EXPERTS], outs[EXPERTS], outs[EXPERTS + 1 : 2 * EXPERTS + 1]
-    piece_ref, across_ref = outs[2 * EXPERTS + 1 : 2 * EXPERTS + 3]
-    *held, sem, sems = outs[2 * EXPERTS + 3 :]
+    across_ref = outs[2 * EXPERTS + 1]
+    *held, sems = outs[2 * EXPERTS + 2 :]
     ids_ref, weight_ref, tokens_ref, old_ref, target_ref = held
     copies = [
         pltpu.make_async_copy(source, target, sems.at[at])
@@ -57,16 +81,10 @@
     ]
     for copy in copies:
         copy.start()
-    group, me, dp = (lax.axis_index(axis) for axis in ("groups", "expert", "dp"))
-    chip_rows, core_rows = piece_rows(latent_ref.shape[0])
-    start = (group * 2 + dp // 2) * chip_rows + (dp % 2) * (chip_rows - core_rows)
-    piece = pltpu.make_async_copy(
-        latent_ref.at[pl.ds(pl.multiple_of(start, ROWS), core_rows)], piece_ref, sem
-    )
-    piece.start()
+    me = lax.axis_index("expert")
     for copy in copies:
         copy.wait()
-    shard = latent_ref.shape[1]
+    shard = across_ref.shape[1] // 2
     for half, bit in enumerate((1, 3)):
         columns = pl.ds(pl.multiple_of((me ^ bit) * shard, LANES), shard)
         across_ref[:, half * shard : (half + 1) * shard] = tokens_ref[:, columns]
@@ -124,31 +142,28 @@
         rows = slice(at * PER_PAIR * SPLIT, (at + 1) * PER_PAIR * SPLIT)
         pages[at][:, :width] = moved[rows].astype(jnp.bfloat16)
         pages[at][:, width:] = tags[rows].astype(jnp.bfloat16)
-    piece.wait()
-
-
-def open_work(ids, weights, tokens, old_latents, latent, old_target):
+
+
+def open_work(ids, weights, tokens, old_latents, old_target, shard):
     token_count, model_width = tokens.shape
     page_count, page_width = old_latents.shape
     send = jax.ShapeDtypeStruct((CAP, model_width), jnp.bfloat16)
     mixing = jax.ShapeDtypeStruct((EXPERTS * CAP, token_count), jnp.float32)
     page = jax.ShapeDtypeStruct((PER_PAIR * SPLIT, page_width // SPLIT + LANES), jnp.bfloat16)
-    piece = jax.ShapeDtypeStruct((piece_rows(latent.shape[0])[1], latent.shape[1]), jnp.bfloat16)
-    across = jax.ShapeDtypeStruct((token_count, 2 * latent.shape[1]), jnp.bfloat16)
+    across = jax.ShapeDtypeStruct((token_count, 2 * shard), jnp.bfloat16)
     spec = pl.BlockSpec(memory_space=VMEM)
     inputs = [
         pltpu.with_memory_space_constraint(value, pltpu.HBM)
-        for value in (ids, weights, tokens, old_latents, old_target, latent)
+        for value in (ids, weights, tokens, old_latents, old_target)
     ]
     results = pl.pallas_call(
         functools.partial(open_kernel, page_count * lax.axis_size("dp")),
-        out_shape=(send,) * EXPERTS + (mixing,) + (page,) * EXPERTS + (piece, across),
-        in_specs=[pl.BlockSpec(memory_space=pltpu.HBM)] * 6,
-        out_specs=(spec,) * (2 * EXPERTS + 3),
+        out_shape=(send,) * EXPERTS + (mixing,) + (page,) * EXPERTS + (across,),
+        in_specs=[pl.BlockSpec(memory_space=pltpu.HBM)] * 5,
+        out_specs=(spec,) * (2 * EXPERTS + 2),
         scratch_shapes=[VMEM(value.shape, value.dtype) for value in inputs[:4]]
         + [
             SMEM(old_target.shape, old_target.dtype),
-            pltpu.SemaphoreType.DMA,
             pltpu.SemaphoreType.DMA((5,)),
         ],
         compiler_params=pltpu.CompilerParams(vmem_limit_bytes=8 << 20),
@@ -158,7 +173,7 @@
         name="open",
     )(*inputs)
     sends, mixing, rest = results[:EXPERTS], results[EXPERTS], results[EXPERTS + 1 :]
-    return sends, mixing, rest[:EXPERTS], rest[EXPERTS], rest[EXPERTS + 1]
+    return sends, mixing, rest[:EXPERTS], rest[EXPERTS]
 
 
 def stacked_rows(refs):
@@ -167,44 +182,49 @@
     )
 
 
-def gate_up_kernel(*refs):
-    rows, (gate_ref, up_ref) = refs[:EXPERTS], refs[EXPERTS : EXPERTS + 2]
-    hidden_ref = refs[-1]
+def gate_kernel(*refs):
+    rows, gate_ref, out_ref = refs[:EXPERTS], refs[EXPERTS], refs[-1]
     block = stacked_rows(rows)
-    step = CHUNK // 2
-    for at in range(0, gate_ref.shape[1], step):
-        columns = slice(at, at + step)
-        gate = jnp.dot(block, gate_ref[:, columns], preferred_element_type=jnp.float32)
-        up = jnp.dot(block, up_ref[:, columns], preferred_element_type=jnp.float32)
-        hidden_ref[:, columns] = (gate / (1.0 + jnp.exp(-gate)) * up).astype(jnp.bfloat16)
-
-
-def gate_up(rows, w_gate, w_up, after):
+    for at in range(0, gate_ref.shape[1], CHUNK):
+        columns = slice(at, at + CHUNK)
+        out_ref[:, columns] = jnp.dot(
+            block, gate_ref[:, columns], preferred_element_type=jnp.float32
+        )
+
+
+def gates(rows, w_gate, after):
     spec, unread = pl.BlockSpec(memory_space=VMEM), pl.BlockSpec(memory_space=pl.ANY)
-    held = [pltpu.with_memory_space_constraint(w, VMEM) for w in (w_gate, w_up)]
     model_width, unit_count = w_gate.shape
     row_count = EXPERTS * CAP
     return pl.pallas_call(
-        gate_up_kernel,
-        out_shape=jax.ShapeDtypeStruct((row_count, unit_count), jnp.bfloat16),
-        in_specs=[spec] * (EXPERTS + 2) + [unread] * len(after),
+        gate_kernel,
+        out_shape=jax.ShapeDtypeStruct((row_count, unit_count), jnp.float32),
+        in_specs=[spec] * (EXPERTS + 1) + [unread] * len(after),
         out_specs=spec,
         compiler_params=pltpu.CompilerParams(vmem_limit_bytes=4 << 20),
         cost_estimate=pl.CostEstimate(
             flops=4 * row_count * model_width * unit_count,
             bytes_accessed=4 * model_width * unit_count,
-            transcendentals=row_count * unit_count,
-        ),
-        name="gate_up",
-    )(*rows, *held, *after)
-
-
-def down_kernel(hidden_ref, down_ref, *refs):
-    pages, outs = refs[:EXPERTS], refs[-EXPERTS:]
+            transcendentals=0,
+        ),
+        name="gates",
+    )(*rows, pltpu.with_memory_space_constraint(w_gate, VMEM), *after)
+
+
+def expert_kernel(*refs):
+    rows, refs = refs[:EXPERTS], refs[EXPERTS:]
+    gates_ref, up_ref, down_ref = refs[:3]
+    pages, outs, hidden_ref = refs[3 : 3 + EXPERTS], refs[-EXPERTS - 1 : -1], refs[-1]
     model_width = down_ref.shape[1]
     for peer in range(EXPERTS):
         outs[peer][:, model_width:] = pages[peer][...]
-    for at in range(0, down_ref.shape[1], CHUNK):
+    block = stacked_rows(rows)
+    for at in range(0, up_ref.shape[1], CHUNK):
+        columns = slice(at, at + CHUNK)
+        gate = gates_ref[:, columns]
+        up = jnp.dot(block, up_ref[:, columns], preferred_element_type=jnp.float32)
+        hidden_ref[:, columns] = (gate / (1.0 + jnp.exp(-gate)) * up).astype(jnp.bfloat16)
+    for at in range(0, model_width, CHUNK):
         columns = slice(at, at + CHUNK)
         result = jnp.dot(
             hidden_ref[...], down_ref[:, columns], preferred_element_type=jnp.float32
@@ -214,28 +234,37 @@
             outs[peer][:, columns] = part.astype(jnp.bfloat16)
 
 
-def down(hidden, w_down, pages, after):
+def experts(rows, gate, w_up, w_down, pages, after):
     spec, unread = pl.BlockSpec(memory_space=VMEM), pl.BlockSpec(memory_space=pl.ANY)
+    held = [pltpu.with_memory_space_constraint(w, VMEM) for w in (w_up, w_down)]
     unit_count, model_width = w_down.shape
+    row_count = EXPERTS * CAP
     return pl.pallas_call(
-        down_kernel,
+        expert_kernel,
         out_shape=(jax.ShapeDtypeStruct((CAP, model_width + pages[0].shape[1]), jnp.bfloat16),)
         * EXPERTS,
-        in_specs=[spec] * (2 + EXPERTS) + [unread] * len(after),
+        in_specs=[spec] * (3 + 2 * EXPERTS) + [unread] * len(after),
         out_specs=(spec,) * EXPERTS,
+        scratch_shapes=[VMEM((row_count, unit_count), jnp.bfloat16)],
         compiler_params=pltpu.CompilerParams(vmem_limit_bytes=4 << 20),
         cost_estimate=pl.CostEstimate(
-            flops=2 * EXPERTS * CAP * model_width * unit_count,
+            flops=2 * row_count * model_width * unit_count,
             bytes_accessed=2 * model_width * unit_count,
             transcendentals=0,
         ),
-        name="down",
-    )(hidden, pltpu.with_memory_space_constraint(w_down, VMEM), *pages, *after)
+        name="experts",
+    )(*rows, gate, *held, *pages, *after)
 
 
 def combine_kernel(mixing_ref, *refs):
-    rows, out_ref = refs[:EXPERTS], refs[EXPERTS]
+    rows, parts, (out_ref, pages_ref) = refs[:EXPERTS], refs[EXPERTS:-2], refs[-2:]
     block = stacked_rows(rows)
+
+    @pl.when(pl.program_id(0) == 0)
+    def _():
+        columns = pl.ds(parts[0].shape[1] - pages_ref.shape[1], pages_ref.shape[1])
+        pages_ref[...] = stacked_rows([part.at[:, columns] for part in parts])
+
     mixing = mixing_ref[...]
     high = mixing.astype(jnp.bfloat16).astype(jnp.float32)
     mixing = jnp.concatenate([high, mixing - high], axis=0).astype(jnp.bfloat16)
@@ -247,25 +276,36 @@
 def combine(mixing, rows, model_width):
     slot_count, token_count = mixing.shape
     width = model_width // 2
+    page_width = rows[0].shape[1] - model_width
     columns = pl.BlockSpec((CAP, width), lambda at: (0, at))
+    whole = pl.BlockSpec(rows[0].shape, lambda at: (0, 0))
     return pl.pallas_call(
         combine_kernel,
         grid=(model_width // width,),
-        out_shape=jax.ShapeDtypeStruct((token_count, model_width), jnp.bfloat16),
-        in_specs=[pl.BlockSpec((slot_count, token_count), lambda at: (0, 0))] + [columns] * EXPERTS,
-        out_specs=pl.BlockSpec((token_count, width), lambda at: (0, at)),
+        out_shape=(
+            jax.ShapeDtypeStruct((token_count, model_width), jnp.bfloat16),
+            jax.ShapeDtypeStruct((slot_count, page_width), jnp.bfloat16),
+        ),
+        in_specs=[pl.BlockSpec((slot_count, token_count), lambda at: (0, 0))]
+        + [columns] * EXPERTS
+        + [whole] * EXPERTS,
+        out_specs=(
+            pl.BlockSpec((token_count, width), lambda at: (0, at)),
+            pl.BlockSpec((slot_count, page_width), lambda at: (0, 0)),
+        ),
         compiler_params=pltpu.CompilerParams(vmem_limit_bytes=8 << 20),
         cost_estimate=pl.CostEstimate(
-            flops=4 * token_count * slot_count * model_width,
+            flops=11530000000,
             bytes_accessed=3 * token_count * model_width,
             transcendentals=0,
         ),
         name="combine",
-    )(mixing, *rows)
+    )(mixing, *rows, *rows)
 
 
 def project_kernel(tokens_ref, theirs_ref, own_ref, *refs):
-    held, (mine_out, theirs_out), (far_ref, sems) = refs[:4], refs[-4:-2], refs[-2:]
+    held, (mine_out, theirs_out) = refs[:4], refs[-5:-3]
+    both_ref, far_ref, sems = refs[-3:]
     group, me, dp = (lax.axis_index(axis) for axis in ("groups", "expert", "dp"))
     shard = own_ref.shape[1]
     chip_rows, core_rows = piece_rows(own_ref.shape[0])
@@ -302,13 +342,16 @@
         return lax.dot_general(left, weights_ref[...], NT, preferred_element_type=jnp.float32)
 
     on_each_core(lambda copy: copy.start())
-    theirs_near = part(theirs_ref[:, :shard], own_ref)
-    mine_near = part(tokens_ref[:, pl.ds(pl.multiple_of(me * shard, LANES), shard)], own_ref)
+    count = tokens_ref.shape[0]
+    for half, bit in enumerate((0, 2)):
+        columns = pl.ds(pl.multiple_of((me ^ bit) * shard, LANES), shard)
+        both_ref[:count, half * shard : (half + 1) * shard] = tokens_ref[:, columns]
+    both_ref[count:, :] = theirs_ref[...]
+    total = part(both_ref[:, :shard], own_ref)
     on_each_core(lambda copy: copy.wait())
-    theirs_far = part(theirs_ref[:, shard:], far_ref)
-    theirs_out[...] = (theirs_near + theirs_far).astype(jnp.bfloat16)
-    far_columns = pl.ds(pl.multiple_of((me ^ 2) * shard, LANES), shard)
-    mine_out[...] = mine_near + part(tokens_ref[:, far_columns], far_ref)
+    total = total + part(both_ref[:, shard:], far_ref)
+    mine_out[...] = total[:count]
+    theirs_out[...] = total[count:].astype(jnp.bfloat16)
 
 
 def project(tokens, theirs, own, held, after):
@@ -323,17 +366,20 @@
         ),
         in_specs=[vmem] * 3 + [hbm] * (4 + len(after)),
         out_specs=(vmem, vmem),
-        scratch_shapes=[VMEM((width, shard), jnp.bfloat16), pltpu.SemaphoreType.DMA((8,))],
+        scratch_shapes=[
+            VMEM((2 * token_count, 2 * shard), jnp.bfloat16),
+            VMEM((width, shard), jnp.bfloat16),
+            pltpu.SemaphoreType.DMA((8,)),
+        ],
         compiler_params=pltpu.CompilerParams(vmem_limit_bytes=8 << 20),
         cost_estimate=pl.CostEstimate(
-            flops=8 * token_count * shard * width, bytes_accessed=4 << 20, transcendentals=0
+            flops=1153000000, bytes_accessed=0, transcendentals=0
         ),
         name="project",
     )(tokens, theirs, own, *held, *after)
 
 
-def finish_kernel(mine_ref, theirs_ref, gain_ref, survive_ref, *refs):
-    arrived, out_ref = refs[:EXPERTS], refs[EXPERTS]
+def finish_kernel(mine_ref, theirs_ref, gain_ref, survive_ref, arrived_ref, out_ref):
     page_count, page_width = out_ref.shape
     projected = mine_ref[...] + theirs_ref[...].astype(jnp.float32)
     nope_part = projected[:, :KV]
@@ -350,14 +396,12 @@
         rebuilt,
         preferred_element_type=jnp.float32,
     )
-    columns = slice(arrived[0].shape[1] - LANES - page_width // SPLIT, None)
-    arrivals = jnp.concatenate([ref[:, columns].astype(jnp.float32) for ref in arrived], axis=0)
     part_width = page_width // SPLIT
-    row_count = arrivals.shape[0]
+    row_count = arrived_ref.shape[0]
     slot = lax.broadcasted_iota(jnp.int32, (row_count, page_count), 1).astype(jnp.float32)
     part_of = lax.broadcasted_iota(jnp.int32, (row_count, page_count), 0) % SPLIT
-    meant = arrivals[:, part_width : part_width + 1] == slot + 1.0
-    arrivals = arrivals[:, :part_width].astype(jnp.bfloat16)
+    meant = arrived_ref[:, part_width:].astype(jnp.float32)[:, :1] == slot + 1.0
+    arrivals = arrived_ref[:, :part_width]
     carried = [
         lax.dot_general(
             jnp.where(meant & (part_of == part), 1.0, 0.0).astype(jnp.bfloat16),
@@ -388,7 +432,7 @@
     return pl.pallas_call(
         finish_kernel,
         out_shape=jax.ShapeDtypeStruct((page_count, page_width), jnp.bfloat16),
-        in_specs=[vmem] * 3 + [pl.BlockSpec(memory_space=SMEM)] + [vmem] * EXPERTS,
+        in_specs=[vmem] * 3 + [pl.BlockSpec(memory_space=SMEM), vmem],
         out_specs=vmem,
         compiler_params=pltpu.CompilerParams(vmem_limit_bytes=6 << 20),
         cost_estimate=pl.CostEstimate(
@@ -397,7 +441,7 @@
             transcendentals=mine.shape[0],
         ),
         name="finish",
-    )(mine, theirs, latent_gain.reshape(1, -1), survive, *arrived)
+    )(mine, theirs, latent_gain.reshape(1, -1), survive, arrived)
 
 
 def swap(value, axis, bit):
@@ -428,27 +472,30 @@
     group_count, dp_count = lax.axis_size("groups"), lax.axis_size("dp")
     plane = ("groups", "dp")
     latent = w_latent.T
-    sends, mixing, pages, piece, across = open_work(
-        route_ids.T, route_weight.T, tokens, old_latents, latent, old_target
-    )
+    piece = cut(latent)
     far_piece = swap(piece, "expert", 2)
+    sends, mixing, pages, across = open_work(
+        route_ids.T, route_weight.T, tokens, old_latents, old_target, latent.shape[1]
+    )
     received = exchanged(sends)
     far_piece = tied(far_piece, received[1])
     first = lax.ppermute(far_piece, plane, plane_pairs(group_count, dp_count, True))
-    theirs = swap(tied(across, *received[1:]), "expert", 1)
-    hidden = gate_up(received, w_gate, w_up, (far_piece,))
-    near = tied(jnp.stack([far_piece, first]), hidden)
+    theirs = swap(tied(across, far_piece), "expert", 1)
+    gate = gates(received, w_gate, (far_piece,))
+    near = tied(jnp.stack([far_piece, first]), gate)
     far = lax.ppermute(near, plane, plane_pairs(group_count, dp_count, False))
     near_other = swap(near, "dp", 1)
-    results = down(hidden, w_down, pages, (near,))
+    results = experts(received, gate, w_up, w_down, pages, (near,))
+    results = [tied(result, theirs) for result in results]
     returned = exchanged(results)
+    far = tied(far, results[0])
     far_other = swap(far, "dp", 1)
     mine, across_sums = project(
-        tokens, theirs, latent, (near, far, near_other, far_other), (results[0],)
+        tokens, theirs, latent, (near, far, near_other, far_other), ()
     )
     their_sums = swap(across_sums, "expert", 1)
-    moe_out = combine(mixing, returned, tokens.shape[1])
-    latents = finish(mine, their_sums, latent_gain, survive, returned, *old_latents.shape)
+    moe_out, arrived = combine(mixing, returned, tokens.shape[1])
+    latents = finish(mine, their_sums, latent_gain, survive, arrived, *old_latents.shape)
     return (moe_out, latents)
 
 

time: 57.2 us -> 45.5 us (0.80)
  waiting for transfers between devices: 21.5 us -> 8.71 us
  Pallas kernels: 16 us -> 16.6 us
    ppermute x11, waiting for transfers between devices: 16.9 us -> 8.7 us  [swap(): return lax.ppermute(value, axis, xor_pairs(lax.axis_size(axis), bit))]
    ppermute x1, waiting for transfers between devices: 4.63 us -> 0.01 us  [block_shards(): far = lax.ppermute(near, plane, plane_pairs(group_count, dp_count, False))]
    pallas_call x3 -> x4, Pallas kernels: 9.28 us -> 10.3 us  [the longest x1 5.18 us: experts(): pl.pallas_call(expert_kernel, out_shape=(jax.ShapeDtypeStruct((CAP, model...]
    ppermute x11, starting transfers between devices: 15.2 us -> 15.9 us  [swap(): return lax.ppermute(value, axis, xor_pairs(lax.axis_size(axis), bit))]
  transfers between devices with their start and end apart: 13 -> 13, of which waited for: 7 -> 5; matrix products, arithmetic and copies ran while one was open for 0% -> 0% of each run, Pallas kernels for 16% -> 31%
where the time goes in v2:
time: 45.5 us; the launch traced here: 45.3 us
  starting transfers between devices  19.1 us (42%)
  Pallas kernels  16.6 us (36%)
  waiting for transfers between devices  8.71 us (19%)
  between operations  0.88 us (2%)
    ppermute x11, starting transfers between devices, swap(): return lax.ppermute(value, axis, xor_pairs(lax.axis_size(axis), bit))  15.9 us
    ppermute x11, waiting for transfers between devices, swap(): return lax.ppermute(value, axis, xor_pairs(lax.axis_size(axis), bit))  8.7 us
    pallas_call x1, Pallas kernels, experts(): pl.pallas_call(expert_kernel, out_shape=(jax.ShapeDtypeStruct((CAP, model...  5.18 us
    pallas_call x1, Pallas kernels, gates(): pl.pallas_call(gate_kernel, out_shape=jax.ShapeDtypeStruct((row_count, un...  2.63 us
    pallas_call x1, Pallas kernels, project(): pl.pallas_call(project_kernel, out_shape=(jax.ShapeDtypeStruct((token_cou...  2.6 us
    pallas_call x1, Pallas kernels, open_work(): pl.pallas_call(functools.partial(open_kernel, page_count * lax.axis_size(...  1.99 us
    pallas_call x1, Pallas kernels, finish(): pl.pallas_call(finish_kernel, out_shape=jax.ShapeDtypeStruct((page_count,...  1.62 us
    ppermute x1, starting transfers between devices, block_shards(): lax.ppermute(far_piece, plane, plane_pairs(group_count, dp_count, True))  1.59 us
  transfers between devices with their start and end apart: 13, of which 5 were waited for; matrix products, arithmetic and copies ran while one was open for 0% of the time, Pallas kernels for 31%

profile of v2, /device:TPU:0, one launch (start us, length us, event | category | flops | bytes accessed | tf_op | source)
XLA Modules:
  0.0 45.3 jit_solution(13329969079826632314)
XLA Ops:
  0.6 0.0 slice-start.8
  0.6 1.1 %cut.1 = bf16[80,896]{1,0:T(8,128)(2,1)S(1)} custom-call(bf16[576,896]{1,0:T(8,128)(2,1)} %bitcast.12), custom_call_target="tpu_custom_call" | custom-call | tf_op jit(solution)/shard_map/cut/pallas_call | solution.py:61
  1.7 4.1 %collective-permute-start.3 = (bf16[80,896]{1,0:T(8,128)(2,1)S(1)}, bf16[80,896]{1,0:T(8,128)(2,1)S(1)}, u32[]{:S(2)}, u32[]{:S(2)}) collective-permute-start(bf16[80,896]{1,0:T(8,128)(2,1)S(1)} %cut.1), channel_id=1, source_target_pairs={{0,8},{4,12},{8,0},{12,4},{1,9},{5,13},{9,1},{13,5},{2,10},{6,14},... | collective-permute-start | bytes 430088 | tf_op jit(solution)/shard_map/ppermute | solution.py:448
  5.8 0.0 slice-start
  5.8 0.0 slice-start.4
  5.8 0.0 slice-start.9
  5.8 0.0 slice-start.11
  5.9 0.0 slice-start.1
  5.9 0.0 slice-start.2
  5.9 0.0 slice-start.3
  5.9 0.0 slice-start.5
  5.9 0.0 slice-start.6
  5.9 0.0 slice-start.7
  5.9 2.0 %open.1 = (bf16[8,3584]{1,0:T(8,128)(2,1)S(1)}, bf16[8,3584]{1,0:T(8,128)(2,1)S(1)}, bf16[8,3584]{1,0:T(8,128)(2,1)S(1)}, bf16[8,3584]{1,0:T(8,128)(2,1)S(1)}, f...) custom-call(s32[8,128]{1,0:T(8,128)} %bitcast.17, ...), custom_call_target="tpu_custom_call" | custom-call | flops 20000000000 | bytes 2097152 | tf_op jit(solution)/shard_map/open/pallas_call | solution.py:159
  7.9 1.6 %collective-permute-start = (bf16[8,3584]{1,0:T(8,128)(2,1)S(1)}, bf16[8,3584]{1,0:T(8,128)(2,1)S(1)}, u32[]{:S(2)}, u32[]{:S(2)}) collective-permute-start(bf16[8,3584]{1,0:T(8,128)(2,1)S(1)} %get-tuple-element.30), channel_id=1, source_target_pairs={{0,4},{4,0},{8,12},{12,8},{1,5},{5,1},{9,13},{13,9},{2,6},{6,2},{1... | collective-permute-start | bytes 172040 | tf_op jit(solution)/shard_map/ppermute | solution.py:448
  9.6 0.3 collective-permute-start.1
  9.9 2.5 %collective-permute-start.2 = (bf16[8,3584]{1,0:T(8,128)(2,1)S(1)}, bf16[8,3584]{1,0:T(8,128)(2,1)S(1)}, u32[]{:S(2)}, u32[]{:S(2)}) collective-permute-start(bf16[8,3584]{1,0:T(8,128)(2,1)S(1)} %get-tuple-element.32), channel_id=1, source_target_pairs={{0,12},{4,8},{8,4},{12,0},{1,13},{5,9},{9,5},{13,1},{2,14},{6,10},... | collective-permute-start | bytes 172040 | tf_op jit(solution)/shard_map/ppermute | solution.py:448
  12.4 0.6 %collective-permute-done.refs_1_ = bf16[8,3584]{1,0:T(8,128)(2,1)S(1)} collective-permute-done((bf16[8,3584]{1,0:T(8,128)(2,1)S(1)}, bf16[8,3584]{1,0:T(8,128)(2,1)S(1)}, u32[]{:S(2)}, u32[]{:S(2)}) %collective-permute-start) | collective-permute-done | bytes 57376 | tf_op jit(solution)/shard_map/ppermute | solution.py:448
  12.9 1.9 %collective-permute-done.3.refs_5_ = bf16[80,896]{1,0:T(8,128)(2,1)S(1)} collective-permute-done((bf16[80,896]{1,0:T(8,128)(2,1)S(1)}, bf16[80,896]{1,0:T(8,128)(2,1)S(1)}, u32[]{:S(2)}, u32[]{:S(2)}) %collective-permute-start.3) | collective-permute-done | bytes 143392 | tf_op jit(solution)/shard_map/ppermute | solution.py:448
  14.8 1.6 %collective-permute-start.4 = (bf16[80,896]{1,0:T(8,128)(2,1)S(1)}, bf16[80,896]{1,0:T(8,128)(2,1)S(1)}, u32[]{:S(2)}, u32[]{:S(2)}) collective-permute-start(bf16[80,896]{1,0:T(8,128)(2,1)S(1)} %collective-permute-done.3.refs_5_), channel_id=1, source_target_pairs={{0,2},{1,17},{2,0},{3,19},{16,18},{17,1},{18,16},{19,3},{4,6},{5,2... | collective-permute-start | bytes 430088 | tf_op jit(solution)/shard_map/ppermute | solution.py:482
  16.4 1.0 %collective-permute-start.5 = (bf16[128,1792]{1,0:T(8,128)(2,1)S(1)}, bf16[128,1792]{1,0:T(8,128)(2,1)S(1)}, u32[]{:S(2)}, u32[]{:S(2)}) collective-permute-start(bf16[128,1792]{1,0:T(8,128)(2,1)S(1)} %get-tuple-element.41), channel_id=1, source_target_pairs={{0,4},{4,0},{8,12},{12,8},{1,5},{5,1},{9,13},{13,9},{2,6},{6,2},{1... | collective-permute-start | bytes 1376264 | tf_op jit(solution)/shard_map/ppermute | solution.py:448
  17.4 0.0 collective-permute-done.1.refs_2_
  17.4 0.0 collective-permute-done.2.refs_3_
  17.4 0.0 slice-done.8
  17.4 0.0 slice-done.9
  17.4 0.0 slice-done.10
  17.4 0.0 slice-done.11
  17.4 2.6 %gates.1.refs_4_ = f32[32,2048]{1,0:T(8,128)S(1)} custom-call(bf16[8,3584]{1,0:T(8,128)(2,1)S(1)} %get-tuple-element.29.refs_0_, bf16[8,3584]{1,0:T(8,128)(2,1)S(1)} %collective-permute-done.refs_1_, bf16[8,3584]{1,0:T(8,128)(2,1)S(1)} %collective-permute-done.1.refs_2_, bf16[8,3584]{1,0:T(8,128)(2,1)S(1)} %collective-permute-done.2.refs_3_, ...), custom_call_target="tpu_custom_call" | custom-call | flops 939524096 | bytes 29360128 | tf_op jit(solution)/shard_map/gates/pallas_call | solution.py:199
  20.1 0.0 collective-permute-done.4
  20.1 1.6 %collective-permute-start.9 = (bf16[2,80,896]{2,1,0:T(8,128)(2,1)S(1)}, bf16[2,80,896]{2,1,0:T(8,128)(2,1)S(1)}, u32[]{:S(2)}, u32[]{:S(2)}) collective-permute-start(bf16[2,80,896]{2,1,0:T(8,128)(2,1)S(1)} %pad_maximum_fusion.refs_11_.refs_0_), channel_id=1, source_target_pairs={{0,16},{1,3},{2,18},{3,1},{16,0},{17,19},{18,2},{19,17},{4,20},{5,... | collective-permute-start | bytes 860168 | tf_op jit(solution)/shard_map/ppermute | solution.py:486
  21.7 0.0 collective-permute-start.10
  21.7 0.0 slice-done
  21.7 0.0 slice-done.4
  21.7 0.0 slice-done.1
  21.7 0.0 slice-done.2
  21.7 0.0 slice-done.3
  21.7 0.0 slice-done.5
  21.7 0.0 slice-done.6
  21.8 0.0 slice-done.7
  21.8 0.0 copy-start
  21.8 0.0 copy-start.3
  21.8 5.2 %experts.1 = (bf16[8,6016]{1,0:T(8,128)(2,1)S(1)}, bf16[8,6016]{1,0:T(8,128)(2,1)S(1)}, bf16[8,6016]{1,0:T(8,128)(2,1)S(1)}, bf16[8,6016]{1,0:T(8,128)(2,1)S(1)}) custom-call(bf16[8,3584]{1,0:T(8,128)(2,1)S(1)} %get-tuple-element.29.refs_0_, bf16[8,3584]{1,0:T(8,128)(2,1)S(1)} %collective-permute-done.refs_1_, ...), custom_call_target="tpu_custom_call" | custom-call | flops 469762048 | bytes 14680064 | tf_op jit(solution)/shard_map/experts/pallas_call | solution.py:242
  27.0 0.2 collective-permute-done.5.theirs_ref
  27.2 0.0 collective-permute-done.9.refs_1_
  27.2 0.4 collective-permute-start.11
  27.6 1.3 %collective-permute-start.6 = (bf16[8,6016]{1,0:T(8,128)(2,1)S(1)}, bf16[8,6016]{1,0:T(8,128)(2,1)S(1)}, u32[]{:S(2)}, u32[]{:S(2)}) collective-permute-start(bf16[8,6016]{1,0:T(8,128)(2,1)S(1)} %get-tuple-element.44), channel_id=1, source_target_pairs={{0,4},{4,0},{8,12},{12,8},{1,5},{5,1},{9,13},{13,9},{2,6},{6,2},{1... | collective-permute-start | bytes 288776 | tf_op jit(solution)/shard_map/ppermute | solution.py:448
  28.9 4.0 %collective-permute-start.7 = (bf16[8,6016]{1,0:T(8,128)(2,1)S(1)}, bf16[8,6016]{1,0:T(8,128)(2,1)S(1)}, u32[]{:S(2)}, u32[]{:S(2)}) collective-permute-start(bf16[8,6016]{1,0:T(8,128)(2,1)S(1)} %get-tuple-element.46), channel_id=1, source_target_pairs={{0,8},{4,12},{8,0},{12,4},{1,9},{5,13},{9,1},{13,5},{2,10},{6,14},... | collective-permute-start | bytes 288776 | tf_op jit(solution)/shard_map/ppermute | solution.py:448
  32.9 0.0 collective-permute-start.8
  32.9 0.0 collective-permute-done.10.refs_2_
  32.9 0.0 collective-permute-done.11.refs_3_
  32.9 0.0 copy-done
  32.9 0.0 copy-done.3
  33.0 2.6 %project.1 = (f32[128,576]{1,0:T(8,128)S(1)}, bf16[128,576]{1,0:T(8,128)(2,1)S(1)}) custom-call(bf16[128,3584]{1,0:T(8,128)(2,1)S(1)} %copy-done.3, bf16[128,1792]{1,0:T(8,128)(2,1)S(1)} %collective-permute-done.5.theirs_ref, bf16[576,896]{1,0:T(8,128)(2,1)S(1)} %bitcast.13, bf16[2,80,896]{2,1,0:T(8,128)(2,1)S(1)} %pad_maximum_fusion.refs_11_.refs_0_, ...), custom_call_target="tpu_custom_call" | custom-call | flops 1152999936 | tf_op jit(solution)/shard_map/project/pallas_call | solution.py:361
  35.6 0.6 %collective-permute-start.12 = (bf16[128,576]{1,0:T(8,128)(2,1)S(1)}, bf16[128,576]{1,0:T(8,128)(2,1)S(1)}, u32[]{:S(2)}, u32[]{:S(2)}) collective-permute-start(bf16[128,576]{1,0:T(8,128)(2,1)S(1)} %get-tuple-element.52), channel_id=1, source_target_pairs={{0,4},{4,0},{8,12},{12,8},{1,5},{5,1},{9,13},{13,9},{2,6},{6,2},{1... | collective-permute-start | bytes 442376 | tf_op jit(solution)/shard_map/ppermute | solution.py:448
  36.2 0.0 collective-permute-done.6.refs_1_.refs_5_
  36.2 4.4 %collective-permute-done.7.refs_2_.refs_6_ = bf16[8,6016]{1,0:T(8,128)(2,1)S(1)} collective-permute-done((bf16[8,6016]{1,0:T(8,128)(2,1)S(1)}, bf16[8,6016]{1,0:T(8,128)(2,1)S(1)}, u32[]{:S(2)}, u32[]{:S(2)}) %collective-permute-start.7) | collective-permute-done | bytes 96288 | tf_op jit(solution)/shard_map/ppermute | solution.py:448
  40.6 0.0 collective-permute-done.8.refs_3_.refs_7_
  40.6 0.0 copy-start.1
  40.6 0.0 copy-start.2
  40.6 1.4 %combine.1 = (bf16[128,3584]{1,0:T(8,128)(2,1)}, bf16[32,2432]{1,0:T(8,128)(2,1)S(1)}) custom-call(f32[32,128]{1,0:T(8,128)S(1)} %get-tuple-element.28.mixing_ref, bf16[8,6016]{1,0:T(8,128)(2,1)S(1)} %get-tuple-element.42.refs_0_.refs_4_, bf16[8,6016]{1,0:T(8,128)(2,1)S(1)} %collective-permute-done.6.refs_1_.refs_5_, ...), custom_call_target="tpu_custom_call" | custom-call | flops 11530000384 | bytes 1376256 | tf_op jit(solution)/shard_map/combine/pallas_call | solution.py:282
  42.1 1.6 %collective-permute-done.12.theirs_ref = bf16[128,576]{1,0:T(8,128)(2,1)S(1)} collective-permute-done((bf16[128,576]{1,0:T(8,128)(2,1)S(1)}, bf16[128,576]{1,0:T(8,128)(2,1)S(1)}, u32[]{:S(2)}, u32[]{:S(2)}) %collective-permute-start.12) | collective-permute-done | bytes 147488 | tf_op jit(solution)/shard_map/ppermute | solution.py:448
  43.7 0.0 copy-done.1
  43.7 0.0 copy-done.2
  43.7 1.6 %finish.1 = bf16[8,9216]{1,0:T(8,128)(2,1)} custom-call(f32[128,576]{1,0:T(8,128)S(1)} %get-tuple-element.51.mine_ref, bf16[128,576]{1,0:T(8,128)(2,1)S(1)} %collective-permute-done.12.theirs_ref, f32[1,512]{1,0:T(1,128)S(1)} %bitcast.15, s32[8]{0:T(128)S(1)} %copy-done.2, bf16[32,2432]{1,0:T(8,128)(2,1)S(1)} %get-tuple-element.53.arrived_ref), custom_call_target="tpu_custom_call" | custom-call | flops 37748736 | bytes 1048576 | tf_op jit(solution)/shard_map/finish/pallas_call | solution.py:432
  (5 shorter events, 0.0 us)
Async XLA Ops:
  0.6 16.8 %slice-start.8 = ((s8[14680064]{0:T(1024)(128)(4,1)}), s8[4194304]{0:T(1024)(128)(4,1)S(1)}, s32[]{:S(2)}) async-start(s8[14680064]{0:T(1024)(128)(4,1)} %bitcast.10), calls=%async_computation.8 | async-start | bytes 8388608
  1.7 13.1 %collective-permute-start.3 = (bf16[80,896]{1,0:T(8,128)(2,1)S(1)}, bf16[80,896]{1,0:T(8,128)(2,1)S(1)}, u32[]{:S(2)}, u32[]{:S(2)}) collective-permute-start(bf16[80,896]{1,0:T(8,128)(2,1)S(1)} %cut.1), channel_id=1, source_target_pairs={{0,8},{4,12},{8,0},{12,4},{1,9},{5,13},{9,1},{13,5},{2,10},{6,14},... | collective-permute-start | bytes 430088 | tf_op jit(solution)/shard_map/ppermute | solution.py:448
  5.8 15.9 %slice-start = ((s8[14680064]{0:T(1024)(128)(4,1)}), s8[4194304]{0:T(1024)(128)(4,1)S(1)}, s32[]{:S(2)}) async-start(s8[14680064]{0:T(1024)(128)(4,1)} %bitcast.6), calls=%async_computation | async-start | bytes 8388608
  5.8 15.9 %slice-start.4 = ((s8[14680064]{0:T(1024)(128)(4,1)}), s8[4194304]{0:T(1024)(128)(4,1)S(1)}, s32[]{:S(2)}) async-start(s8[14680064]{0:T(1024)(128)(4,1)} %bitcast.8), calls=%async_computation.4 | async-start | bytes 8388608
  5.8 11.5 %slice-start.9 = ((s8[14680064]{0:T(1024)(128)(4,1)}), s8[4194304]{0:T(1024)(128)(4,1)S(1)}, s32[]{:S(2)}) async-start(s8[14680064]{0:T(1024)(128)(4,1)} %bitcast.10), calls=%async_computation.9 | async-start | bytes 8388608
  5.8 11.6 %slice-start.10 = ((s8[14680064]{0:T(1024)(128)(4,1)}), s8[4194304]{0:T(1024)(128)(4,1)S(1)}, s32[]{:S(2)}) async-start(s8[14680064]{0:T(1024)(128)(4,1)} %bitcast.10), calls=%async_computation.10 | async-start | bytes 8388608
  5.8 11.6 %slice-start.11 = ((s8[14680064]{0:T(1024)(128)(4,1)}), s8[2097152]{0:T(1024)(128)(4,1)S(1)}, s32[]{:S(2)}) async-start(s8[14680064]{0:T(1024)(128)(4,1)} %bitcast.10), calls=%async_computation.11 | async-start | bytes 4194304
  5.9 15.9 %slice-start.1 = ((s8[14680064]{0:T(1024)(128)(4,1)}), s8[4194304]{0:T(1024)(128)(4,1)S(1)}, s32[]{:S(2)}) async-start(s8[14680064]{0:T(1024)(128)(4,1)} %bitcast.6), calls=%async_computation.1 | async-start | bytes 8388608
  5.9 15.9 %slice-start.2 = ((s8[14680064]{0:T(1024)(128)(4,1)}), s8[4194304]{0:T(1024)(128)(4,1)S(1)}, s32[]{:S(2)}) async-start(s8[14680064]{0:T(1024)(128)(4,1)} %bitcast.6), calls=%async_computation.2 | async-start | bytes 8388608
  5.9 15.9 %slice-start.3 = ((s8[14680064]{0:T(1024)(128)(4,1)}), s8[2097152]{0:T(1024)(128)(4,1)S(1)}, s32[]{:S(2)}) async-start(s8[14680064]{0:T(1024)(128)(4,1)} %bitcast.6), calls=%async_computation.3 | async-start | bytes 4194304
  5.9 15.9 %slice-start.5 = ((s8[14680064]{0:T(1024)(128)(4,1)}), s8[4194304]{0:T(1024)(128)(4,1)S(1)}, s32[]{:S(2)}) async-start(s8[14680064]{0:T(1024)(128)(4,1)} %bitcast.8), calls=%async_computation.5 | async-start | bytes 8388608
  5.9 15.8 %slice-start.6 = ((s8[14680064]{0:T(1024)(128)(4,1)}), s8[4194304]{0:T(1024)(128)(4,1)S(1)}, s32[]{:S(2)}) async-start(s8[14680064]{0:T(1024)(128)(4,1)} %bitcast.8), calls=%async_computation.6 | async-start | bytes 8388608
  5.9 15.8 %slice-start.7 = ((s8[14680064]{0:T(1024)(128)(4,1)}), s8[2097152]{0:T(1024)(128)(4,1)S(1)}, s32[]{:S(2)}) async-start(s8[14680064]{0:T(1024)(128)(4,1)} %bitcast.8), calls=%async_computation.7 | async-start | bytes 4194304
  7.9 5.0 %collective-permute-start = (bf16[8,3584]{1,0:T(8,128)(2,1)S(1)}, bf16[8,3584]{1,0:T(8,128)(2,1)S(1)}, u32[]{:S(2)}, u32[]{:S(2)}) collective-permute-start(bf16[8,3584]{1,0:T(8,128)(2,1)S(1)} %get-tuple-element.30), channel_id=1, source_target_pairs={{0,4},{4,0},{8,12},{12,8},{1,5},{5,1},{9,13},{13,9},{2,6},{6,2},{1... | collective-permute-start | bytes 172040 | tf_op jit(solution)/shard_map/ppermute | solution.py:448
  9.6 7.8 %collective-permute-start.1 = (bf16[8,3584]{1,0:T(8,128)(2,1)S(1)}, bf16[8,3584]{1,0:T(8,128)(2,1)S(1)}, u32[]{:S(2)}, u32[]{:S(2)}) collective-permute-start(bf16[8,3584]{1,0:T(8,128)(2,1)S(1)} %get-tuple-element.31), channel_id=1, source_target_pairs={{0,8},{4,12},{8,0},{12,4},{1,9},{5,13},{9,1},{13,5},{2,10},{6,14},... | collective-permute-start | bytes 172040 | tf_op jit(solution)/shard_map/ppermute | solution.py:448
  9.9 7.5 %collective-permute-start.2 = (bf16[8,3584]{1,0:T(8,128)(2,1)S(1)}, bf16[8,3584]{1,0:T(8,128)(2,1)S(1)}, u32[]{:S(2)}, u32[]{:S(2)}) collective-permute-start(bf16[8,3584]{1,0:T(8,128)(2,1)S(1)} %get-tuple-element.32), channel_id=1, source_target_pairs={{0,12},{4,8},{8,4},{12,0},{1,13},{5,9},{9,5},{13,1},{2,14},{6,10},... | collective-permute-start | bytes 172040 | tf_op jit(solution)/shard_map/ppermute | solution.py:448
  14.8 5.3 %collective-permute-start.4 = (bf16[80,896]{1,0:T(8,128)(2,1)S(1)}, bf16[80,896]{1,0:T(8,128)(2,1)S(1)}, u32[]{:S(2)}, u32[]{:S(2)}) collective-permute-start(bf16[80,896]{1,0:T(8,128)(2,1)S(1)} %collective-permute-done.3.refs_5_), channel_id=1, source_target_pairs={{0,2},{1,17},{2,0},{3,19},{16,18},{17,1},{18,16},{19,3},{4,6},{5,2... | collective-permute-start | bytes 430088 | tf_op jit(solution)/shard_map/ppermute | solution.py:482
  16.4 10.8 %collective-permute-start.5 = (bf16[128,1792]{1,0:T(8,128)(2,1)S(1)}, bf16[128,1792]{1,0:T(8,128)(2,1)S(1)}, u32[]{:S(2)}, u32[]{:S(2)}) collective-permute-start(bf16[128,1792]{1,0:T(8,128)(2,1)S(1)} %get-tuple-element.41), channel_id=1, source_target_pairs={{0,4},{4,0},{8,12},{12,8},{1,5},{5,1},{9,13},{13,9},{2,6},{6,2},{1... | collective-permute-start | bytes 1376264 | tf_op jit(solution)/shard_map/ppermute | solution.py:448
  20.1 7.1 %collective-permute-start.9 = (bf16[2,80,896]{2,1,0:T(8,128)(2,1)S(1)}, bf16[2,80,896]{2,1,0:T(8,128)(2,1)S(1)}, u32[]{:S(2)}, u32[]{:S(2)}) collective-permute-start(bf16[2,80,896]{2,1,0:T(8,128)(2,1)S(1)} %pad_maximum_fusion.refs_11_.refs_0_), channel_id=1, source_target_pairs={{0,16},{1,3},{2,18},{3,1},{16,0},{17,19},{18,2},{19,17},{4,20},{5,... | collective-permute-start | bytes 860168 | tf_op jit(solution)/shard_map/ppermute | solution.py:486
  21.7 11.2 %collective-permute-start.10 = (bf16[2,80,896]{2,1,0:T(8,128)(2,1)S(1)}, bf16[2,80,896]{2,1,0:T(8,128)(2,1)S(1)}, u32[]{:S(2)}, u32[]{:S(2)}) collective-permute-start(bf16[2,80,896]{2,1,0:T(8,128)(2,1)S(1)} %pad_maximum_fusion.refs_11_.refs_0_), channel_id=1, source_target_pairs={{0,1},{1,0},{2,3},{3,2},{4,5},{5,4},{6,7},{7,6},{8,9},{9,8},{10,11... | collective-permute-start | bytes 860168 | tf_op jit(solution)/shard_map/ppermute | solution.py:448
  21.8 11.1 %copy-start = (bf16[896,576]{0,1:T(8,128)(2,1)S(1)}, bf16[896,576]{0,1:T(8,128)(2,1)}, u32[]{:S(2)}) copy-start(bf16[896,576]{0,1:T(8,128)(2,1)} %param.15) | copy-start | bytes 3096580
  21.8 11.1 %copy-start.3 = (bf16[128,3584]{1,0:T(8,128)(2,1)S(1)}, bf16[128,3584]{1,0:T(8,128)(2,1)}, u32[]{:S(2)}) copy-start(bf16[128,3584]{1,0:T(8,128)(2,1)} %tokens_ref.1) | copy-start | bytes 2752516
  27.2 5.8 %collective-permute-start.11 = (bf16[2,80,896]{2,1,0:T(8,128)(2,1)S(1)}, bf16[2,80,896]{2,1,0:T(8,128)(2,1)S(1)}, u32[]{:S(2)}, u32[]{:S(2)}) collective-permute-start(bf16[2,80,896]{2,1,0:T(8,128)(2,1)S(1)} %collective-permute-done.9.refs_1_), channel_id=1, source_target_pairs={{0,1},{1,0},{2,3},{3,2},{4,5},{5,4},{6,7},{7,6},{8,9},{9,8},{10,11... | collective-permute-start | bytes 860168 | tf_op jit(solution)/shard_map/ppermute | solution.py:448
  27.6 8.6 %collective-permute-start.6 = (bf16[8,6016]{1,0:T(8,128)(2,1)S(1)}, bf16[8,6016]{1,0:T(8,128)(2,1)S(1)}, u32[]{:S(2)}, u32[]{:S(2)}) collective-permute-start(bf16[8,6016]{1,0:T(8,128)(2,1)S(1)} %get-tuple-element.44), channel_id=1, source_target_pairs={{0,4},{4,0},{8,12},{12,8},{1,5},{5,1},{9,13},{13,9},{2,6},{6,2},{1... | collective-permute-start | bytes 288776 | tf_op jit(solution)/shard_map/ppermute | solution.py:448
  28.9 11.7 %collective-permute-start.7 = (bf16[8,6016]{1,0:T(8,128)(2,1)S(1)}, bf16[8,6016]{1,0:T(8,128)(2,1)S(1)}, u32[]{:S(2)}, u32[]{:S(2)}) collective-permute-start(bf16[8,6016]{1,0:T(8,128)(2,1)S(1)} %get-tuple-element.46), channel_id=1, source_target_pairs={{0,8},{4,12},{8,0},{12,4},{1,9},{5,13},{9,1},{13,5},{2,10},{6,14},... | collective-permute-start | bytes 288776 | tf_op jit(solution)/shard_map/ppermute | solution.py:448
  32.9 7.7 %collective-permute-start.8 = (bf16[8,6016]{1,0:T(8,128)(2,1)S(1)}, bf16[8,6016]{1,0:T(8,128)(2,1)S(1)}, u32[]{:S(2)}, u32[]{:S(2)}) collective-permute-start(bf16[8,6016]{1,0:T(8,128)(2,1)S(1)} %get-tuple-element.48), channel_id=1, source_target_pairs={{0,12},{4,8},{8,4},{12,0},{1,13},{5,9},{9,5},{13,1},{2,14},{6,10},... | collective-permute-start | bytes 288776 | tf_op jit(solution)/shard_map/ppermute | solution.py:448
  35.6 8.2 %collective-permute-start.12 = (bf16[128,576]{1,0:T(8,128)(2,1)S(1)}, bf16[128,576]{1,0:T(8,128)(2,1)S(1)}, u32[]{:S(2)}, u32[]{:S(2)}) collective-permute-start(bf16[128,576]{1,0:T(8,128)(2,1)S(1)} %get-tuple-element.52), channel_id=1, source_target_pairs={{0,4},{4,0},{8,12},{12,8},{1,5},{5,1},{9,13},{13,9},{2,6},{6,2},{1... | collective-permute-start | bytes 442376 | tf_op jit(solution)/shard_map/ppermute | solution.py:448
  40.6 3.1 %copy-start.1 = (f32[512]{0:T(512)S(1)}, f32[512]{0:T(512)}, u32[]{:S(2)}) copy-start(f32[512]{0:T(512)} %param.16) | copy-start | bytes 6148
  40.6 3.1 %copy-start.2 = (s32[8]{0:T(128)S(1)}, s32[8]{0:T(128)}, u32[]{:S(2)}) copy-start(s32[8]{0:T(128)} %survive_ref.1) | copy-start | bytes 100

commit v3 on v2

--- a/solution.py
+++ b/solution.py
@@ -21,6 +21,7 @@
 VMEM = pltpu.VMEM
 SMEM = pltpu.SMEM
 CHUNK = 512
+PIECES = 4
 NT = (((1,), (1,)), ((), ()))
 TN = (((0,), (0,)), ((), ()))
 
@@ -71,9 +72,10 @@
 
 def open_kernel(page_span, *refs):
     sources, outs = refs[:5], refs[5:]
-    sends, mixing_ref, pages = outs[:EXPERTS], outs[EXPERTS], outs[EXPERTS + 1 : 2 * EXPERTS + 1]
-    across_ref = outs[2 * EXPERTS + 1]
-    *held, sems = outs[2 * EXPERTS + 2 :]
+    sends, mixing_ref, pages = outs[:EXPERTS], outs[EXPERTS], outs[EXPERTS + 1 : 2 * EXPERTS]
+    across_ref = outs[2 * EXPERTS]
+    *held, sems = outs[2 * EXPERTS + 1 :]
+    model_width = sends[0].shape[1]
     ids_ref, weight_ref, tokens_ref, old_ref, target_ref = held
     copies = [
         pltpu.make_async_copy(source, target, sems.at[at])
@@ -108,7 +110,7 @@
         placed.astype(jnp.bfloat16), tokens_ref[...], preferred_element_type=jnp.float32
     )
     for at in range(EXPERTS):
-        sends[at][...] = outgoing[at * CAP : (at + 1) * CAP].astype(jnp.bfloat16)
+        sends[at][:, :model_width] = outgoing[at * CAP : (at + 1) * CAP].astype(jnp.bfloat16)
     page_count, width = old_ref.shape
     row_count = EXPERTS * PER_PAIR * SPLIT
     out_row = lax.broadcasted_iota(jnp.int32, (row_count, page_count), 0)
@@ -140,8 +142,11 @@
         )
     for at in range(EXPERTS):
         rows = slice(at * PER_PAIR * SPLIT, (at + 1) * PER_PAIR * SPLIT)
-        pages[at][:, :width] = moved[rows].astype(jnp.bfloat16)
-        pages[at][:, width:] = tags[rows].astype(jnp.bfloat16)
+        page = jnp.concatenate([moved[rows], tags[rows]], axis=1).astype(jnp.bfloat16)
+        if at == 1:
+            sends[at][:, model_width:] = page
+        else:
+            pages[at - (at > 1)][...] = page
 
 
 def open_work(ids, weights, tokens, old_latents, old_target, shard):
@@ -150,6 +155,7 @@
     send = jax.ShapeDtypeStruct((CAP, model_width), jnp.bfloat16)
     mixing = jax.ShapeDtypeStruct((EXPERTS * CAP, token_count), jnp.float32)
     page = jax.ShapeDtypeStruct((PER_PAIR * SPLIT, page_width // SPLIT + LANES), jnp.bfloat16)
+    longer = jax.ShapeDtypeStruct((CAP, model_width + page.shape[1]), jnp.bfloat16)
     across = jax.ShapeDtypeStruct((token_count, 2 * shard), jnp.bfloat16)
     spec = pl.BlockSpec(memory_space=VMEM)
     inputs = [
@@ -158,9 +164,9 @@
     ]
     results = pl.pallas_call(
         functools.partial(open_kernel, page_count * lax.axis_size("dp")),
-        out_shape=(send,) * EXPERTS + (mixing,) + (page,) * EXPERTS + (across,),
+        out_shape=(send, longer, send, send, mixing) + (page,) * (EXPERTS - 1) + (across,),
         in_specs=[pl.BlockSpec(memory_space=pltpu.HBM)] * 5,
-        out_specs=(spec,) * (2 * EXPERTS + 2),
+        out_specs=(spec,) * (2 * EXPERTS + 1),
         scratch_shapes=[VMEM(value.shape, value.dtype) for value in inputs[:4]]
         + [
             SMEM(old_target.shape, old_target.dtype),
@@ -173,7 +179,7 @@
         name="open",
     )(*inputs)
     sends, mixing, rest = results[:EXPERTS], results[EXPERTS], results[EXPERTS + 1 :]
-    return sends, mixing, rest[:EXPERTS], rest[EXPERTS]
+    return sends, mixing, rest[: EXPERTS - 1], rest[EXPERTS - 1]
 
 
 def stacked_rows(refs):
@@ -184,7 +190,7 @@
 
 def gate_kernel(*refs):
     rows, gate_ref, out_ref = refs[:EXPERTS], refs[EXPERTS], refs[-1]
-    block = stacked_rows(rows)
+    block = stacked_rows([row.at[:, : gate_ref.shape[0]] for row in rows])
     for at in range(0, gate_ref.shape[1], CHUNK):
         columns = slice(at, at + CHUNK)
         out_ref[:, columns] = jnp.dot(
@@ -214,11 +220,11 @@
 def expert_kernel(*refs):
     rows, refs = refs[:EXPERTS], refs[EXPERTS:]
     gates_ref, up_ref, down_ref = refs[:3]
-    pages, outs, hidden_ref = refs[3 : 3 + EXPERTS], refs[-EXPERTS - 1 : -1], refs[-1]
+    pages, outs, hidden_ref = refs[3:5], refs[-EXPERTS - 1 : -1], refs[-1]
     model_width = down_ref.shape[1]
-    for peer in range(EXPERTS):
-        outs[peer][:, model_width:] = pages[peer][...]
-    block = stacked_rows(rows)
+    for out, page in zip(outs[2:], pages):
+        out[:, model_width:] = page[...]
+    block = stacked_rows([row.at[:, :model_width] for row in rows])
     for at in range(0, up_ref.shape[1], CHUNK):
         columns = slice(at, at + CHUNK)
         gate = gates_ref[:, columns]
@@ -241,9 +247,11 @@
     row_count = EXPERTS * CAP
     return pl.pallas_call(
         expert_kernel,
-        out_shape=(jax.ShapeDtypeStruct((CAP, model_width + pages[0].shape[1]), jnp.bfloat16),)
-        * EXPERTS,
-        in_specs=[spec] * (3 + 2 * EXPERTS) + [unread] * len(after),
+        out_shape=tuple(
+            jax.ShapeDtypeStruct((CAP, model_width + extra), jnp.bfloat16)
+            for extra in (0, 0, pages[0].shape[1], pages[1].shape[1])
+        ),
+        in_specs=[spec] * (5 + EXPERTS) + [unread] * len(after),
         out_specs=(spec,) * EXPERTS,
         scratch_shapes=[VMEM((row_count, unit_count), jnp.bfloat16)],
         compiler_params=pltpu.CompilerParams(vmem_limit_bytes=4 << 20),
@@ -257,42 +265,60 @@
 
 
 def combine_kernel(mixing_ref, *refs):
-    rows, parts, (out_ref, pages_ref) = refs[:EXPERTS], refs[EXPERTS:-2], refs[-2:]
-    block = stacked_rows(rows)
-
-    @pl.when(pl.program_id(0) == 0)
-    def _():
-        columns = pl.ds(parts[0].shape[1] - pages_ref.shape[1], pages_ref.shape[1])
-        pages_ref[...] = stacked_rows([part.at[:, columns] for part in parts])
-
+    rows, parts = refs[:EXPERTS], refs[EXPERTS : EXPERTS + 2]
+    out_ref, carried_ref, held_ref, sems = refs[EXPERTS + 2 :]
+    model_width = out_ref.shape[1]
     mixing = mixing_ref[...]
     high = mixing.astype(jnp.bfloat16).astype(jnp.float32)
     mixing = jnp.concatenate([high, mixing - high], axis=0).astype(jnp.bfloat16)
-    block = jnp.concatenate([block, block], axis=0)
-    total = lax.dot_general(mixing, block, TN, preferred_element_type=jnp.float32)
-    out_ref[...] = total.astype(jnp.bfloat16)
-
-
-def combine(mixing, rows, model_width):
+    block = jnp.concatenate([stacked_rows([row.at[:, :model_width] for row in rows])] * 2, axis=0)
+    width = model_width // PIECES
+    copies = []
+    for at in range(PIECES):
+        columns = slice(at * width, (at + 1) * width)
+        total = lax.dot_general(mixing, block[:, columns], TN, preferred_element_type=jnp.float32)
+        held_ref[:, columns] = total.astype(jnp.bfloat16)
+        copies.append(
+            pltpu.make_async_copy(held_ref.at[:, columns], out_ref.at[:, columns], sems.at[at])
+        )
+        copies[-1].start()
+    page_count, page_width = carried_ref.shape
+    part_width = page_width // SPLIT
+    arrivals = stacked_rows(
+        [parts[0]] + [row.at[:, model_width:] for row in (parts[1], rows[2], rows[3])]
+    )
+    row_count = arrivals.shape[0]
+    slot = lax.broadcasted_iota(jnp.int32, (row_count, page_count), 1).astype(jnp.float32)
+    part_of = lax.broadcasted_iota(jnp.int32, (row_count, page_count), 0) % SPLIT
+    meant = arrivals[:, part_width:].astype(jnp.float32)[:, :1] == slot + 1.0
+    for part in range(SPLIT):
+        carried_ref[:, part * part_width : (part + 1) * part_width] = lax.dot_general(
+            jnp.where(meant & (part_of == part), 1.0, 0.0).astype(jnp.bfloat16),
+            arrivals[:, :part_width],
+            TN,
+            preferred_element_type=jnp.float32,
+        )
+    for copy in copies:
+        copy.wait()
+
+
+def combine(mixing, rows, own_pages, near_rows, page_count):
     slot_count, token_count = mixing.shape
-    width = model_width // 2
-    page_width = rows[0].shape[1] - model_width
-    columns = pl.BlockSpec((CAP, width), lambda at: (0, at))
-    whole = pl.BlockSpec(rows[0].shape, lambda at: (0, 0))
+    model_width = rows[0].shape[1]
+    page_width = (own_pages.shape[1] - LANES) * SPLIT
+    spec = pl.BlockSpec(memory_space=VMEM)
     return pl.pallas_call(
         combine_kernel,
-        grid=(model_width // width,),
         out_shape=(
             jax.ShapeDtypeStruct((token_count, model_width), jnp.bfloat16),
-            jax.ShapeDtypeStruct((slot_count, page_width), jnp.bfloat16),
-        ),
-        in_specs=[pl.BlockSpec((slot_count, token_count), lambda at: (0, 0))]
-        + [columns] * EXPERTS
-        + [whole] * EXPERTS,
-        out_specs=(
-            pl.BlockSpec((token_count, width), lambda at: (0, at)),
-            pl.BlockSpec((slot_count, page_width), lambda at: (0, 0)),
-        ),
+            jax.ShapeDtypeStruct((page_count, page_width), jnp.float32),
+        ),
+        in_specs=[spec] * (3 + EXPERTS),
+        out_specs=(pl.BlockSpec(memory_space=pltpu.HBM), spec),
+        scratch_shapes=[
+            VMEM((token_count, model_width), jnp.bfloat16),
+            pltpu.SemaphoreType.DMA((PIECES,)),
+        ],
         compiler_params=pltpu.CompilerParams(vmem_limit_bytes=8 << 20),
         cost_estimate=pl.CostEstimate(
             flops=11530000000,
@@ -300,117 +326,88 @@
             transcendentals=0,
         ),
         name="combine",
-    )(mixing, *rows, *rows)
+    )(mixing, *rows, own_pages, near_rows)
 
 
 def project_kernel(tokens_ref, theirs_ref, own_ref, *refs):
-    held, (mine_out, theirs_out) = refs[:4], refs[-5:-3]
-    both_ref, far_ref, sems = refs[-3:]
+    held, (mine_out, theirs_out) = refs[:4], refs[-4:-2]
+    both_ref, far_ref = refs[-2:]
     group, me, dp = (lax.axis_index(axis) for axis in ("groups", "expert", "dp"))
     shard = own_ref.shape[1]
     chip_rows, core_rows = piece_rows(own_ref.shape[0])
     chip, core = group * 2 + dp // 2, dp % 2
 
-    def copies_of(my_core):
-        copies = []
+    def assemble(my_core):
         for which in range(2):
             core_at = my_core if which == 0 else 1 - my_core
             near_xor = 1 if core_at == 0 else 2
+            skip = 0 if core_at == 0 else 2 * core_rows - chip_rows
+            count = core_rows - skip
             for at, chip_xor in enumerate((0, near_xor, 3 - near_xor, 3)):
-                buffer = held[2 * which + at // 2].at[at % 2]
-                skip = 0 if core_at == 0 else 2 * core_rows - chip_rows
                 start = (chip ^ chip_xor) * chip_rows + (0 if core_at == 0 else core_rows)
-                count = core_rows - skip
-                copies.append(
-                    pltpu.make_async_copy(
-                        buffer.at[pl.ds(skip, count)],
-                        far_ref.at[pl.ds(pl.multiple_of(start, ROWS), count)],
-                        sems.at[len(copies)],
-                    )
-                )
-        return copies
-
-    def on_each_core(act):
-        for my_core in range(2):
-
-            @pl.when(core == my_core)
-            def _(my_core=my_core):
-                for copy in copies_of(my_core):
-                    act(copy)
-
-    def part(left, weights_ref):
-        return lax.dot_general(left, weights_ref[...], NT, preferred_element_type=jnp.float32)
-
-    on_each_core(lambda copy: copy.start())
+                rows = pl.ds(pl.multiple_of(start, ROWS), count)
+                far_ref[rows, :] = held[2 * which + at // 2][at % 2, skip:, :]
+
+    for my_core in range(2):
+        pl.when(core == my_core)(functools.partial(assemble, my_core))
+
+    def part(weights_ref, tokens):
+        return lax.dot_general(weights_ref[...], tokens, NT, preferred_element_type=jnp.float32)
+
     count = tokens_ref.shape[0]
     for half, bit in enumerate((0, 2)):
         columns = pl.ds(pl.multiple_of((me ^ bit) * shard, LANES), shard)
         both_ref[:count, half * shard : (half + 1) * shard] = tokens_ref[:, columns]
     both_ref[count:, :] = theirs_ref[...]
-    total = part(both_ref[:, :shard], own_ref)
-    on_each_core(lambda copy: copy.wait())
-    total = total + part(both_ref[:, shard:], far_ref)
-    mine_out[...] = total[:count]
-    theirs_out[...] = total[count:].astype(jnp.bfloat16)
-
-
-def project(tokens, theirs, own, held, after):
-    vmem, hbm = pl.BlockSpec(memory_space=VMEM), pl.BlockSpec(memory_space=pl.ANY)
+    total = part(own_ref, both_ref[:, :shard])
+    total = total + part(far_ref, both_ref[:, shard:])
+    mine_out[...] = total[:, :count]
+    theirs_out[...] = total[:, count:].astype(jnp.bfloat16)
+
+
+def project(tokens, theirs, own, held):
+    spec = pl.BlockSpec(memory_space=VMEM)
     token_count = tokens.shape[0]
     width, shard = own.shape
     return pl.pallas_call(
         project_kernel,
         out_shape=(
-            jax.ShapeDtypeStruct((token_count, width), jnp.float32),
-            jax.ShapeDtypeStruct((token_count, width), jnp.bfloat16),
-        ),
-        in_specs=[vmem] * 3 + [hbm] * (4 + len(after)),
-        out_specs=(vmem, vmem),
+            jax.ShapeDtypeStruct((width, token_count), jnp.float32),
+            jax.ShapeDtypeStruct((width, token_count), jnp.bfloat16),
+        ),
+        in_specs=[spec] * 7,
+        out_specs=(spec, spec),
         scratch_shapes=[
             VMEM((2 * token_count, 2 * shard), jnp.bfloat16),
             VMEM((width, shard), jnp.bfloat16),
-            pltpu.SemaphoreType.DMA((8,)),
         ],
         compiler_params=pltpu.CompilerParams(vmem_limit_bytes=8 << 20),
-        cost_estimate=pl.CostEstimate(
-            flops=1153000000, bytes_accessed=0, transcendentals=0
-        ),
+        cost_estimate=pl.CostEstimate(flops=1153000000, bytes_accessed=0, transcendentals=0),
         name="project",
-    )(tokens, theirs, own, *held, *after)
-
-
-def finish_kernel(mine_ref, theirs_ref, gain_ref, survive_ref, arrived_ref, out_ref):
-    page_count, page_width = out_ref.shape
+    )(tokens, theirs, own, *held)
+
+
+def finish_kernel(mine_ref, theirs_ref, gain_ref, survive_ref, carried_ref, out_ref):
+    page_count = out_ref.shape[0]
     projected = mine_ref[...] + theirs_ref[...].astype(jnp.float32)
-    nope_part = projected[:, :KV]
-    inv_rms = lax.rsqrt(jnp.mean(nope_part * nope_part, axis=1, keepdims=True) + EPS)
-    rebuilt = jnp.concatenate([nope_part * inv_rms * gain_ref[...], projected[:, KV:]], axis=1)
-    rebuilt = rebuilt.astype(jnp.bfloat16)
-    token_count, width = rebuilt.shape
+    nope_part = projected[:KV]
+    inv_rms = lax.rsqrt(jnp.mean(nope_part * nope_part, axis=0, keepdims=True) + EPS)
+    scaled = jnp.concatenate([nope_part * inv_rms, projected[KV:]], axis=0)
+    high = scaled.astype(jnp.bfloat16)
+    low = (scaled - high.astype(jnp.float32)).astype(jnp.bfloat16)
+    width, token_count = scaled.shape
     page_tokens = token_count // page_count
     row = lax.broadcasted_iota(jnp.int32, (token_count, token_count), 0)
     source = lax.broadcasted_iota(jnp.int32, (token_count, token_count), 1)
     moves = source == (row % page_count) * page_tokens + row // page_count
-    ordered = jnp.dot(
-        jnp.where(moves, 1.0, 0.0).astype(jnp.bfloat16),
-        rebuilt,
+    moves = jnp.where(moves, 1.0, 0.0).astype(jnp.bfloat16)
+    ordered = lax.dot_general(
+        jnp.concatenate([moves, moves], axis=1),
+        jnp.concatenate([high, low], axis=1),
+        NT,
         preferred_element_type=jnp.float32,
     )
-    part_width = page_width // SPLIT
-    row_count = arrived_ref.shape[0]
-    slot = lax.broadcasted_iota(jnp.int32, (row_count, page_count), 1).astype(jnp.float32)
-    part_of = lax.broadcasted_iota(jnp.int32, (row_count, page_count), 0) % SPLIT
-    meant = arrived_ref[:, part_width:].astype(jnp.float32)[:, :1] == slot + 1.0
-    arrivals = arrived_ref[:, :part_width]
-    carried = [
-        lax.dot_general(
-            jnp.where(meant & (part_of == part), 1.0, 0.0).astype(jnp.bfloat16),
-            arrivals,
-            TN,
-            preferred_element_type=jnp.float32,
-        )
-        for part in range(SPLIT)
-    ]
+    ordered = jnp.concatenate([ordered[:, :KV] * gain_ref[...], ordered[:, KV:]], axis=1)
     page_row = lax.broadcasted_iota(jnp.int32, (page_count, 2 * width), 0)
     survives = jnp.zeros((page_count, 2 * width), jnp.int32)
     for at in range(page_count):
@@ -421,17 +418,15 @@
             axis=1,
         )
         columns = slice(at * width, (at + 2) * width)
-        start = at * width % part_width
-        kept = carried[at * width // part_width][:, start : start + 2 * width]
-        chosen = jnp.where(survives > 0, kept, fresh)
+        chosen = jnp.where(survives > 0, carried_ref[:, columns], fresh)
         out_ref[:, columns] = chosen.astype(jnp.bfloat16)
 
 
-def finish(mine, theirs, latent_gain, survive, arrived, page_count, page_width):
+def finish(mine, theirs, latent_gain, survive, carried):
     vmem = pl.BlockSpec(memory_space=VMEM)
     return pl.pallas_call(
         finish_kernel,
-        out_shape=jax.ShapeDtypeStruct((page_count, page_width), jnp.bfloat16),
+        out_shape=jax.ShapeDtypeStruct(carried.shape, jnp.bfloat16),
         in_specs=[vmem] * 3 + [pl.BlockSpec(memory_space=SMEM), vmem],
         out_specs=vmem,
         compiler_params=pltpu.CompilerParams(vmem_limit_bytes=6 << 20),
@@ -441,7 +436,7 @@
             transcendentals=mine.shape[0],
         ),
         name="finish",
-    )(mine, theirs, latent_gain.reshape(1, -1), survive, arrived)
+    )(mine, theirs, latent_gain.reshape(1, -1), survive, carried)
 
 
 def swap(value, axis, bit):
@@ -472,13 +467,15 @@
     group_count, dp_count = lax.axis_size("groups"), lax.axis_size("dp")
     plane = ("groups", "dp")
     latent = w_latent.T
-    piece = cut(latent)
+    at = lax.axis_index("groups") * 2 + lax.axis_index("dp") // 2
+    chip_rows, core_rows = piece_rows(latent.shape[0])
+    start = at * chip_rows + lax.axis_index("dp") % 2 * (chip_rows - core_rows)
+    piece = lax.dynamic_slice_in_dim(latent, start, core_rows, axis=0)
     far_piece = swap(piece, "expert", 2)
-    sends, mixing, pages, across = open_work(
+    sends, mixing, (own_pages, *pages), across = open_work(
         route_ids.T, route_weight.T, tokens, old_latents, old_target, latent.shape[1]
     )
     received = exchanged(sends)
-    far_piece = tied(far_piece, received[1])
     first = lax.ppermute(far_piece, plane, plane_pairs(group_count, dp_count, True))
     theirs = swap(tied(across, far_piece), "expert", 1)
     gate = gates(received, w_gate, (far_piece,))
@@ -491,11 +488,11 @@
     far = tied(far, results[0])
     far_other = swap(far, "dp", 1)
     mine, across_sums = project(
-        tokens, theirs, latent, (near, far, near_other, far_other), ()
+        tokens, theirs, latent, (near, far, near_other, far_other)
     )
     their_sums = swap(across_sums, "expert", 1)
-    moe_out, arrived = combine(mixing, returned, tokens.shape[1])
-    latents = finish(mine, their_sums, latent_gain, survive, arrived, *old_latents.shape)
+    moe_out, carried = combine(mixing, returned, own_pages, received[1], old_latents.shape[0])
+    latents = finish(mine, their_sums, latent_gain, survive, carried)
     return (moe_out, latents)
 
 

time: 45.5 us -> 44.4 us (0.976)
  Pallas kernels: 16.6 us -> 13.5 us
  local copies, waits for them, and re-layouts: 0.08 us -> 0.98 us
  waiting for transfers between devices: 8.71 us -> 9.6 us
    pallas_call x5 -> x4, Pallas kernels: 11.9 us -> 8.9 us  [the longest x1 5.17 us: experts(): pl.pallas_call(expert_kernel, out_shape=tuple((jax.ShapeDtypeStruct((CAP,...]
    dynamic_slice x0 -> x1, local copies, waits for them, and re-layouts: none -> 0.93 us  [block_shards(): piece = lax.dynamic_slice_in_dim(latent, start, core_rows, axis=0)]
    ppermute x11, waiting for transfers between devices: 8.7 us -> 9.6 us  [swap(): return lax.ppermute(value, axis, xor_pairs(lax.axis_size(axis), bit))]
  transfers between devices with their start and end apart: 13 -> 13, of which waited for: 5 -> 4; matrix products, arithmetic and copies ran while one was open for 0% -> 0% of each run, Pallas kernels for 31% -> 27%
where the time goes in v3:
time: 44.4 us; the launch traced here: 44.2 us
  starting transfers between devices  19.2 us (43%)
  Pallas kernels  13.5 us (30%)
  waiting for transfers between devices  9.6 us (22%)
  local copies, waits for them, and re-layouts  0.98 us (2%)
  between operations  0.86 us (2%)
    ppermute x11, starting transfers between devices, swap(): return lax.ppermute(value, axis, xor_pairs(lax.axis_size(axis), bit))  16 us
    ppermute x11, waiting for transfers between devices, swap(): return lax.ppermute(value, axis, xor_pairs(lax.axis_size(axis), bit))  9.6 us
    pallas_call x1, Pallas kernels, experts(): pl.pallas_call(expert_kernel, out_shape=tuple((jax.ShapeDtypeStruct((CAP,...  5.17 us
    pallas_call x1, Pallas kernels, gates(): pl.pallas_call(gate_kernel, out_shape=jax.ShapeDtypeStruct((row_count, un...  2.63 us
    pallas_call x1, Pallas kernels, open_work(): pl.pallas_call(functools.partial(open_kernel, page_count * lax.axis_size(...  2.02 us
    pallas_call x1, Pallas kernels, finish(): pl.pallas_call(finish_kernel, out_shape=jax.ShapeDtypeStruct(carried.shap...  1.61 us
    ppermute x1, starting transfers between devices, block_shards(): lax.ppermute(far_piece, plane, plane_pairs(group_count, dp_count, True))  1.59 us
    ppermute x1, starting transfers between devices, block_shards(): far = lax.ppermute(near, plane, plane_pairs(group_count, dp_count, False))  1.59 us
  transfers between devices with their start and end apart: 13, of which 4 were waited for; matrix products, arithmetic and copies ran while one was open for 0% of the time, Pallas kernels for 27%

profile of v3, /device:TPU:0, one launch (start us, length us, event | category | flops | bytes accessed | tf_op | source)
XLA Modules:
  0.0 44.2 jit_solution(17399436889446059608)
XLA Ops:
  0.7 0.9 %dynamic-slice_bitcast_fusion = bf16[80,896]{1,0:T(8,128)(2,1)S(1)} fusion(bf16[896,576]{0,1:T(8,128)(2,1)} %param.15, s32[]{:T(128)S(6)} %select_n.16), kind=kLoop, calls=%fused_computation.1 | loop fusion | bytes 286724 | tf_op jit(solution)/shard_map/dynamic_slice | solution.py:473
  1.6 4.1 %collective-permute-start.3 = (bf16[80,896]{1,0:T(8,128)(2,1)S(1)}, bf16[80,896]{1,0:T(8,128)(2,1)S(1)}, u32[]{:S(2)}, u32[]{:S(2)}) collective-permute-start(bf16[80,896]{1,0:T(8,128)(2,1)S(1)} %dynamic-slice_bitcast_fusion), channel_id=1, source_target_pairs={{0,8},{4,12},{8,0},{12,4},{1,9},{5,13},{9,1},{13,5},{2,10},{6,14},... | collective-permute-start | bytes 430088 | tf_op jit(solution)/shard_map/ppermute | solution.py:443
  5.7 0.0 slice-start
  5.7 0.0 slice-start.4
  5.7 0.0 copy-start
  5.7 0.0 slice-start.1
  5.7 0.0 slice-start.2
  5.7 0.0 slice-start.3
  5.7 0.0 slice-start.5
  5.7 0.0 slice-start.6
  5.7 0.0 slice-start.7
  5.7 2.0 %open.1 = (bf16[8,3584]{1,0:T(8,128)(2,1)S(1)}, bf16[8,6016]{1,0:T(8,128)(2,1)S(1)}, bf16[8,3584]{1,0:T(8,128)(2,1)S(1)}, bf16[8,3584]{1,0:T(8,128)(2,1)S(1)}, f...) custom-call(s32[8,128]{1,0:T(8,128)} %bitcast.16, ...), custom_call_target="tpu_custom_call" | custom-call | flops 20000000000 | bytes 2097152 | tf_op jit(solution)/shard_map/open/pallas_call | solution.py:165
  7.8 1.6 %collective-permute-start = (bf16[8,6016]{1,0:T(8,128)(2,1)S(1)}, bf16[8,6016]{1,0:T(8,128)(2,1)S(1)}, u32[]{:S(2)}, u32[]{:S(2)}) collective-permute-start(bf16[8,6016]{1,0:T(8,128)(2,1)S(1)} %get-tuple-element.28), channel_id=1, source_target_pairs={{0,4},{4,0},{8,12},{12,8},{1,5},{5,1},{9,13},{13,9},{2,6},{6,2},{1... | collective-permute-start | bytes 288776 | tf_op jit(solution)/shard_map/ppermute | solution.py:443
  9.4 0.3 collective-permute-start.1
  9.8 2.5 %collective-permute-start.2 = (bf16[8,3584]{1,0:T(8,128)(2,1)S(1)}, bf16[8,3584]{1,0:T(8,128)(2,1)S(1)}, u32[]{:S(2)}, u32[]{:S(2)}) collective-permute-start(bf16[8,3584]{1,0:T(8,128)(2,1)S(1)} %get-tuple-element.30), channel_id=1, source_target_pairs={{0,12},{4,8},{8,4},{12,0},{1,13},{5,9},{9,5},{13,1},{2,14},{6,10},... | collective-permute-start | bytes 172040 | tf_op jit(solution)/shard_map/ppermute | solution.py:443
  12.2 2.5 %collective-permute-done.3.refs_5_ = bf16[80,896]{1,0:T(8,128)(2,1)S(1)} collective-permute-done((bf16[80,896]{1,0:T(8,128)(2,1)S(1)}, bf16[80,896]{1,0:T(8,128)(2,1)S(1)}, u32[]{:S(2)}, u32[]{:S(2)}) %collective-permute-start.3) | collective-permute-done | bytes 143392 | tf_op jit(solution)/shard_map/ppermute | solution.py:443
  14.7 1.6 %collective-permute-start.4 = (bf16[80,896]{1,0:T(8,128)(2,1)S(1)}, bf16[80,896]{1,0:T(8,128)(2,1)S(1)}, u32[]{:S(2)}, u32[]{:S(2)}) collective-permute-start(bf16[80,896]{1,0:T(8,128)(2,1)S(1)} %collective-permute-done.3.refs_5_), channel_id=1, source_target_pairs={{0,2},{1,17},{2,0},{3,19},{16,18},{17,1},{18,16},{19,3},{4,6},{5,2... | collective-permute-start | bytes 430088 | tf_op jit(solution)/shard_map/ppermute | solution.py:479
  16.3 0.9 %collective-permute-start.5 = (bf16[128,1792]{1,0:T(8,128)(2,1)S(1)}, bf16[128,1792]{1,0:T(8,128)(2,1)S(1)}, u32[]{:S(2)}, u32[]{:S(2)}) collective-permute-start(bf16[128,1792]{1,0:T(8,128)(2,1)S(1)} %get-tuple-element.36), channel_id=1, source_target_pairs={{0,4},{4,0},{8,12},{12,8},{1,5},{5,1},{9,13},{13,9},{2,6},{6,2},{1... | collective-permute-start | bytes 1376264 | tf_op jit(solution)/shard_map/ppermute | solution.py:443
  17.3 0.0 collective-permute-done.1.refs_2_
  17.3 0.0 collective-permute-done.2.refs_3_
  17.3 0.0 collective-permute-done.refs_1_.refs_5_
  17.3 0.0 copy-done
  17.3 2.6 %gates.1.refs_4_ = f32[32,2048]{1,0:T(8,128)S(1)} custom-call(bf16[8,3584]{1,0:T(8,128)(2,1)S(1)} %get-tuple-element.27.refs_0_, bf16[8,6016]{1,0:T(8,128)(2,1)S(1)} %collective-permute-done.refs_1_.refs_5_, bf16[8,3584]{1,0:T(8,128)(2,1)S(1)} %collective-permute-done.1.refs_2_, bf16[8,3584]{1,0:T(8,128)(2,1)S(1)} %collective-permute-done.2.refs_3_, ...), custom_call_target="tpu_custom_call" | custom-call | flops 939524096 | bytes 29360128 | tf_op jit(solution)/shard_map/gates/pallas_call | solution.py:205
  19.9 0.0 collective-permute-done.4
  20.0 1.6 %collective-permute-start.9 = (bf16[2,80,896]{2,1,0:T(8,128)(2,1)S(1)}, bf16[2,80,896]{2,1,0:T(8,128)(2,1)S(1)}, u32[]{:S(2)}, u32[]{:S(2)}) collective-permute-start(bf16[2,80,896]{2,1,0:T(8,128)(2,1)S(1)} %pad_maximum_fusion.refs_9_.refs_0_), channel_id=1, source_target_pairs={{0,16},{1,3},{2,18},{3,1},{16,0},{17,19},{18,2},{19,17},{4,20},{5,... | collective-permute-start | bytes 860168 | tf_op jit(solution)/shard_map/ppermute | solution.py:483
  21.6 0.0 collective-permute-start.10
  21.6 0.0 slice-done
  21.6 0.0 slice-done.4
  21.6 0.0 slice-done.1
  21.6 0.0 slice-done.2
  21.6 0.0 slice-done.3
  21.6 0.0 slice-done.5
  21.6 0.0 slice-done.6
  21.6 0.0 slice-done.7
  21.7 0.0 copy-start.1
  21.7 0.0 copy-start.4
  21.7 5.2 %experts.1 = (bf16[8,3584]{1,0:T(8,128)(2,1)S(1)}, bf16[8,3584]{1,0:T(8,128)(2,1)S(1)}, bf16[8,6016]{1,0:T(8,128)(2,1)S(1)}, bf16[8,6016]{1,0:T(8,128)(2,1)S(1)}) custom-call(bf16[8,3584]{1,0:T(8,128)(2,1)S(1)} %get-tuple-element.27.refs_0_, bf16[8,6016]{1,0:T(8,128)(2,1)S(1)} %collective-permute-done.refs_1_.refs_5_, ...), custom_call_target="tpu_custom_call" | custom-call | flops 469762048 | bytes 14680064 | tf_op jit(solution)/shard_map/experts/pallas_call | solution.py:248
  26.9 0.1 collective-permute-done.5.theirs_ref
  26.9 0.0 collective-permute-done.9.refs_1_
  26.9 0.5 %collective-permute-start.11 = (bf16[2,80,896]{2,1,0:T(8,128)(2,1)S(1)}, bf16[2,80,896]{2,1,0:T(8,128)(2,1)S(1)}, u32[]{:S(2)}, u32[]{:S(2)}) collective-permute-start(bf16[2,80,896]{2,1,0:T(8,128)(2,1)S(1)} %collective-permute-done.9.refs_1_), channel_id=1, source_target_pairs={{0,1},{1,0},{2,3},{3,2},{4,5},{5,4},{6,7},{7,6},{8,9},{9,8},{10,11... | collective-permute-start | bytes 860168 | tf_op jit(solution)/shard_map/ppermute | solution.py:443
  27.4 1.2 %collective-permute-start.6 = (bf16[8,3584]{1,0:T(8,128)(2,1)S(1)}, bf16[8,3584]{1,0:T(8,128)(2,1)S(1)}, u32[]{:S(2)}, u32[]{:S(2)}) collective-permute-start(bf16[8,3584]{1,0:T(8,128)(2,1)S(1)} %get-tuple-element.39), channel_id=1, source_target_pairs={{0,4},{4,0},{8,12},{12,8},{1,5},{5,1},{9,13},{13,9},{2,6},{6,2},{1... | collective-permute-start | bytes 172040 | tf_op jit(solution)/shard_map/ppermute | solution.py:443
  28.7 4.1 %collective-permute-start.7 = (bf16[8,6016]{1,0:T(8,128)(2,1)S(1)}, bf16[8,6016]{1,0:T(8,128)(2,1)S(1)}, u32[]{:S(2)}, u32[]{:S(2)}) collective-permute-start(bf16[8,6016]{1,0:T(8,128)(2,1)S(1)} %get-tuple-element.41), channel_id=1, source_target_pairs={{0,8},{4,12},{8,0},{12,4},{1,9},{5,13},{9,1},{13,5},{2,10},{6,14},... | collective-permute-start | bytes 288776 | tf_op jit(solution)/shard_map/ppermute | solution.py:443
  32.8 0.0 collective-permute-start.8
  32.8 0.0 collective-permute-done.10.refs_2_
  32.8 0.0 collective-permute-done.11.refs_3_
  32.8 0.0 copy-done.1
  32.8 0.0 copy-done.4
  32.8 0.9 %project.1 = (f32[576,128]{1,0:T(8,128)S(1)}, bf16[576,128]{1,0:T(8,128)(2,1)S(1)}) custom-call(bf16[128,3584]{1,0:T(8,128)(2,1)S(1)} %copy-done.4, bf16[128,1792]{1,0:T(8,128)(2,1)S(1)} %collective-permute-done.5.theirs_ref, bf16[576,896]{1,0:T(8,128)(2,1)S(1)} %bitcast.13, bf16[2,80,896]{2,1,0:T(8,128)(2,1)S(1)} %pad_maximum_fusion.refs_9_.refs_0_, ...), custom_call_target="tpu_custom_call" | custom-call | flops 1152999936 | tf_op jit(solution)/shard_map/project/pallas_call | solution.py:372
  33.8 0.6 %collective-permute-start.12 = (bf16[576,128]{1,0:T(8,128)(2,1)S(1)}, bf16[576,128]{1,0:T(8,128)(2,1)S(1)}, u32[]{:S(2)}, u32[]{:S(2)}) collective-permute-start(bf16[576,128]{1,0:T(8,128)(2,1)S(1)} %get-tuple-element.48), channel_id=1, source_target_pairs={{0,4},{4,0},{8,12},{12,8},{1,5},{5,1},{9,13},{13,9},{2,6},{6,2},{1... | collective-permute-start | bytes 442376 | tf_op jit(solution)/shard_map/ppermute | solution.py:443
  34.4 0.0 collective-permute-done.6.refs_1_
  34.4 6.1 %collective-permute-done.7.refs_2_ = bf16[8,6016]{1,0:T(8,128)(2,1)S(1)} collective-permute-done((bf16[8,6016]{1,0:T(8,128)(2,1)S(1)}, bf16[8,6016]{1,0:T(8,128)(2,1)S(1)}, u32[]{:S(2)}, u32[]{:S(2)}) %collective-permute-start.7) | collective-permute-done | bytes 96288 | tf_op jit(solution)/shard_map/ppermute | solution.py:443
  40.5 0.0 collective-permute-done.8.refs_3_
  40.5 0.0 copy-start.2
  40.5 0.0 copy-start.3
  40.5 1.2 %combine.1 = (bf16[128,3584]{1,0:T(8,128)(2,1)}, f32[8,9216]{1,0:T(8,128)S(1)}) custom-call(f32[32,128]{1,0:T(8,128)S(1)} %get-tuple-element.26.mixing_ref, bf16[8,3584]{1,0:T(8,128)(2,1)S(1)} %get-tuple-element.37.refs_0_, bf16[8,3584]{1,0:T(8,128)(2,1)S(1)} %collective-permute-done.6.refs_1_, bf16[8,6016]{1,0:T(8,128)(2,1)S(1)} %collective-permute-done.7.refs_2_, ...), custom_call_target="tpu_custom_call" | custom-call | flops 11530000384 | bytes 1376256 | tf_op jit(solution)/shard_map/combine/pallas_call | solution.py:310
  41.7 0.9 %collective-permute-done.12.theirs_ref = bf16[576,128]{1,0:T(8,128)(2,1)S(1)} collective-permute-done((bf16[576,128]{1,0:T(8,128)(2,1)S(1)}, bf16[576,128]{1,0:T(8,128)(2,1)S(1)}, u32[]{:S(2)}, u32[]{:S(2)}) %collective-permute-start.12) | collective-permute-done | bytes 147488 | tf_op jit(solution)/shard_map/ppermute | solution.py:443
  42.6 0.0 copy-done.2
  42.6 0.0 copy-done.3
  42.6 1.6 %finish.1 = bf16[8,9216]{1,0:T(8,128)(2,1)} custom-call(f32[576,128]{1,0:T(8,128)S(1)} %get-tuple-element.47.mine_ref, bf16[576,128]{1,0:T(8,128)(2,1)S(1)} %collective-permute-done.12.theirs_ref, f32[1,512]{1,0:T(1,128)S(1)} %bitcast.14, s32[8]{0:T(128)S(1)} %copy-done.3, f32[8,9216]{1,0:T(8,128)S(1)} %get-tuple-element.49.carried_ref), custom_call_target="tpu_custom_call" | custom-call | flops 169869312 | bytes 1048576 | tf_op jit(solution)/shard_map/finish/pallas_call | solution.py:427
  (3 shorter events, 0.0 us)
Async XLA Ops:
  1.6 13.2 %collective-permute-start.3 = (bf16[80,896]{1,0:T(8,128)(2,1)S(1)}, bf16[80,896]{1,0:T(8,128)(2,1)S(1)}, u32[]{:S(2)}, u32[]{:S(2)}) collective-permute-start(bf16[80,896]{1,0:T(8,128)(2,1)S(1)} %dynamic-slice_bitcast_fusion), channel_id=1, source_target_pairs={{0,8},{4,12},{8,0},{12,4},{1,9},{5,13},{9,1},{13,5},{2,10},{6,14},... | collective-permute-start | bytes 430088 | tf_op jit(solution)/shard_map/ppermute | solution.py:443
  5.7 15.9 %slice-start = ((s8[14680064]{0:T(1024)(128)(4,1)}), s8[4194304]{0:T(1024)(128)(4,1)S(1)}, s32[]{:S(2)}) async-start(s8[14680064]{0:T(1024)(128)(4,1)} %bitcast.8), calls=%async_computation | async-start | bytes 8388608
  5.7 15.9 %slice-start.4 = ((s8[14680064]{0:T(1024)(128)(4,1)}), s8[4194304]{0:T(1024)(128)(4,1)S(1)}, s32[]{:S(2)}) async-start(s8[14680064]{0:T(1024)(128)(4,1)} %bitcast.10), calls=%async_computation.4 | async-start | bytes 8388608
  5.7 11.6 %copy-start = (bf16[3584,2048]{1,0:T(8,128)(2,1)S(1)}, bf16[3584,2048]{1,0:T(8,128)(2,1)}, u32[]{:S(2)}) copy-start(bf16[3584,2048]{1,0:T(8,128)(2,1)} %refs_4_.3) | copy-start | bytes 44040196
  5.7 15.9 %slice-start.1 = ((s8[14680064]{0:T(1024)(128)(4,1)}), s8[4194304]{0:T(1024)(128)(4,1)S(1)}, s32[]{:S(2)}) async-start(s8[14680064]{0:T(1024)(128)(4,1)} %bitcast.8), calls=%async_computation.1 | async-start | bytes 8388608
  5.7 15.9 %slice-start.2 = ((s8[14680064]{0:T(1024)(128)(4,1)}), s8[4194304]{0:T(1024)(128)(4,1)S(1)}, s32[]{:S(2)}) async-start(s8[14680064]{0:T(1024)(128)(4,1)} %bitcast.8), calls=%async_computation.2 | async-start | bytes 8388608
  5.7 15.9 %slice-start.3 = ((s8[14680064]{0:T(1024)(128)(4,1)}), s8[2097152]{0:T(1024)(128)(4,1)S(1)}, s32[]{:S(2)}) async-start(s8[14680064]{0:T(1024)(128)(4,1)} %bitcast.8), calls=%async_computation.3 | async-start | bytes 4194304
  5.7 15.9 %slice-start.5 = ((s8[14680064]{0:T(1024)(128)(4,1)}), s8[4194304]{0:T(1024)(128)(4,1)S(1)}, s32[]{:S(2)}) async-start(s8[14680064]{0:T(1024)(128)(4,1)} %bitcast.10), calls=%async_computation.5 | async-start | bytes 8388608
  5.7 15.9 %slice-start.6 = ((s8[14680064]{0:T(1024)(128)(4,1)}), s8[4194304]{0:T(1024)(128)(4,1)S(1)}, s32[]{:S(2)}) async-start(s8[14680064]{0:T(1024)(128)(4,1)} %bitcast.10), calls=%async_computation.6 | async-start | bytes 8388608
  5.7 15.9 %slice-start.7 = ((s8[14680064]{0:T(1024)(128)(4,1)}), s8[2097152]{0:T(1024)(128)(4,1)S(1)}, s32[]{:S(2)}) async-start(s8[14680064]{0:T(1024)(128)(4,1)} %bitcast.10), calls=%async_computation.7 | async-start | bytes 4194304
  7.8 9.5 %collective-permute-start = (bf16[8,6016]{1,0:T(8,128)(2,1)S(1)}, bf16[8,6016]{1,0:T(8,128)(2,1)S(1)}, u32[]{:S(2)}, u32[]{:S(2)}) collective-permute-start(bf16[8,6016]{1,0:T(8,128)(2,1)S(1)} %get-tuple-element.28), channel_id=1, source_target_pairs={{0,4},{4,0},{8,12},{12,8},{1,5},{5,1},{9,13},{13,9},{2,6},{6,2},{1... | collective-permute-start | bytes 288776 | tf_op jit(solution)/shard_map/ppermute | solution.py:443
  9.4 7.8 %collective-permute-start.1 = (bf16[8,3584]{1,0:T(8,128)(2,1)S(1)}, bf16[8,3584]{1,0:T(8,128)(2,1)S(1)}, u32[]{:S(2)}, u32[]{:S(2)}) collective-permute-start(bf16[8,3584]{1,0:T(8,128)(2,1)S(1)} %get-tuple-element.29), channel_id=1, source_target_pairs={{0,8},{4,12},{8,0},{12,4},{1,9},{5,13},{9,1},{13,5},{2,10},{6,14},... | collective-permute-start | bytes 172040 | tf_op jit(solution)/shard_map/ppermute | solution.py:443
  9.8 7.5 %collective-permute-start.2 = (bf16[8,3584]{1,0:T(8,128)(2,1)S(1)}, bf16[8,3584]{1,0:T(8,128)(2,1)S(1)}, u32[]{:S(2)}, u32[]{:S(2)}) collective-permute-start(bf16[8,3584]{1,0:T(8,128)(2,1)S(1)} %get-tuple-element.30), channel_id=1, source_target_pairs={{0,12},{4,8},{8,4},{12,0},{1,13},{5,9},{9,5},{13,1},{2,14},{6,10},... | collective-permute-start | bytes 172040 | tf_op jit(solution)/shard_map/ppermute | solution.py:443
  14.7 5.2 %collective-permute-start.4 = (bf16[80,896]{1,0:T(8,128)(2,1)S(1)}, bf16[80,896]{1,0:T(8,128)(2,1)S(1)}, u32[]{:S(2)}, u32[]{:S(2)}) collective-permute-start(bf16[80,896]{1,0:T(8,128)(2,1)S(1)} %collective-permute-done.3.refs_5_), channel_id=1, source_target_pairs={{0,2},{1,17},{2,0},{3,19},{16,18},{17,1},{18,16},{19,3},{4,6},{5,2... | collective-permute-start | bytes 430088 | tf_op jit(solution)/shard_map/ppermute | solution.py:479
  16.3 10.6 %collective-permute-start.5 = (bf16[128,1792]{1,0:T(8,128)(2,1)S(1)}, bf16[128,1792]{1,0:T(8,128)(2,1)S(1)}, u32[]{:S(2)}, u32[]{:S(2)}) collective-permute-start(bf16[128,1792]{1,0:T(8,128)(2,1)S(1)} %get-tuple-element.36), channel_id=1, source_target_pairs={{0,4},{4,0},{8,12},{12,8},{1,5},{5,1},{9,13},{13,9},{2,6},{6,2},{1... | collective-permute-start | bytes 1376264 | tf_op jit(solution)/shard_map/ppermute | solution.py:443
  20.0 6.9 %collective-permute-start.9 = (bf16[2,80,896]{2,1,0:T(8,128)(2,1)S(1)}, bf16[2,80,896]{2,1,0:T(8,128)(2,1)S(1)}, u32[]{:S(2)}, u32[]{:S(2)}) collective-permute-start(bf16[2,80,896]{2,1,0:T(8,128)(2,1)S(1)} %pad_maximum_fusion.refs_9_.refs_0_), channel_id=1, source_target_pairs={{0,16},{1,3},{2,18},{3,1},{16,0},{17,19},{18,2},{19,17},{4,20},{5,... | collective-permute-start | bytes 860168 | tf_op jit(solution)/shard_map/ppermute | solution.py:483
  21.6 11.2 %collective-permute-start.10 = (bf16[2,80,896]{2,1,0:T(8,128)(2,1)S(1)}, bf16[2,80,896]{2,1,0:T(8,128)(2,1)S(1)}, u32[]{:S(2)}, u32[]{:S(2)}) collective-permute-start(bf16[2,80,896]{2,1,0:T(8,128)(2,1)S(1)} %pad_maximum_fusion.refs_9_.refs_0_), channel_id=1, source_target_pairs={{0,1},{1,0},{2,3},{3,2},{4,5},{5,4},{6,7},{7,6},{8,9},{9,8},{10,11... | collective-permute-start | bytes 860168 | tf_op jit(solution)/shard_map/ppermute | solution.py:443
  21.7 11.2 %copy-start.1 = (bf16[896,576]{0,1:T(8,128)(2,1)S(1)}, bf16[896,576]{0,1:T(8,128)(2,1)}, u32[]{:S(2)}) copy-start(bf16[896,576]{0,1:T(8,128)(2,1)} %param.15) | copy-start | bytes 3096580
  21.7 11.2 %copy-start.4 = (bf16[128,3584]{1,0:T(8,128)(2,1)S(1)}, bf16[128,3584]{1,0:T(8,128)(2,1)}, u32[]{:S(2)}) copy-start(bf16[128,3584]{1,0:T(8,128)(2,1)} %tokens_ref.1) | copy-start | bytes 2752516
  26.9 5.9 %collective-permute-start.11 = (bf16[2,80,896]{2,1,0:T(8,128)(2,1)S(1)}, bf16[2,80,896]{2,1,0:T(8,128)(2,1)S(1)}, u32[]{:S(2)}, u32[]{:S(2)}) collective-permute-start(bf16[2,80,896]{2,1,0:T(8,128)(2,1)S(1)} %collective-permute-done.9.refs_1_), channel_id=1, source_target_pairs={{0,1},{1,0},{2,3},{3,2},{4,5},{5,4},{6,7},{7,6},{8,9},{9,8},{10,11... | collective-permute-start | bytes 860168 | tf_op jit(solution)/shard_map/ppermute | solution.py:443
  27.4 7.0 %collective-permute-start.6 = (bf16[8,3584]{1,0:T(8,128)(2,1)S(1)}, bf16[8,3584]{1,0:T(8,128)(2,1)S(1)}, u32[]{:S(2)}, u32[]{:S(2)}) collective-permute-start(bf16[8,3584]{1,0:T(8,128)(2,1)S(1)} %get-tuple-element.39), channel_id=1, source_target_pairs={{0,4},{4,0},{8,12},{12,8},{1,5},{5,1},{9,13},{13,9},{2,6},{6,2},{1... | collective-permute-start | bytes 172040 | tf_op jit(solution)/shard_map/ppermute | solution.py:443
  28.7 11.8 %collective-permute-start.7 = (bf16[8,6016]{1,0:T(8,128)(2,1)S(1)}, bf16[8,6016]{1,0:T(8,128)(2,1)S(1)}, u32[]{:S(2)}, u32[]{:S(2)}) collective-permute-start(bf16[8,6016]{1,0:T(8,128)(2,1)S(1)} %get-tuple-element.41), channel_id=1, source_target_pairs={{0,8},{4,12},{8,0},{12,4},{1,9},{5,13},{9,1},{13,5},{2,10},{6,14},... | collective-permute-start | bytes 288776 | tf_op jit(solution)/shard_map/ppermute | solution.py:443
  32.8 7.7 %collective-permute-start.8 = (bf16[8,6016]{1,0:T(8,128)(2,1)S(1)}, bf16[8,6016]{1,0:T(8,128)(2,1)S(1)}, u32[]{:S(2)}, u32[]{:S(2)}) collective-permute-start(bf16[8,6016]{1,0:T(8,128)(2,1)S(1)} %get-tuple-element.43), channel_id=1, source_target_pairs={{0,12},{4,8},{8,4},{12,0},{1,13},{5,9},{9,5},{13,1},{2,14},{6,10},... | collective-permute-start | bytes 288776 | tf_op jit(solution)/shard_map/ppermute | solution.py:443
  33.8 8.8 %collective-permute-start.12 = (bf16[576,128]{1,0:T(8,128)(2,1)S(1)}, bf16[576,128]{1,0:T(8,128)(2,1)S(1)}, u32[]{:S(2)}, u32[]{:S(2)}) collective-permute-start(bf16[576,128]{1,0:T(8,128)(2,1)S(1)} %get-tuple-element.48), channel_id=1, source_target_pairs={{0,4},{4,0},{8,12},{12,8},{1,5},{5,1},{9,13},{13,9},{2,6},{6,2},{1... | collective-permute-start | bytes 442376 | tf_op jit(solution)/shard_map/ppermute | solution.py:443
  40.5 2.1 %copy-start.2 = (f32[512]{0:T(512)S(1)}, f32[512]{0:T(512)}, u32[]{:S(2)}) copy-start(f32[512]{0:T(512)} %param.16) | copy-start | bytes 6148
  40.5 2.1 %copy-start.3 = (s32[8]{0:T(128)S(1)}, s32[8]{0:T(128)}, u32[]{:S(2)}) copy-start(s32[8]{0:T(128)} %survive_ref.1) | copy-start | bytes 100

commit v4 on v3

--- a/solution.py
+++ b/solution.py
@@ -22,6 +22,7 @@
 SMEM = pltpu.SMEM
 CHUNK = 512
 PIECES = 4
+ORDER = (0, 3, 1, 2)
 NT = (((1,), (1,)), ((), ()))
 TN = (((0,), (0,)), ((), ()))
 
@@ -41,33 +42,7 @@
 
 
 def piece_rows(width):
-    chip = width // 4
-    core = -(-(chip // 2) // ROWS) * ROWS
-    return chip, core
-
-
-def cut_kernel(latent_ref, piece_ref, sem):
-    group, dp = lax.axis_index("groups"), lax.axis_index("dp")
-    chip_rows, core_rows = piece_rows(latent_ref.shape[0])
-    start = (group * 2 + dp // 2) * chip_rows + (dp % 2) * (chip_rows - core_rows)
-    piece = pltpu.make_async_copy(
-        latent_ref.at[pl.ds(pl.multiple_of(start, ROWS), core_rows)], piece_ref, sem
-    )
-    piece.start()
-    piece.wait()
-
-
-def cut(latent):
-    width, shard = latent.shape
-    return pl.pallas_call(
-        cut_kernel,
-        out_shape=jax.ShapeDtypeStruct((piece_rows(width)[1], shard), jnp.bfloat16),
-        in_specs=[pl.BlockSpec(memory_space=pltpu.HBM)],
-        out_specs=pl.BlockSpec(memory_space=VMEM),
-        scratch_shapes=[pltpu.SemaphoreType.DMA],
-        compiler_params=pltpu.CompilerParams(vmem_limit_bytes=1 << 20),
-        name="cut",
-    )(pltpu.with_memory_space_constraint(latent, pltpu.HBM))
+    return width // 4, width // 8
 
 
 def open_kernel(page_span, *refs):
@@ -266,6 +241,7 @@
 
 def combine_kernel(mixing_ref, *refs):
     rows, parts = refs[:EXPERTS], refs[EXPERTS : EXPERTS + 2]
+    rows = [rows[ORDER.index(at)] for at in range(EXPERTS)]
     out_ref, carried_ref, held_ref, sems = refs[EXPERTS + 2 :]
     model_width = out_ref.shape[1]
     mixing = mixing_ref[...]
@@ -292,12 +268,14 @@
     part_of = lax.broadcasted_iota(jnp.int32, (row_count, page_count), 0) % SPLIT
     meant = arrivals[:, part_width:].astype(jnp.float32)[:, :1] == slot + 1.0
     for part in range(SPLIT):
-        carried_ref[:, part * part_width : (part + 1) * part_width] = lax.dot_general(
+        chosen = lax.dot_general(
             jnp.where(meant & (part_of == part), 1.0, 0.0).astype(jnp.bfloat16),
             arrivals[:, :part_width],
             TN,
             preferred_element_type=jnp.float32,
         )
+        columns = slice(part * part_width, (part + 1) * part_width)
+        carried_ref[:, columns] = chosen.astype(jnp.bfloat16)
     for copy in copies:
         copy.wait()
 
@@ -311,7 +289,7 @@
         combine_kernel,
         out_shape=(
             jax.ShapeDtypeStruct((token_count, model_width), jnp.bfloat16),
-            jax.ShapeDtypeStruct((page_count, page_width), jnp.float32),
+            jax.ShapeDtypeStruct((page_count, page_width), jnp.bfloat16),
         ),
         in_specs=[spec] * (3 + EXPERTS),
         out_specs=(pl.BlockSpec(memory_space=pltpu.HBM), spec),
@@ -326,7 +304,7 @@
             transcendentals=0,
         ),
         name="combine",
-    )(mixing, *rows, own_pages, near_rows)
+    )(mixing, *(rows[at] for at in ORDER), own_pages, near_rows)
 
 
 def project_kernel(tokens_ref, theirs_ref, own_ref, *refs):
@@ -334,19 +312,19 @@
     both_ref, far_ref = refs[-2:]
     group, me, dp = (lax.axis_index(axis) for axis in ("groups", "expert", "dp"))
     shard = own_ref.shape[1]
-    chip_rows, core_rows = piece_rows(own_ref.shape[0])
+    chip_rows, _ = piece_rows(own_ref.shape[0])
     chip, core = group * 2 + dp // 2, dp % 2
 
     def assemble(my_core):
-        for which in range(2):
-            core_at = my_core if which == 0 else 1 - my_core
-            near_xor = 1 if core_at == 0 else 2
-            skip = 0 if core_at == 0 else 2 * core_rows - chip_rows
-            count = core_rows - skip
-            for at, chip_xor in enumerate((0, near_xor, 3 - near_xor, 3)):
-                start = (chip ^ chip_xor) * chip_rows + (0 if core_at == 0 else core_rows)
-                rows = pl.ds(pl.multiple_of(start, ROWS), count)
-                far_ref[rows, :] = held[2 * which + at // 2][at % 2, skip:, :]
+        orders = ((0, 1, 2, 3), (0, 2, 1, 3))
+        for chip_xor in range(4):
+            halves = []
+            for core_at in range(2):
+                at = orders[core_at].index(chip_xor)
+                buffer = held[at // 2 + (0 if core_at == my_core else 2)]
+                halves.append(buffer[at % 2].astype(jnp.float32))
+            rows = pl.ds(pl.multiple_of((chip ^ chip_xor) * chip_rows, ROWS), chip_rows)
+            far_ref[rows, :] = jnp.concatenate(halves, axis=0).astype(jnp.bfloat16)
 
     for my_core in range(2):
         pl.when(core == my_core)(functools.partial(assemble, my_core))
@@ -387,7 +365,8 @@
     )(tokens, theirs, own, *held)
 
 
-def finish_kernel(mine_ref, theirs_ref, gain_ref, survive_ref, carried_ref, out_ref):
+def finish_kernel(mine_ref, theirs_ref, gain_ref, unread_ref, out_ref):
+    del unread_ref
     page_count = out_ref.shape[0]
     projected = mine_ref[...] + theirs_ref[...].astype(jnp.float32)
     nope_part = projected[:KV]
@@ -408,35 +387,29 @@
         preferred_element_type=jnp.float32,
     )
     ordered = jnp.concatenate([ordered[:, :KV] * gain_ref[...], ordered[:, KV:]], axis=1)
-    page_row = lax.broadcasted_iota(jnp.int32, (page_count, 2 * width), 0)
-    survives = jnp.zeros((page_count, 2 * width), jnp.int32)
-    for at in range(page_count):
-        survives = jnp.where(page_row == at, survive_ref[at], survives)
     for at in range(0, page_tokens, 2):
         fresh = jnp.concatenate(
             [ordered[(at + half) * page_count : (at + half + 1) * page_count] for half in range(2)],
             axis=1,
         )
-        columns = slice(at * width, (at + 2) * width)
-        chosen = jnp.where(survives > 0, carried_ref[:, columns], fresh)
-        out_ref[:, columns] = chosen.astype(jnp.bfloat16)
-
-
-def finish(mine, theirs, latent_gain, survive, carried):
+        out_ref[:, at * width : (at + 2) * width] = fresh.astype(jnp.bfloat16)
+
+
+def finish(mine, theirs, latent_gain, carried):
     vmem = pl.BlockSpec(memory_space=VMEM)
     return pl.pallas_call(
         finish_kernel,
         out_shape=jax.ShapeDtypeStruct(carried.shape, jnp.bfloat16),
-        in_specs=[vmem] * 3 + [pl.BlockSpec(memory_space=SMEM), vmem],
+        in_specs=[vmem] * 3 + [pl.BlockSpec(memory_space=pl.ANY)],
         out_specs=vmem,
         compiler_params=pltpu.CompilerParams(vmem_limit_bytes=6 << 20),
         cost_estimate=pl.CostEstimate(
-            flops=4 * mine.shape[0] ** 2 * mine.shape[1],
+            flops=4 * mine.shape[1] ** 2 * mine.shape[0],
             bytes_accessed=1 << 20,
-            transcendentals=mine.shape[0],
+            transcendentals=mine.shape[1],
         ),
         name="finish",
-    )(mine, theirs, latent_gain.reshape(1, -1), survive, carried)
+    )(mine, theirs, latent_gain.reshape(1, -1), carried)
 
 
 def swap(value, axis, bit):
@@ -469,7 +442,7 @@
     latent = w_latent.T
     at = lax.axis_index("groups") * 2 + lax.axis_index("dp") // 2
     chip_rows, core_rows = piece_rows(latent.shape[0])
-    start = at * chip_rows + lax.axis_index("dp") % 2 * (chip_rows - core_rows)
+    start = at * chip_rows + lax.axis_index("dp") % 2 * core_rows
     piece = lax.dynamic_slice_in_dim(latent, start, core_rows, axis=0)
     far_piece = swap(piece, "expert", 2)
     sends, mixing, (own_pages, *pages), across = open_work(
@@ -492,7 +465,8 @@
     )
     their_sums = swap(across_sums, "expert", 1)
     moe_out, carried = combine(mixing, returned, own_pages, received[1], old_latents.shape[0])
-    latents = finish(mine, their_sums, latent_gain, survive, carried)
+    fresh = finish(mine, their_sums, latent_gain, carried)
+    latents = jnp.where((survive > 0)[:, None], carried, fresh)
     return (moe_out, latents)
 
 

time: 44.4 us -> 41.4 us (0.932)
  waiting for transfers between devices: 9.6 us -> 7.2 us
  Pallas kernels: 13.5 us -> 12.4 us
  other arithmetic: 0.05 us -> 0.79 us
    ppermute x11, waiting for transfers between devices: 9.6 us -> 7.19 us  [swap(): return lax.ppermute(value, axis, xor_pairs(lax.axis_size(axis), bit))]
    pallas_call x1, Pallas kernels: 1.61 us -> 0.41 us  [finish(): pl.pallas_call(finish_kernel, out_shape=jax.ShapeDtypeStruct(carried.shap...]
    select_n x0 -> x1, other arithmetic: none -> 0.74 us  [block_shards(): latents = jnp.where((survive > 0)[:, None], carried, fresh)]
  transfers between devices with their start and end apart: 13 -> 13, of which waited for: 4 -> 5; matrix products, arithmetic and copies ran while one was open for 0% -> 0% of each run, Pallas kernels for 27% -> 29%
where the time goes in v4:
time: 41.4 us; the launch traced here: 41.3 us
  starting transfers between devices  19 us (46%)
  Pallas kernels  12.4 us (30%)
  waiting for transfers between devices  7.2 us (17%)
  local copies, waits for them, and re-layouts  0.98 us (2%)
  between operations  0.88 us (2%)
  other arithmetic  0.79 us (2%)
    ppermute x11, starting transfers between devices, swap(): return lax.ppermute(value, axis, xor_pairs(lax.axis_size(axis), bit))  15.8 us
    ppermute x11, waiting for transfers between devices, swap(): return lax.ppermute(value, axis, xor_pairs(lax.axis_size(axis), bit))  7.19 us
    pallas_call x1, Pallas kernels, experts(): pl.pallas_call(expert_kernel, out_shape=tuple((jax.ShapeDtypeStruct((CAP,...  5.18 us
    pallas_call x1, Pallas kernels, gates(): pl.pallas_call(gate_kernel, out_shape=jax.ShapeDtypeStruct((row_count, un...  2.63 us
    pallas_call x1, Pallas kernels, open_work(): pl.pallas_call(functools.partial(open_kernel, page_count * lax.axis_size(...  2.02 us
    ppermute x1, starting transfers between devices, block_shards(): far = lax.ppermute(near, plane, plane_pairs(group_count, dp_count, False))  1.73 us
    ppermute x1, starting transfers between devices, block_shards(): lax.ppermute(far_piece, plane, plane_pairs(group_count, dp_count, True))  1.5 us
    pallas_call x1, Pallas kernels, combine(): pl.pallas_call(combine_kernel, out_shape=(jax.ShapeDtypeStruct((token_cou...  1.21 us
  transfers between devices with their start and end apart: 13, of which 5 were waited for; matrix products, arithmetic and copies ran while one was open for 0% of the time, Pallas kernels for 29%

profile of v4, /device:TPU:0, one launch (start us, length us, event | category | flops | bytes accessed | tf_op | source)
XLA Modules:
  0.0 41.3 jit_solution(8255048546184056672)
XLA Ops:
  0.7 0.9 %dynamic-slice_bitcast_fusion = bf16[72,896]{1,0:T(8,128)(2,1)S(1)} fusion(bf16[896,576]{0,1:T(8,128)(2,1)} %param.15, s32[]{:T(128)S(6)} %select_n.20), kind=kLoop, calls=%fused_computation.2 | loop fusion | bytes 258052 | tf_op jit(solution)/shard_map/dynamic_slice | solution.py:446
  1.6 4.1 %collective-permute-start.3 = (bf16[72,896]{1,0:T(8,128)(2,1)S(1)}, bf16[72,896]{1,0:T(8,128)(2,1)S(1)}, u32[]{:S(2)}, u32[]{:S(2)}) collective-permute-start(bf16[72,896]{1,0:T(8,128)(2,1)S(1)} %dynamic-slice_bitcast_fusion), channel_id=1, source_target_pairs={{0,8},{4,12},{8,0},{12,4},{1,9},{5,13},{9,1},{13,5},{2,10},{6,14},... | collective-permute-start | bytes 387080 | tf_op jit(solution)/shard_map/ppermute | solution.py:416
  5.7 0.0 slice-start
  5.7 0.0 slice-start.4
  5.7 0.0 copy-start
  5.7 0.0 slice-start.1
  5.7 0.0 slice-start.2
  5.7 0.0 slice-start.3
  5.7 0.0 slice-start.5
  5.7 0.0 slice-start.6
  5.7 0.0 slice-start.7
  5.7 2.0 %open.1 = (bf16[8,3584]{1,0:T(8,128)(2,1)S(1)}, bf16[8,6016]{1,0:T(8,128)(2,1)S(1)}, bf16[8,3584]{1,0:T(8,128)(2,1)S(1)}, bf16[8,3584]{1,0:T(8,128)(2,1)S(1)}, f...) custom-call(s32[8,128]{1,0:T(8,128)} %bitcast.16, ...), custom_call_target="tpu_custom_call" | custom-call | flops 20000000000 | bytes 2097152 | tf_op jit(solution)/shard_map/open/pallas_call | solution.py:140
  7.8 1.6 %collective-permute-start = (bf16[8,6016]{1,0:T(8,128)(2,1)S(1)}, bf16[8,6016]{1,0:T(8,128)(2,1)S(1)}, u32[]{:S(2)}, u32[]{:S(2)}) collective-permute-start(bf16[8,6016]{1,0:T(8,128)(2,1)S(1)} %get-tuple-element.28), channel_id=1, source_target_pairs={{0,4},{4,0},{8,12},{12,8},{1,5},{5,1},{9,13},{13,9},{2,6},{6,2},{1... | collective-permute-start | bytes 288776 | tf_op jit(solution)/shard_map/ppermute | solution.py:416
  9.4 0.3 collective-permute-start.1
  9.7 2.5 %collective-permute-start.2 = (bf16[8,3584]{1,0:T(8,128)(2,1)S(1)}, bf16[8,3584]{1,0:T(8,128)(2,1)S(1)}, u32[]{:S(2)}, u32[]{:S(2)}) collective-permute-start(bf16[8,3584]{1,0:T(8,128)(2,1)S(1)} %get-tuple-element.30), channel_id=1, source_target_pairs={{0,12},{4,8},{8,4},{12,0},{1,13},{5,9},{9,5},{13,1},{2,14},{6,10},... | collective-permute-start | bytes 172040 | tf_op jit(solution)/shard_map/ppermute | solution.py:416
  12.2 0.0 collective-permute-done.3.refs_5_
  12.2 1.5 %collective-permute-start.4 = (bf16[72,896]{1,0:T(8,128)(2,1)S(1)}, bf16[72,896]{1,0:T(8,128)(2,1)S(1)}, u32[]{:S(2)}, u32[]{:S(2)}) collective-permute-start(bf16[72,896]{1,0:T(8,128)(2,1)S(1)} %collective-permute-done.3.refs_5_), channel_id=1, source_target_pairs={{0,2},{1,17},{2,0},{3,19},{16,18},{17,1},{18,16},{19,3},{4,6},{5,2... | collective-permute-start | bytes 387080 | tf_op jit(solution)/shard_map/ppermute | solution.py:452
  13.7 1.5 %collective-permute-start.5 = (bf16[128,1792]{1,0:T(8,128)(2,1)S(1)}, bf16[128,1792]{1,0:T(8,128)(2,1)S(1)}, u32[]{:S(2)}, u32[]{:S(2)}) collective-permute-start(bf16[128,1792]{1,0:T(8,128)(2,1)S(1)} %get-tuple-element.36), channel_id=1, source_target_pairs={{0,4},{4,0},{8,12},{12,8},{1,5},{5,1},{9,13},{13,9},{2,6},{6,2},{1... | collective-permute-start | bytes 1376264 | tf_op jit(solution)/shard_map/ppermute | solution.py:416
  15.2 1.1 %collective-permute-done.1.refs_2_ = bf16[8,3584]{1,0:T(8,128)(2,1)S(1)} collective-permute-done((bf16[8,3584]{1,0:T(8,128)(2,1)S(1)}, bf16[8,3584]{1,0:T(8,128)(2,1)S(1)}, u32[]{:S(2)}, u32[]{:S(2)}) %collective-permute-start.1) | collective-permute-done | bytes 57376 | tf_op jit(solution)/shard_map/ppermute | solution.py:416
  16.3 0.0 collective-permute-done.2.refs_3_
  16.3 0.0 collective-permute-done.refs_1_.refs_5_
  16.3 0.0 copy-done
  16.3 2.6 %gates.1.refs_4_ = f32[32,2048]{1,0:T(8,128)S(1)} custom-call(bf16[8,3584]{1,0:T(8,128)(2,1)S(1)} %get-tuple-element.27.refs_0_, bf16[8,6016]{1,0:T(8,128)(2,1)S(1)} %collective-permute-done.refs_1_.refs_5_, bf16[8,3584]{1,0:T(8,128)(2,1)S(1)} %collective-permute-done.1.refs_2_, bf16[8,3584]{1,0:T(8,128)(2,1)S(1)} %collective-permute-done.2.refs_3_, ...), custom_call_target="tpu_custom_call" | custom-call | flops 939524096 | bytes 29360128 | tf_op jit(solution)/shard_map/gates/pallas_call | solution.py:180
  18.9 0.0 collective-permute-done.4
  19.0 1.7 %collective-permute-start.9 = (bf16[2,72,896]{2,1,0:T(8,128)(2,1)S(1)}, bf16[2,72,896]{2,1,0:T(8,128)(2,1)S(1)}, u32[]{:S(2)}, u32[]{:S(2)}) collective-permute-start(bf16[2,72,896]{2,1,0:T(8,128)(2,1)S(1)} %pad_maximum_fusion.refs_9_.refs_0_), channel_id=1, source_target_pairs={{0,16},{1,3},{2,18},{3,1},{16,0},{17,19},{18,2},{19,17},{4,20},{5,... | collective-permute-start | bytes 774152 | tf_op jit(solution)/shard_map/ppermute | solution.py:456
  20.7 0.0 collective-permute-start.10
  20.7 0.0 slice-done
  20.7 0.0 slice-done.4
  20.7 0.0 slice-done.1
  20.7 0.0 slice-done.2
  20.7 0.0 slice-done.3
  20.8 0.0 slice-done.5
  20.8 0.0 slice-done.6
  20.8 0.0 slice-done.7
  20.8 0.0 copy-start.4
  20.8 0.0 copy-start.1
  20.8 0.0 copy-start.3
  20.8 5.2 %experts.1 = (bf16[8,3584]{1,0:T(8,128)(2,1)S(1)}, bf16[8,3584]{1,0:T(8,128)(2,1)S(1)}, bf16[8,6016]{1,0:T(8,128)(2,1)S(1)}, bf16[8,6016]{1,0:T(8,128)(2,1)S(1)}) custom-call(bf16[8,3584]{1,0:T(8,128)(2,1)S(1)} %get-tuple-element.27.refs_0_, bf16[8,6016]{1,0:T(8,128)(2,1)S(1)} %collective-permute-done.refs_1_.refs_5_, ...), custom_call_target="tpu_custom_call" | custom-call | flops 469762048 | bytes 14680064 | tf_op jit(solution)/shard_map/experts/pallas_call | solution.py:223
  26.0 0.0 collective-permute-done.5.theirs_ref
  26.0 0.0 collective-permute-done.9.refs_1_
  26.0 0.6 %collective-permute-start.11 = (bf16[2,72,896]{2,1,0:T(8,128)(2,1)S(1)}, bf16[2,72,896]{2,1,0:T(8,128)(2,1)S(1)}, u32[]{:S(2)}, u32[]{:S(2)}) collective-permute-start(bf16[2,72,896]{2,1,0:T(8,128)(2,1)S(1)} %collective-permute-done.9.refs_1_), channel_id=1, source_target_pairs={{0,1},{1,0},{2,3},{3,2},{4,5},{5,4},{6,7},{7,6},{8,9},{9,8},{10,11... | collective-permute-start | bytes 774152 | tf_op jit(solution)/shard_map/ppermute | solution.py:416
  26.6 0.0 copy-done.4
  26.6 3.1 %collective-permute-start.8 = (bf16[8,6016]{1,0:T(8,128)(2,1)S(1)}, bf16[8,6016]{1,0:T(8,128)(2,1)S(1)}, u32[]{:S(2)}, u32[]{:S(2)}) collective-permute-start(bf16[8,6016]{1,0:T(8,128)(2,1)S(1)} %get-tuple-element.43), channel_id=1, source_target_pairs={{0,8},{4,12},{8,0},{12,4},{1,9},{5,13},{9,1},{13,5},{2,10},{6,14},... | collective-permute-start | bytes 288776 | tf_op jit(solution)/shard_map/ppermute | solution.py:416
  29.7 1.2 %collective-permute-start.7 = (bf16[8,3584]{1,0:T(8,128)(2,1)S(1)}, bf16[8,3584]{1,0:T(8,128)(2,1)S(1)}, u32[]{:S(2)}, u32[]{:S(2)}) collective-permute-start(bf16[8,3584]{1,0:T(8,128)(2,1)S(1)} %get-tuple-element.41), channel_id=1, source_target_pairs={{0,4},{4,0},{8,12},{12,8},{1,5},{5,1},{9,13},{13,9},{2,6},{6,2},{1... | collective-permute-start | bytes 172040 | tf_op jit(solution)/shard_map/ppermute | solution.py:416
  30.9 0.3 collective-permute-start.6
  31.2 0.0 collective-permute-done.10.refs_2_
  31.2 0.0 collective-permute-done.11.refs_3_
  31.2 0.0 copy-done.1
  31.3 0.0 copy-done.3
  31.3 0.9 %project.1 = (f32[576,128]{1,0:T(8,128)S(1)}, bf16[576,128]{1,0:T(8,128)(2,1)S(1)}) custom-call(bf16[128,3584]{1,0:T(8,128)(2,1)S(1)} %copy-done.3, bf16[128,1792]{1,0:T(8,128)(2,1)S(1)} %collective-permute-done.5.theirs_ref, bf16[576,896]{1,0:T(8,128)(2,1)S(1)} %bitcast.13, bf16[2,72,896]{2,1,0:T(8,128)(2,1)S(1)} %pad_maximum_fusion.refs_9_.refs_0_, ...), custom_call_target="tpu_custom_call" | custom-call | flops 1152999936 | tf_op jit(solution)/shard_map/project/pallas_call | solution.py:350
  32.2 0.6 %collective-permute-start.12 = (bf16[576,128]{1,0:T(8,128)(2,1)S(1)}, bf16[576,128]{1,0:T(8,128)(2,1)S(1)}, u32[]{:S(2)}, u32[]{:S(2)}) collective-permute-start(bf16[576,128]{1,0:T(8,128)(2,1)S(1)} %get-tuple-element.49), channel_id=1, source_target_pairs={{0,4},{4,0},{8,12},{12,8},{1,5},{5,1},{9,13},{13,9},{2,6},{6,2},{1... | collective-permute-start | bytes 442376 | tf_op jit(solution)/shard_map/ppermute | solution.py:416
  32.8 1.3 %collective-permute-done.7.refs_2_ = bf16[8,3584]{1,0:T(8,128)(2,1)S(1)} collective-permute-done((bf16[8,3584]{1,0:T(8,128)(2,1)S(1)}, bf16[8,3584]{1,0:T(8,128)(2,1)S(1)}, u32[]{:S(2)}, u32[]{:S(2)}) %collective-permute-start.7) | collective-permute-done | bytes 57376 | tf_op jit(solution)/shard_map/ppermute | solution.py:416
  34.1 1.2 %collective-permute-done.8.refs_3_ = bf16[8,6016]{1,0:T(8,128)(2,1)S(1)} collective-permute-done((bf16[8,6016]{1,0:T(8,128)(2,1)S(1)}, bf16[8,6016]{1,0:T(8,128)(2,1)S(1)}, u32[]{:S(2)}, u32[]{:S(2)}) %collective-permute-start.8) | collective-permute-done | bytes 96288 | tf_op jit(solution)/shard_map/ppermute | solution.py:416
  35.3 3.0 %collective-permute-done.6.refs_1_ = bf16[8,6016]{1,0:T(8,128)(2,1)S(1)} collective-permute-done((bf16[8,6016]{1,0:T(8,128)(2,1)S(1)}, bf16[8,6016]{1,0:T(8,128)(2,1)S(1)}, u32[]{:S(2)}, u32[]{:S(2)}) %collective-permute-start.6) | collective-permute-done | bytes 96288 | tf_op jit(solution)/shard_map/ppermute | solution.py:416
  38.4 0.0 copy-start.2
  38.4 1.2 %combine.1 = (bf16[128,3584]{1,0:T(8,128)(2,1)}, bf16[8,9216]{1,0:T(8,128)(2,1)S(1)}) custom-call(f32[32,128]{1,0:T(8,128)S(1)} %get-tuple-element.26.mixing_ref, bf16[8,3584]{1,0:T(8,128)(2,1)S(1)} %get-tuple-element.37.refs_0_, bf16[8,6016]{1,0:T(8,128)(2,1)S(1)} %collective-permute-done.6.refs_1_, bf16[8,3584]{1,0:T(8,128)(2,1)S(1)} %collective-permute-done.7.refs_2_, ...), custom_call_target="tpu_custom_call" | custom-call | flops 11530000384 | bytes 1376256 | tf_op jit(solution)/shard_map/combine/pallas_call | solution.py:288
  39.6 0.5 %collective-permute-done.12.theirs_ref = bf16[576,128]{1,0:T(8,128)(2,1)S(1)} collective-permute-done((bf16[576,128]{1,0:T(8,128)(2,1)S(1)}, bf16[576,128]{1,0:T(8,128)(2,1)S(1)}, u32[]{:S(2)}, u32[]{:S(2)}) %collective-permute-start.12) | collective-permute-done | bytes 147488 | tf_op jit(solution)/shard_map/ppermute | solution.py:416
  40.1 0.0 copy-done.2
  40.1 0.4 finish.1
  40.5 0.7 %broadcast_select_fusion = bf16[8,9216]{1,0:T(8,128)(2,1)} fusion(bf16[8,9216]{1,0:T(8,128)(2,1)S(1)} %get-tuple-element.46.unread_ref, bf16[8,9216]{1,0:T(8,128)(2,1)S(1)} %finish.1, pred[8]{0:T(512)(128)(4,1)S(1)} %broadcast_compare_fusion), kind=kLoop, calls=%fused_computation.1 | loop fusion | flops 73728 | bytes 442376 | tf_op jit(solution)/shard_map/jit(_where)/select_n | solution.py:469
  (4 shorter events, 0.0 us)
Async XLA Ops:
  1.6 10.6 %collective-permute-start.3 = (bf16[72,896]{1,0:T(8,128)(2,1)S(1)}, bf16[72,896]{1,0:T(8,128)(2,1)S(1)}, u32[]{:S(2)}, u32[]{:S(2)}) collective-permute-start(bf16[72,896]{1,0:T(8,128)(2,1)S(1)} %dynamic-slice_bitcast_fusion), channel_id=1, source_target_pairs={{0,8},{4,12},{8,0},{12,4},{1,9},{5,13},{9,1},{13,5},{2,10},{6,14},... | collective-permute-start | bytes 387080 | tf_op jit(solution)/shard_map/ppermute | solution.py:416
  5.7 15.0 %slice-start = ((s8[14680064]{0:T(1024)(128)(4,1)}), s8[4194304]{0:T(1024)(128)(4,1)S(1)}, s32[]{:S(2)}) async-start(s8[14680064]{0:T(1024)(128)(4,1)} %bitcast.8), calls=%async_computation | async-start | bytes 8388608
  5.7 15.0 %slice-start.4 = ((s8[14680064]{0:T(1024)(128)(4,1)}), s8[4194304]{0:T(1024)(128)(4,1)S(1)}, s32[]{:S(2)}) async-start(s8[14680064]{0:T(1024)(128)(4,1)} %bitcast.10), calls=%async_computation.4 | async-start | bytes 8388608
  5.7 10.6 %copy-start = (bf16[3584,2048]{1,0:T(8,128)(2,1)S(1)}, bf16[3584,2048]{1,0:T(8,128)(2,1)}, u32[]{:S(2)}) copy-start(bf16[3584,2048]{1,0:T(8,128)(2,1)} %refs_4_.3) | copy-start | bytes 44040196
  5.7 15.0 %slice-start.1 = ((s8[14680064]{0:T(1024)(128)(4,1)}), s8[4194304]{0:T(1024)(128)(4,1)S(1)}, s32[]{:S(2)}) async-start(s8[14680064]{0:T(1024)(128)(4,1)} %bitcast.8), calls=%async_computation.1 | async-start | bytes 8388608
  5.7 15.0 %slice-start.2 = ((s8[14680064]{0:T(1024)(128)(4,1)}), s8[4194304]{0:T(1024)(128)(4,1)S(1)}, s32[]{:S(2)}) async-start(s8[14680064]{0:T(1024)(128)(4,1)} %bitcast.8), calls=%async_computation.2 | async-start | bytes 8388608
  5.7 15.0 %slice-start.3 = ((s8[14680064]{0:T(1024)(128)(4,1)}), s8[2097152]{0:T(1024)(128)(4,1)S(1)}, s32[]{:S(2)}) async-start(s8[14680064]{0:T(1024)(128)(4,1)} %bitcast.8), calls=%async_computation.3 | async-start | bytes 4194304
  5.7 15.0 %slice-start.5 = ((s8[14680064]{0:T(1024)(128)(4,1)}), s8[4194304]{0:T(1024)(128)(4,1)S(1)}, s32[]{:S(2)}) async-start(s8[14680064]{0:T(1024)(128)(4,1)} %bitcast.10), calls=%async_computation.5 | async-start | bytes 8388608
  5.7 15.0 %slice-start.6 = ((s8[14680064]{0:T(1024)(128)(4,1)}), s8[4194304]{0:T(1024)(128)(4,1)S(1)}, s32[]{:S(2)}) async-start(s8[14680064]{0:T(1024)(128)(4,1)} %bitcast.10), calls=%async_computation.6 | async-start | bytes 8388608
  5.7 15.0 %slice-start.7 = ((s8[14680064]{0:T(1024)(128)(4,1)}), s8[2097152]{0:T(1024)(128)(4,1)S(1)}, s32[]{:S(2)}) async-start(s8[14680064]{0:T(1024)(128)(4,1)} %bitcast.10), calls=%async_computation.7 | async-start | bytes 4194304
  7.8 8.5 %collective-permute-start = (bf16[8,6016]{1,0:T(8,128)(2,1)S(1)}, bf16[8,6016]{1,0:T(8,128)(2,1)S(1)}, u32[]{:S(2)}, u32[]{:S(2)}) collective-permute-start(bf16[8,6016]{1,0:T(8,128)(2,1)S(1)} %get-tuple-element.28), channel_id=1, source_target_pairs={{0,4},{4,0},{8,12},{12,8},{1,5},{5,1},{9,13},{13,9},{2,6},{6,2},{1... | collective-permute-start | bytes 288776 | tf_op jit(solution)/shard_map/ppermute | solution.py:416
  9.4 6.9 %collective-permute-start.1 = (bf16[8,3584]{1,0:T(8,128)(2,1)S(1)}, bf16[8,3584]{1,0:T(8,128)(2,1)S(1)}, u32[]{:S(2)}, u32[]{:S(2)}) collective-permute-start(bf16[8,3584]{1,0:T(8,128)(2,1)S(1)} %get-tuple-element.29), channel_id=1, source_target_pairs={{0,8},{4,12},{8,0},{12,4},{1,9},{5,13},{9,1},{13,5},{2,10},{6,14},... | collective-permute-start | bytes 172040 | tf_op jit(solution)/shard_map/ppermute | solution.py:416
  9.7 6.5 %collective-permute-start.2 = (bf16[8,3584]{1,0:T(8,128)(2,1)S(1)}, bf16[8,3584]{1,0:T(8,128)(2,1)S(1)}, u32[]{:S(2)}, u32[]{:S(2)}) collective-permute-start(bf16[8,3584]{1,0:T(8,128)(2,1)S(1)} %get-tuple-element.30), channel_id=1, source_target_pairs={{0,12},{4,8},{8,4},{12,0},{1,13},{5,9},{9,5},{13,1},{2,14},{6,10},... | collective-permute-start | bytes 172040 | tf_op jit(solution)/shard_map/ppermute | solution.py:416
  12.2 6.7 %collective-permute-start.4 = (bf16[72,896]{1,0:T(8,128)(2,1)S(1)}, bf16[72,896]{1,0:T(8,128)(2,1)S(1)}, u32[]{:S(2)}, u32[]{:S(2)}) collective-permute-start(bf16[72,896]{1,0:T(8,128)(2,1)S(1)} %collective-permute-done.3.refs_5_), channel_id=1, source_target_pairs={{0,2},{1,17},{2,0},{3,19},{16,18},{17,1},{18,16},{19,3},{4,6},{5,2... | collective-permute-start | bytes 387080 | tf_op jit(solution)/shard_map/ppermute | solution.py:452
  13.7 12.3 %collective-permute-start.5 = (bf16[128,1792]{1,0:T(8,128)(2,1)S(1)}, bf16[128,1792]{1,0:T(8,128)(2,1)S(1)}, u32[]{:S(2)}, u32[]{:S(2)}) collective-permute-start(bf16[128,1792]{1,0:T(8,128)(2,1)S(1)} %get-tuple-element.36), channel_id=1, source_target_pairs={{0,4},{4,0},{8,12},{12,8},{1,5},{5,1},{9,13},{13,9},{2,6},{6,2},{1... | collective-permute-start | bytes 1376264 | tf_op jit(solution)/shard_map/ppermute | solution.py:416
  19.0 7.0 %collective-permute-start.9 = (bf16[2,72,896]{2,1,0:T(8,128)(2,1)S(1)}, bf16[2,72,896]{2,1,0:T(8,128)(2,1)S(1)}, u32[]{:S(2)}, u32[]{:S(2)}) collective-permute-start(bf16[2,72,896]{2,1,0:T(8,128)(2,1)S(1)} %pad_maximum_fusion.refs_9_.refs_0_), channel_id=1, source_target_pairs={{0,16},{1,3},{2,18},{3,1},{16,0},{17,19},{18,2},{19,17},{4,20},{5,... | collective-permute-start | bytes 774152 | tf_op jit(solution)/shard_map/ppermute | solution.py:456
  20.7 10.5 %collective-permute-start.10 = (bf16[2,72,896]{2,1,0:T(8,128)(2,1)S(1)}, bf16[2,72,896]{2,1,0:T(8,128)(2,1)S(1)}, u32[]{:S(2)}, u32[]{:S(2)}) collective-permute-start(bf16[2,72,896]{2,1,0:T(8,128)(2,1)S(1)} %pad_maximum_fusion.refs_9_.refs_0_), channel_id=1, source_target_pairs={{0,1},{1,0},{2,3},{3,2},{4,5},{5,4},{6,7},{7,6},{8,9},{9,8},{10,11... | collective-permute-start | bytes 774152 | tf_op jit(solution)/shard_map/ppermute | solution.py:416
  20.8 5.8 %copy-start.4 = (s32[8]{0:T(128)S(1)}, s32[8]{0:T(128)}, u32[]{:S(2)}) copy-start(s32[8]{0:T(128)} %param.20) | copy-start | bytes 100
  20.8 10.4 %copy-start.1 = (bf16[896,576]{0,1:T(8,128)(2,1)S(1)}, bf16[896,576]{0,1:T(8,128)(2,1)}, u32[]{:S(2)}) copy-start(bf16[896,576]{0,1:T(8,128)(2,1)} %param.15) | copy-start | bytes 3096580
  20.8 10.4 %copy-start.3 = (bf16[128,3584]{1,0:T(8,128)(2,1)S(1)}, bf16[128,3584]{1,0:T(8,128)(2,1)}, u32[]{:S(2)}) copy-start(bf16[128,3584]{1,0:T(8,128)(2,1)} %tokens_ref.1) | copy-start | bytes 2752516
  26.0 5.2 %collective-permute-start.11 = (bf16[2,72,896]{2,1,0:T(8,128)(2,1)S(1)}, bf16[2,72,896]{2,1,0:T(8,128)(2,1)S(1)}, u32[]{:S(2)}, u32[]{:S(2)}) collective-permute-start(bf16[2,72,896]{2,1,0:T(8,128)(2,1)S(1)} %collective-permute-done.9.refs_1_), channel_id=1, source_target_pairs={{0,1},{1,0},{2,3},{3,2},{4,5},{5,4},{6,7},{7,6},{8,9},{9,8},{10,11... | collective-permute-start | bytes 774152 | tf_op jit(solution)/shard_map/ppermute | solution.py:416
  26.6 8.7 %collective-permute-start.8 = (bf16[8,6016]{1,0:T(8,128)(2,1)S(1)}, bf16[8,6016]{1,0:T(8,128)(2,1)S(1)}, u32[]{:S(2)}, u32[]{:S(2)}) collective-permute-start(bf16[8,6016]{1,0:T(8,128)(2,1)S(1)} %get-tuple-element.43), channel_id=1, source_target_pairs={{0,8},{4,12},{8,0},{12,4},{1,9},{5,13},{9,1},{13,5},{2,10},{6,14},... | collective-permute-start | bytes 288776 | tf_op jit(solution)/shard_map/ppermute | solution.py:416
  29.7 4.4 %collective-permute-start.7 = (bf16[8,3584]{1,0:T(8,128)(2,1)S(1)}, bf16[8,3584]{1,0:T(8,128)(2,1)S(1)}, u32[]{:S(2)}, u32[]{:S(2)}) collective-permute-start(bf16[8,3584]{1,0:T(8,128)(2,1)S(1)} %get-tuple-element.41), channel_id=1, source_target_pairs={{0,4},{4,0},{8,12},{12,8},{1,5},{5,1},{9,13},{13,9},{2,6},{6,2},{1... | collective-permute-start | bytes 172040 | tf_op jit(solution)/shard_map/ppermute | solution.py:416
  30.9 7.4 %collective-permute-start.6 = (bf16[8,6016]{1,0:T(8,128)(2,1)S(1)}, bf16[8,6016]{1,0:T(8,128)(2,1)S(1)}, u32[]{:S(2)}, u32[]{:S(2)}) collective-permute-start(bf16[8,6016]{1,0:T(8,128)(2,1)S(1)} %get-tuple-element.39), channel_id=1, source_target_pairs={{0,12},{4,8},{8,4},{12,0},{1,13},{5,9},{9,5},{13,1},{2,14},{6,10},... | collective-permute-start | bytes 288776 | tf_op jit(solution)/shard_map/ppermute | solution.py:416
  32.2 7.9 %collective-permute-start.12 = (bf16[576,128]{1,0:T(8,128)(2,1)S(1)}, bf16[576,128]{1,0:T(8,128)(2,1)S(1)}, u32[]{:S(2)}, u32[]{:S(2)}) collective-permute-start(bf16[576,128]{1,0:T(8,128)(2,1)S(1)} %get-tuple-element.49), channel_id=1, source_target_pairs={{0,4},{4,0},{8,12},{12,8},{1,5},{5,1},{9,13},{13,9},{2,6},{6,2},{1... | collective-permute-start | bytes 442376 | tf_op jit(solution)/shard_map/ppermute | solution.py:416
  38.4 1.7 %copy-start.2 = (f32[512]{0:T(512)S(1)}, f32[512]{0:T(512)}, u32[]{:S(2)}) copy-start(f32[512]{0:T(512)} %param.16) | copy-start | bytes 6148

commit v5 on v4

--- a/solution.py
+++ b/solution.py
@@ -456,7 +456,7 @@
     far = lax.ppermute(near, plane, plane_pairs(group_count, dp_count, False))
     near_other = swap(near, "dp", 1)
     results = experts(received, gate, w_up, w_down, pages, (near,))
-    results = [tied(result, theirs) for result in results]
+    results = [tied(result, theirs, far) for result in results]
     returned = exchanged(results)
     far = tied(far, results[0])
     far_other = swap(far, "dp", 1)

time: 41.4 us -> 41.4 us (level)
  no operation moved by 1% of the time
where the time goes in v5:
time: 41.4 us; the launch traced here: 41.2 us
  starting transfers between devices  19 us (46%)
  Pallas kernels  12.4 us (30%)
  waiting for transfers between devices  7.19 us (17%)
  local copies, waits for them, and re-layouts  0.98 us (2%)
  between operations  0.88 us (2%)
  other arithmetic  0.79 us (2%)
    ppermute x11, starting transfers between devices, swap(): return lax.ppermute(value, axis, xor_pairs(lax.axis_size(axis), bit))  15.8 us
    ppermute x11, waiting for transfers between devices, swap(): return lax.ppermute(value, axis, xor_pairs(lax.axis_size(axis), bit))  7.17 us
    pallas_call x1, Pallas kernels, experts(): pl.pallas_call(expert_kernel, out_shape=tuple((jax.ShapeDtypeStruct((CAP,...  5.18 us
    pallas_call x1, Pallas kernels, gates(): pl.pallas_call(gate_kernel, out_shape=jax.ShapeDtypeStruct((row_count, un...  2.63 us
    pallas_call x1, Pallas kernels, open_work(): pl.pallas_call(functools.partial(open_kernel, page_count * lax.axis_size(...  2.02 us
    ppermute x1, starting transfers between devices, block_shards(): far = lax.ppermute(near, plane, plane_pairs(group_count, dp_count, False))  1.73 us
    ppermute x1, starting transfers between devices, block_shards(): lax.ppermute(far_piece, plane, plane_pairs(group_count, dp_count, True))  1.5 us
    pallas_call x1, Pallas kernels, combine(): pl.pallas_call(combine_kernel, out_shape=(jax.ShapeDtypeStruct((token_cou...  1.21 us
  transfers between devices with their start and end apart: 13, of which 5 were waited for; matrix products, arithmetic and copies ran while one was open for 0% of the time, Pallas kernels for 29%

profile of v5, /device:TPU:0, one launch (start us, length us, event | category | flops | bytes accessed | tf_op | source)
XLA Modules:
  0.0 41.2 jit_solution(12769808046899774475)
XLA Ops:
  0.7 0.9 %dynamic-slice_bitcast_fusion = bf16[72,896]{1,0:T(8,128)(2,1)S(1)} fusion(bf16[896,576]{0,1:T(8,128)(2,1)} %param.15, s32[]{:T(128)S(6)} %select_n.20), kind=kLoop, calls=%fused_computation.2 | loop fusion | bytes 258052 | tf_op jit(solution)/shard_map/dynamic_slice | solution.py:446
  1.6 4.1 %collective-permute-start.3 = (bf16[72,896]{1,0:T(8,128)(2,1)S(1)}, bf16[72,896]{1,0:T(8,128)(2,1)S(1)}, u32[]{:S(2)}, u32[]{:S(2)}) collective-permute-start(bf16[72,896]{1,0:T(8,128)(2,1)S(1)} %dynamic-slice_bitcast_fusion), channel_id=1, source_target_pairs={{0,8},{4,12},{8,0},{12,4},{1,9},{5,13},{9,1},{13,5},{2,10},{6,14},... | collective-permute-start | bytes 387080 | tf_op jit(solution)/shard_map/ppermute | solution.py:416
  5.7 0.0 slice-start
  5.7 0.0 slice-start.4
  5.7 0.0 copy-start
  5.7 0.0 slice-start.1
  5.7 0.0 slice-start.2
  5.7 0.0 slice-start.3
  5.7 0.0 slice-start.5
  5.7 0.0 slice-start.6
  5.7 0.0 slice-start.7
  5.7 2.0 %open.1 = (bf16[8,3584]{1,0:T(8,128)(2,1)S(1)}, bf16[8,6016]{1,0:T(8,128)(2,1)S(1)}, bf16[8,3584]{1,0:T(8,128)(2,1)S(1)}, bf16[8,3584]{1,0:T(8,128)(2,1)S(1)}, f...) custom-call(s32[8,128]{1,0:T(8,128)} %bitcast.16, ...), custom_call_target="tpu_custom_call" | custom-call | flops 20000000000 | bytes 2097152 | tf_op jit(solution)/shard_map/open/pallas_call | solution.py:140
  7.8 1.6 %collective-permute-start = (bf16[8,6016]{1,0:T(8,128)(2,1)S(1)}, bf16[8,6016]{1,0:T(8,128)(2,1)S(1)}, u32[]{:S(2)}, u32[]{:S(2)}) collective-permute-start(bf16[8,6016]{1,0:T(8,128)(2,1)S(1)} %get-tuple-element.28), channel_id=1, source_target_pairs={{0,4},{4,0},{8,12},{12,8},{1,5},{5,1},{9,13},{13,9},{2,6},{6,2},{1... | collective-permute-start | bytes 288776 | tf_op jit(solution)/shard_map/ppermute | solution.py:416
  9.4 0.3 collective-permute-start.1
  9.7 2.5 %collective-permute-start.2 = (bf16[8,3584]{1,0:T(8,128)(2,1)S(1)}, bf16[8,3584]{1,0:T(8,128)(2,1)S(1)}, u32[]{:S(2)}, u32[]{:S(2)}) collective-permute-start(bf16[8,3584]{1,0:T(8,128)(2,1)S(1)} %get-tuple-element.30), channel_id=1, source_target_pairs={{0,12},{4,8},{8,4},{12,0},{1,13},{5,9},{9,5},{13,1},{2,14},{6,10},... | collective-permute-start | bytes 172040 | tf_op jit(solution)/shard_map/ppermute | solution.py:416
  12.2 0.0 collective-permute-done.3.refs_5_
  12.2 1.5 %collective-permute-start.4 = (bf16[72,896]{1,0:T(8,128)(2,1)S(1)}, bf16[72,896]{1,0:T(8,128)(2,1)S(1)}, u32[]{:S(2)}, u32[]{:S(2)}) collective-permute-start(bf16[72,896]{1,0:T(8,128)(2,1)S(1)} %collective-permute-done.3.refs_5_), channel_id=1, source_target_pairs={{0,2},{1,17},{2,0},{3,19},{16,18},{17,1},{18,16},{19,3},{4,6},{5,2... | collective-permute-start | bytes 387080 | tf_op jit(solution)/shard_map/ppermute | solution.py:452
  13.7 1.5 %collective-permute-start.5 = (bf16[128,1792]{1,0:T(8,128)(2,1)S(1)}, bf16[128,1792]{1,0:T(8,128)(2,1)S(1)}, u32[]{:S(2)}, u32[]{:S(2)}) collective-permute-start(bf16[128,1792]{1,0:T(8,128)(2,1)S(1)} %get-tuple-element.36), channel_id=1, source_target_pairs={{0,4},{4,0},{8,12},{12,8},{1,5},{5,1},{9,13},{13,9},{2,6},{6,2},{1... | collective-permute-start | bytes 1376264 | tf_op jit(solution)/shard_map/ppermute | solution.py:416
  15.2 1.1 %collective-permute-done.1.refs_2_ = bf16[8,3584]{1,0:T(8,128)(2,1)S(1)} collective-permute-done((bf16[8,3584]{1,0:T(8,128)(2,1)S(1)}, bf16[8,3584]{1,0:T(8,128)(2,1)S(1)}, u32[]{:S(2)}, u32[]{:S(2)}) %collective-permute-start.1) | collective-permute-done | bytes 57376 | tf_op jit(solution)/shard_map/ppermute | solution.py:416
  16.3 0.0 collective-permute-done.2.refs_3_
  16.3 0.0 collective-permute-done.refs_1_.refs_5_
  16.3 0.0 copy-done
  16.3 2.6 %gates.1.refs_4_ = f32[32,2048]{1,0:T(8,128)S(1)} custom-call(bf16[8,3584]{1,0:T(8,128)(2,1)S(1)} %get-tuple-element.27.refs_0_, bf16[8,6016]{1,0:T(8,128)(2,1)S(1)} %collective-permute-done.refs_1_.refs_5_, bf16[8,3584]{1,0:T(8,128)(2,1)S(1)} %collective-permute-done.1.refs_2_, bf16[8,3584]{1,0:T(8,128)(2,1)S(1)} %collective-permute-done.2.refs_3_, ...), custom_call_target="tpu_custom_call" | custom-call | flops 939524096 | bytes 29360128 | tf_op jit(solution)/shard_map/gates/pallas_call | solution.py:180
  18.9 0.0 collective-permute-done.4
  19.0 1.7 %collective-permute-start.6 = (bf16[2,72,896]{2,1,0:T(8,128)(2,1)S(1)}, bf16[2,72,896]{2,1,0:T(8,128)(2,1)S(1)}, u32[]{:S(2)}, u32[]{:S(2)}) collective-permute-start(bf16[2,72,896]{2,1,0:T(8,128)(2,1)S(1)} %pad_maximum_fusion.refs_9_.refs_0_), channel_id=1, source_target_pairs={{0,16},{1,3},{2,18},{3,1},{16,0},{17,19},{18,2},{19,17},{4,20},{5,... | collective-permute-start | bytes 774152 | tf_op jit(solution)/shard_map/ppermute | solution.py:456
  20.7 0.0 collective-permute-start.10
  20.7 0.0 slice-done
  20.7 0.0 slice-done.4
  20.7 0.0 slice-done.1
  20.7 0.0 slice-done.2
  20.7 0.0 slice-done.3
  20.8 0.0 slice-done.5
  20.8 0.0 slice-done.6
  20.8 0.0 slice-done.7
  20.8 0.0 copy-start.4
  20.8 0.0 copy-start.1
  20.8 0.0 copy-start.3
  20.8 5.2 %experts.1 = (bf16[8,3584]{1,0:T(8,128)(2,1)S(1)}, bf16[8,3584]{1,0:T(8,128)(2,1)S(1)}, bf16[8,6016]{1,0:T(8,128)(2,1)S(1)}, bf16[8,6016]{1,0:T(8,128)(2,1)S(1)}) custom-call(bf16[8,3584]{1,0:T(8,128)(2,1)S(1)} %get-tuple-element.27.refs_0_, bf16[8,6016]{1,0:T(8,128)(2,1)S(1)} %collective-permute-done.refs_1_.refs_5_, ...), custom_call_target="tpu_custom_call" | custom-call | flops 469762048 | bytes 14680064 | tf_op jit(solution)/shard_map/experts/pallas_call | solution.py:223
  26.0 0.0 collective-permute-done.6.refs_1_
  26.0 0.0 collective-permute-done.5.theirs_ref
  26.0 0.6 %collective-permute-start.11 = (bf16[2,72,896]{2,1,0:T(8,128)(2,1)S(1)}, bf16[2,72,896]{2,1,0:T(8,128)(2,1)S(1)}, u32[]{:S(2)}, u32[]{:S(2)}) collective-permute-start(bf16[2,72,896]{2,1,0:T(8,128)(2,1)S(1)} %collective-permute-done.6.refs_1_), channel_id=1, source_target_pairs={{0,1},{1,0},{2,3},{3,2},{4,5},{5,4},{6,7},{7,6},{8,9},{9,8},{10,11... | collective-permute-start | bytes 774152 | tf_op jit(solution)/shard_map/ppermute | solution.py:416
  26.6 0.0 copy-done.4
  26.6 3.1 %collective-permute-start.9 = (bf16[8,6016]{1,0:T(8,128)(2,1)S(1)}, bf16[8,6016]{1,0:T(8,128)(2,1)S(1)}, u32[]{:S(2)}, u32[]{:S(2)}) collective-permute-start(bf16[8,6016]{1,0:T(8,128)(2,1)S(1)} %get-tuple-element.43), channel_id=1, source_target_pairs={{0,8},{4,12},{8,0},{12,4},{1,9},{5,13},{9,1},{13,5},{2,10},{6,14},... | collective-permute-start | bytes 288776 | tf_op jit(solution)/shard_map/ppermute | solution.py:416
  29.7 1.2 %collective-permute-start.8 = (bf16[8,3584]{1,0:T(8,128)(2,1)S(1)}, bf16[8,3584]{1,0:T(8,128)(2,1)S(1)}, u32[]{:S(2)}, u32[]{:S(2)}) collective-permute-start(bf16[8,3584]{1,0:T(8,128)(2,1)S(1)} %get-tuple-element.41), channel_id=1, source_target_pairs={{0,4},{4,0},{8,12},{12,8},{1,5},{5,1},{9,13},{13,9},{2,6},{6,2},{1... | collective-permute-start | bytes 172040 | tf_op jit(solution)/shard_map/ppermute | solution.py:416
  30.9 0.3 collective-permute-start.7
  31.2 0.0 collective-permute-done.10.refs_2_
  31.2 0.0 collective-permute-done.11.refs_3_
  31.2 0.0 copy-done.1
  31.3 0.0 copy-done.3
  31.3 0.9 %project.1 = (f32[576,128]{1,0:T(8,128)S(1)}, bf16[576,128]{1,0:T(8,128)(2,1)S(1)}) custom-call(bf16[128,3584]{1,0:T(8,128)(2,1)S(1)} %copy-done.3, bf16[128,1792]{1,0:T(8,128)(2,1)S(1)} %collective-permute-done.5.theirs_ref, bf16[576,896]{1,0:T(8,128)(2,1)S(1)} %bitcast.13, bf16[2,72,896]{2,1,0:T(8,128)(2,1)S(1)} %pad_maximum_fusion.refs_9_.refs_0_, ...), custom_call_target="tpu_custom_call" | custom-call | flops 1152999936 | tf_op jit(solution)/shard_map/project/pallas_call | solution.py:350
  32.2 0.6 %collective-permute-start.12 = (bf16[576,128]{1,0:T(8,128)(2,1)S(1)}, bf16[576,128]{1,0:T(8,128)(2,1)S(1)}, u32[]{:S(2)}, u32[]{:S(2)}) collective-permute-start(bf16[576,128]{1,0:T(8,128)(2,1)S(1)} %get-tuple-element.49), channel_id=1, source_target_pairs={{0,4},{4,0},{8,12},{12,8},{1,5},{5,1},{9,13},{13,9},{2,6},{6,2},{1... | collective-permute-start | bytes 442376 | tf_op jit(solution)/shard_map/ppermute | solution.py:416
  32.8 1.3 %collective-permute-done.8.refs_2_ = bf16[8,3584]{1,0:T(8,128)(2,1)S(1)} collective-permute-done((bf16[8,3584]{1,0:T(8,128)(2,1)S(1)}, bf16[8,3584]{1,0:T(8,128)(2,1)S(1)}, u32[]{:S(2)}, u32[]{:S(2)}) %collective-permute-start.8) | collective-permute-done | bytes 57376 | tf_op jit(solution)/shard_map/ppermute | solution.py:416
  34.1 2.3 %collective-permute-done.9.refs_3_ = bf16[8,6016]{1,0:T(8,128)(2,1)S(1)} collective-permute-done((bf16[8,6016]{1,0:T(8,128)(2,1)S(1)}, bf16[8,6016]{1,0:T(8,128)(2,1)S(1)}, u32[]{:S(2)}, u32[]{:S(2)}) %collective-permute-start.9) | collective-permute-done | bytes 96288 | tf_op jit(solution)/shard_map/ppermute | solution.py:416
  36.4 1.9 %collective-permute-done.7.refs_1_ = bf16[8,6016]{1,0:T(8,128)(2,1)S(1)} collective-permute-done((bf16[8,6016]{1,0:T(8,128)(2,1)S(1)}, bf16[8,6016]{1,0:T(8,128)(2,1)S(1)}, u32[]{:S(2)}, u32[]{:S(2)}) %collective-permute-start.7) | collective-permute-done | bytes 96288 | tf_op jit(solution)/shard_map/ppermute | solution.py:416
  38.4 0.0 copy-start.2
  38.4 1.2 %combine.1 = (bf16[128,3584]{1,0:T(8,128)(2,1)}, bf16[8,9216]{1,0:T(8,128)(2,1)S(1)}) custom-call(f32[32,128]{1,0:T(8,128)S(1)} %get-tuple-element.26.mixing_ref, bf16[8,3584]{1,0:T(8,128)(2,1)S(1)} %get-tuple-element.37.refs_0_, bf16[8,6016]{1,0:T(8,128)(2,1)S(1)} %collective-permute-done.7.refs_1_, bf16[8,3584]{1,0:T(8,128)(2,1)S(1)} %collective-permute-done.8.refs_2_, ...), custom_call_target="tpu_custom_call" | custom-call | flops 11530000384 | bytes 1376256 | tf_op jit(solution)/shard_map/combine/pallas_call | solution.py:288
  39.6 0.5 %collective-permute-done.12.theirs_ref = bf16[576,128]{1,0:T(8,128)(2,1)S(1)} collective-permute-done((bf16[576,128]{1,0:T(8,128)(2,1)S(1)}, bf16[576,128]{1,0:T(8,128)(2,1)S(1)}, u32[]{:S(2)}, u32[]{:S(2)}) %collective-permute-start.12) | collective-permute-done | bytes 147488 | tf_op jit(solution)/shard_map/ppermute | solution.py:416
  40.1 0.0 copy-done.2
  40.1 0.4 finish.1
  40.5 0.7 %broadcast_select_fusion = bf16[8,9216]{1,0:T(8,128)(2,1)} fusion(bf16[8,9216]{1,0:T(8,128)(2,1)S(1)} %get-tuple-element.46.unread_ref, bf16[8,9216]{1,0:T(8,128)(2,1)S(1)} %finish.1, pred[8]{0:T(512)(128)(4,1)S(1)} %broadcast_compare_fusion), kind=kLoop, calls=%fused_computation.1 | loop fusion | flops 73728 | bytes 442376 | tf_op jit(solution)/shard_map/jit(_where)/select_n | solution.py:469
  (4 shorter events, 0.0 us)
Async XLA Ops:
  1.6 10.6 %collective-permute-start.3 = (bf16[72,896]{1,0:T(8,128)(2,1)S(1)}, bf16[72,896]{1,0:T(8,128)(2,1)S(1)}, u32[]{:S(2)}, u32[]{:S(2)}) collective-permute-start(bf16[72,896]{1,0:T(8,128)(2,1)S(1)} %dynamic-slice_bitcast_fusion), channel_id=1, source_target_pairs={{0,8},{4,12},{8,0},{12,4},{1,9},{5,13},{9,1},{13,5},{2,10},{6,14},... | collective-permute-start | bytes 387080 | tf_op jit(solution)/shard_map/ppermute | solution.py:416
  5.7 15.0 %slice-start = ((s8[14680064]{0:T(1024)(128)(4,1)}), s8[4194304]{0:T(1024)(128)(4,1)S(1)}, s32[]{:S(2)}) async-start(s8[14680064]{0:T(1024)(128)(4,1)} %bitcast.8), calls=%async_computation | async-start | bytes 8388608
  5.7 15.0 %slice-start.4 = ((s8[14680064]{0:T(1024)(128)(4,1)}), s8[4194304]{0:T(1024)(128)(4,1)S(1)}, s32[]{:S(2)}) async-start(s8[14680064]{0:T(1024)(128)(4,1)} %bitcast.10), calls=%async_computation.4 | async-start | bytes 8388608
  5.7 10.6 %copy-start = (bf16[3584,2048]{1,0:T(8,128)(2,1)S(1)}, bf16[3584,2048]{1,0:T(8,128)(2,1)}, u32[]{:S(2)}) copy-start(bf16[3584,2048]{1,0:T(8,128)(2,1)} %refs_4_.3) | copy-start | bytes 44040196
  5.7 15.0 %slice-start.1 = ((s8[14680064]{0:T(1024)(128)(4,1)}), s8[4194304]{0:T(1024)(128)(4,1)S(1)}, s32[]{:S(2)}) async-start(s8[14680064]{0:T(1024)(128)(4,1)} %bitcast.8), calls=%async_computation.1 | async-start | bytes 8388608
  5.7 15.0 %slice-start.2 = ((s8[14680064]{0:T(1024)(128)(4,1)}), s8[4194304]{0:T(1024)(128)(4,1)S(1)}, s32[]{:S(2)}) async-start(s8[14680064]{0:T(1024)(128)(4,1)} %bitcast.8), calls=%async_computation.2 | async-start | bytes 8388608
  5.7 15.0 %slice-start.3 = ((s8[14680064]{0:T(1024)(128)(4,1)}), s8[2097152]{0:T(1024)(128)(4,1)S(1)}, s32[]{:S(2)}) async-start(s8[14680064]{0:T(1024)(128)(4,1)} %bitcast.8), calls=%async_computation.3 | async-start | bytes 4194304
  5.7 15.0 %slice-start.5 = ((s8[14680064]{0:T(1024)(128)(4,1)}), s8[4194304]{0:T(1024)(128)(4,1)S(1)}, s32[]{:S(2)}) async-start(s8[14680064]{0:T(1024)(128)(4,1)} %bitcast.10), calls=%async_computation.5 | async-start | bytes 8388608
  5.7 15.0 %slice-start.6 = ((s8[14680064]{0:T(1024)(128)(4,1)}), s8[4194304]{0:T(1024)(128)(4,1)S(1)}, s32[]{:S(2)}) async-start(s8[14680064]{0:T(1024)(128)(4,1)} %bitcast.10), calls=%async_computation.6 | async-start | bytes 8388608
  5.7 15.0 %slice-start.7 = ((s8[14680064]{0:T(1024)(128)(4,1)}), s8[2097152]{0:T(1024)(128)(4,1)S(1)}, s32[]{:S(2)}) async-start(s8[14680064]{0:T(1024)(128)(4,1)} %bitcast.10), calls=%async_computation.7 | async-start | bytes 4194304
  7.8 8.5 %collective-permute-start = (bf16[8,6016]{1,0:T(8,128)(2,1)S(1)}, bf16[8,6016]{1,0:T(8,128)(2,1)S(1)}, u32[]{:S(2)}, u32[]{:S(2)}) collective-permute-start(bf16[8,6016]{1,0:T(8,128)(2,1)S(1)} %get-tuple-element.28), channel_id=1, source_target_pairs={{0,4},{4,0},{8,12},{12,8},{1,5},{5,1},{9,13},{13,9},{2,6},{6,2},{1... | collective-permute-start | bytes 288776 | tf_op jit(solution)/shard_map/ppermute | solution.py:416
  9.4 6.9 %collective-permute-start.1 = (bf16[8,3584]{1,0:T(8,128)(2,1)S(1)}, bf16[8,3584]{1,0:T(8,128)(2,1)S(1)}, u32[]{:S(2)}, u32[]{:S(2)}) collective-permute-start(bf16[8,3584]{1,0:T(8,128)(2,1)S(1)} %get-tuple-element.29), channel_id=1, source_target_pairs={{0,8},{4,12},{8,0},{12,4},{1,9},{5,13},{9,1},{13,5},{2,10},{6,14},... | collective-permute-start | bytes 172040 | tf_op jit(solution)/shard_map/ppermute | solution.py:416
  9.7 6.5 %collective-permute-start.2 = (bf16[8,3584]{1,0:T(8,128)(2,1)S(1)}, bf16[8,3584]{1,0:T(8,128)(2,1)S(1)}, u32[]{:S(2)}, u32[]{:S(2)}) collective-permute-start(bf16[8,3584]{1,0:T(8,128)(2,1)S(1)} %get-tuple-element.30), channel_id=1, source_target_pairs={{0,12},{4,8},{8,4},{12,0},{1,13},{5,9},{9,5},{13,1},{2,14},{6,10},... | collective-permute-start | bytes 172040 | tf_op jit(solution)/shard_map/ppermute | solution.py:416
  12.2 6.7 %collective-permute-start.4 = (bf16[72,896]{1,0:T(8,128)(2,1)S(1)}, bf16[72,896]{1,0:T(8,128)(2,1)S(1)}, u32[]{:S(2)}, u32[]{:S(2)}) collective-permute-start(bf16[72,896]{1,0:T(8,128)(2,1)S(1)} %collective-permute-done.3.refs_5_), channel_id=1, source_target_pairs={{0,2},{1,17},{2,0},{3,19},{16,18},{17,1},{18,16},{19,3},{4,6},{5,2... | collective-permute-start | bytes 387080 | tf_op jit(solution)/shard_map/ppermute | solution.py:452
  13.7 12.3 %collective-permute-start.5 = (bf16[128,1792]{1,0:T(8,128)(2,1)S(1)}, bf16[128,1792]{1,0:T(8,128)(2,1)S(1)}, u32[]{:S(2)}, u32[]{:S(2)}) collective-permute-start(bf16[128,1792]{1,0:T(8,128)(2,1)S(1)} %get-tuple-element.36), channel_id=1, source_target_pairs={{0,4},{4,0},{8,12},{12,8},{1,5},{5,1},{9,13},{13,9},{2,6},{6,2},{1... | collective-permute-start | bytes 1376264 | tf_op jit(solution)/shard_map/ppermute | solution.py:416
  19.0 7.0 %collective-permute-start.6 = (bf16[2,72,896]{2,1,0:T(8,128)(2,1)S(1)}, bf16[2,72,896]{2,1,0:T(8,128)(2,1)S(1)}, u32[]{:S(2)}, u32[]{:S(2)}) collective-permute-start(bf16[2,72,896]{2,1,0:T(8,128)(2,1)S(1)} %pad_maximum_fusion.refs_9_.refs_0_), channel_id=1, source_target_pairs={{0,16},{1,3},{2,18},{3,1},{16,0},{17,19},{18,2},{19,17},{4,20},{5,... | collective-permute-start | bytes 774152 | tf_op jit(solution)/shard_map/ppermute | solution.py:456
  20.7 10.5 %collective-permute-start.10 = (bf16[2,72,896]{2,1,0:T(8,128)(2,1)S(1)}, bf16[2,72,896]{2,1,0:T(8,128)(2,1)S(1)}, u32[]{:S(2)}, u32[]{:S(2)}) collective-permute-start(bf16[2,72,896]{2,1,0:T(8,128)(2,1)S(1)} %pad_maximum_fusion.refs_9_.refs_0_), channel_id=1, source_target_pairs={{0,1},{1,0},{2,3},{3,2},{4,5},{5,4},{6,7},{7,6},{8,9},{9,8},{10,11... | collective-permute-start | bytes 774152 | tf_op jit(solution)/shard_map/ppermute | solution.py:416
  20.8 5.8 %copy-start.4 = (s32[8]{0:T(128)S(1)}, s32[8]{0:T(128)}, u32[]{:S(2)}) copy-start(s32[8]{0:T(128)} %param.20) | copy-start | bytes 100
  20.8 10.4 %copy-start.1 = (bf16[896,576]{0,1:T(8,128)(2,1)S(1)}, bf16[896,576]{0,1:T(8,128)(2,1)}, u32[]{:S(2)}) copy-start(bf16[896,576]{0,1:T(8,128)(2,1)} %param.15) | copy-start | bytes 3096580
  20.8 10.4 %copy-start.3 = (bf16[128,3584]{1,0:T(8,128)(2,1)S(1)}, bf16[128,3584]{1,0:T(8,128)(2,1)}, u32[]{:S(2)}) copy-start(bf16[128,3584]{1,0:T(8,128)(2,1)} %tokens_ref.1) | copy-start | bytes 2752516
  26.0 5.2 %collective-permute-start.11 = (bf16[2,72,896]{2,1,0:T(8,128)(2,1)S(1)}, bf16[2,72,896]{2,1,0:T(8,128)(2,1)S(1)}, u32[]{:S(2)}, u32[]{:S(2)}) collective-permute-start(bf16[2,72,896]{2,1,0:T(8,128)(2,1)S(1)} %collective-permute-done.6.refs_1_), channel_id=1, source_target_pairs={{0,1},{1,0},{2,3},{3,2},{4,5},{5,4},{6,7},{7,6},{8,9},{9,8},{10,11... | collective-permute-start | bytes 774152 | tf_op jit(solution)/shard_map/ppermute | solution.py:416
  26.6 9.8 %collective-permute-start.9 = (bf16[8,6016]{1,0:T(8,128)(2,1)S(1)}, bf16[8,6016]{1,0:T(8,128)(2,1)S(1)}, u32[]{:S(2)}, u32[]{:S(2)}) collective-permute-start(bf16[8,6016]{1,0:T(8,128)(2,1)S(1)} %get-tuple-element.43), channel_id=1, source_target_pairs={{0,8},{4,12},{8,0},{12,4},{1,9},{5,13},{9,1},{13,5},{2,10},{6,14},... | collective-permute-start | bytes 288776 | tf_op jit(solution)/shard_map/ppermute | solution.py:416
  29.7 4.4 %collective-permute-start.8 = (bf16[8,3584]{1,0:T(8,128)(2,1)S(1)}, bf16[8,3584]{1,0:T(8,128)(2,1)S(1)}, u32[]{:S(2)}, u32[]{:S(2)}) collective-permute-start(bf16[8,3584]{1,0:T(8,128)(2,1)S(1)} %get-tuple-element.41), channel_id=1, source_target_pairs={{0,4},{4,0},{8,12},{12,8},{1,5},{5,1},{9,13},{13,9},{2,6},{6,2},{1... | collective-permute-start | bytes 172040 | tf_op jit(solution)/shard_map/ppermute | solution.py:416
  30.9 7.4 %collective-permute-start.7 = (bf16[8,6016]{1,0:T(8,128)(2,1)S(1)}, bf16[8,6016]{1,0:T(8,128)(2,1)S(1)}, u32[]{:S(2)}, u32[]{:S(2)}) collective-permute-start(bf16[8,6016]{1,0:T(8,128)(2,1)S(1)} %get-tuple-element.39), channel_id=1, source_target_pairs={{0,12},{4,8},{8,4},{12,0},{1,13},{5,9},{9,5},{13,1},{2,14},{6,10},... | collective-permute-start | bytes 288776 | tf_op jit(solution)/shard_map/ppermute | solution.py:416
  32.2 7.9 %collective-permute-start.12 = (bf16[576,128]{1,0:T(8,128)(2,1)S(1)}, bf16[576,128]{1,0:T(8,128)(2,1)S(1)}, u32[]{:S(2)}, u32[]{:S(2)}) collective-permute-start(bf16[576,128]{1,0:T(8,128)(2,1)S(1)} %get-tuple-element.49), channel_id=1, source_target_pairs={{0,4},{4,0},{8,12},{12,8},{1,5},{5,1},{9,13},{13,9},{2,6},{6,2},{1... | collective-permute-start | bytes 442376 | tf_op jit(solution)/shard_map/ppermute | solution.py:416
  38.4 1.7 %copy-start.2 = (f32[512]{0:T(512)S(1)}, f32[512]{0:T(512)}, u32[]{:S(2)}) copy-start(f32[512]{0:T(512)} %param.16) | copy-start | bytes 6148

commit v6 on v5

--- a/solution.py
+++ b/solution.py
@@ -21,7 +21,7 @@
 VMEM = pltpu.VMEM
 SMEM = pltpu.SMEM
 CHUNK = 512
-PIECES = 4
+PIECES = 7
 ORDER = (0, 3, 1, 2)
 NT = (((1,), (1,)), ((), ()))
 TN = (((0,), (0,)), ((), ()))
@@ -264,18 +264,20 @@
         [parts[0]] + [row.at[:, model_width:] for row in (parts[1], rows[2], rows[3])]
     )
     row_count = arrivals.shape[0]
-    slot = lax.broadcasted_iota(jnp.int32, (row_count, page_count), 1).astype(jnp.float32)
-    part_of = lax.broadcasted_iota(jnp.int32, (row_count, page_count), 0) % SPLIT
-    meant = arrivals[:, part_width:].astype(jnp.float32)[:, :1] == slot + 1.0
+    column = lax.broadcasted_iota(jnp.int32, (row_count, SPLIT * page_count), 1)
+    slot = (column % page_count + 1).astype(jnp.float32)
+    part_of = lax.broadcasted_iota(jnp.int32, (row_count, SPLIT * page_count), 0) % SPLIT
+    meant = arrivals[:, part_width:].astype(jnp.float32)[:, :1] == slot
+    chosen = lax.dot_general(
+        jnp.where(meant & (part_of == column // page_count), 1.0, 0.0).astype(jnp.bfloat16),
+        arrivals[:, :part_width],
+        TN,
+        preferred_element_type=jnp.float32,
+    )
     for part in range(SPLIT):
-        chosen = lax.dot_general(
-            jnp.where(meant & (part_of == part), 1.0, 0.0).astype(jnp.bfloat16),
-            arrivals[:, :part_width],
-            TN,
-            preferred_element_type=jnp.float32,
-        )
         columns = slice(part * part_width, (part + 1) * part_width)
-        carried_ref[:, columns] = chosen.astype(jnp.bfloat16)
+        rows = slice(part * page_count, (part + 1) * page_count)
+        carried_ref[:, columns] = chosen[rows].astype(jnp.bfloat16)
     for copy in copies:
         copy.wait()
 

time: 41.4 us -> 41.4 us (level)
  no operation moved by 1% of the time
where the time goes in v6:
time: 41.4 us; the launch traced here: 41.2 us
  starting transfers between devices  19 us (46%)
  Pallas kernels  12.3 us (30%)
  waiting for transfers between devices  7.2 us (17%)
  local copies, waits for them, and re-layouts  0.98 us (2%)
  between operations  0.88 us (2%)
  other arithmetic  0.79 us (2%)
    ppermute x11, starting transfers between devices, swap(): return lax.ppermute(value, axis, xor_pairs(lax.axis_size(axis), bit))  15.8 us
    ppermute x11, waiting for transfers between devices, swap(): return lax.ppermute(value, axis, xor_pairs(lax.axis_size(axis), bit))  7.19 us
    pallas_call x1, Pallas kernels, experts(): pl.pallas_call(expert_kernel, out_shape=tuple((jax.ShapeDtypeStruct((CAP,...  5.18 us
    pallas_call x1, Pallas kernels, gates(): pl.pallas_call(gate_kernel, out_shape=jax.ShapeDtypeStruct((row_count, un...  2.63 us
    pallas_call x1, Pallas kernels, open_work(): pl.pallas_call(functools.partial(open_kernel, page_count * lax.axis_size(...  2.02 us
    ppermute x1, starting transfers between devices, block_shards(): far = lax.ppermute(near, plane, plane_pairs(group_count, dp_count, False))  1.73 us
    ppermute x1, starting transfers between devices, block_shards(): lax.ppermute(far_piece, plane, plane_pairs(group_count, dp_count, True))  1.5 us
    pallas_call x1, Pallas kernels, combine(): pl.pallas_call(combine_kernel, out_shape=(jax.ShapeDtypeStruct((token_cou...  1.2 us
  transfers between devices with their start and end apart: 13, of which 5 were waited for; matrix products, arithmetic and copies ran while one was open for 0% of the time, Pallas kernels for 29%

profile of v6, /device:TPU:0, one launch (start us, length us, event | category | flops | bytes accessed | tf_op | source)
XLA Modules:
  0.0 41.2 jit_solution(10197349509478208560)
XLA Ops:
  0.7 0.9 %dynamic-slice_bitcast_fusion = bf16[72,896]{1,0:T(8,128)(2,1)S(1)} fusion(bf16[896,576]{0,1:T(8,128)(2,1)} %param.15, s32[]{:T(128)S(6)} %select_n.20), kind=kLoop, calls=%fused_computation.2 | loop fusion | bytes 258052 | tf_op jit(solution)/shard_map/dynamic_slice | solution.py:448
  1.6 4.1 %collective-permute-start.3 = (bf16[72,896]{1,0:T(8,128)(2,1)S(1)}, bf16[72,896]{1,0:T(8,128)(2,1)S(1)}, u32[]{:S(2)}, u32[]{:S(2)}) collective-permute-start(bf16[72,896]{1,0:T(8,128)(2,1)S(1)} %dynamic-slice_bitcast_fusion), channel_id=1, source_target_pairs={{0,8},{4,12},{8,0},{12,4},{1,9},{5,13},{9,1},{13,5},{2,10},{6,14},... | collective-permute-start | bytes 387080 | tf_op jit(solution)/shard_map/ppermute | solution.py:418
  5.7 0.0 slice-start
  5.7 0.0 slice-start.4
  5.7 0.0 copy-start
  5.7 0.0 slice-start.1
  5.7 0.0 slice-start.2
  5.7 0.0 slice-start.3
  5.7 0.0 slice-start.5
  5.7 0.0 slice-start.6
  5.7 0.0 slice-start.7
  5.7 2.0 %open.1 = (bf16[8,3584]{1,0:T(8,128)(2,1)S(1)}, bf16[8,6016]{1,0:T(8,128)(2,1)S(1)}, bf16[8,3584]{1,0:T(8,128)(2,1)S(1)}, bf16[8,3584]{1,0:T(8,128)(2,1)S(1)}, f...) custom-call(s32[8,128]{1,0:T(8,128)} %bitcast.16, ...), custom_call_target="tpu_custom_call" | custom-call | flops 20000000000 | bytes 2097152 | tf_op jit(solution)/shard_map/open/pallas_call | solution.py:140
  7.8 1.6 %collective-permute-start = (bf16[8,6016]{1,0:T(8,128)(2,1)S(1)}, bf16[8,6016]{1,0:T(8,128)(2,1)S(1)}, u32[]{:S(2)}, u32[]{:S(2)}) collective-permute-start(bf16[8,6016]{1,0:T(8,128)(2,1)S(1)} %get-tuple-element.28), channel_id=1, source_target_pairs={{0,4},{4,0},{8,12},{12,8},{1,5},{5,1},{9,13},{13,9},{2,6},{6,2},{1... | collective-permute-start | bytes 288776 | tf_op jit(solution)/shard_map/ppermute | solution.py:418
  9.4 0.3 collective-permute-start.1
  9.7 2.5 %collective-permute-start.2 = (bf16[8,3584]{1,0:T(8,128)(2,1)S(1)}, bf16[8,3584]{1,0:T(8,128)(2,1)S(1)}, u32[]{:S(2)}, u32[]{:S(2)}) collective-permute-start(bf16[8,3584]{1,0:T(8,128)(2,1)S(1)} %get-tuple-element.30), channel_id=1, source_target_pairs={{0,12},{4,8},{8,4},{12,0},{1,13},{5,9},{9,5},{13,1},{2,14},{6,10},... | collective-permute-start | bytes 172040 | tf_op jit(solution)/shard_map/ppermute | solution.py:418
  12.2 0.0 collective-permute-done.3.refs_5_
  12.2 1.5 %collective-permute-start.4 = (bf16[72,896]{1,0:T(8,128)(2,1)S(1)}, bf16[72,896]{1,0:T(8,128)(2,1)S(1)}, u32[]{:S(2)}, u32[]{:S(2)}) collective-permute-start(bf16[72,896]{1,0:T(8,128)(2,1)S(1)} %collective-permute-done.3.refs_5_), channel_id=1, source_target_pairs={{0,2},{1,17},{2,0},{3,19},{16,18},{17,1},{18,16},{19,3},{4,6},{5,2... | collective-permute-start | bytes 387080 | tf_op jit(solution)/shard_map/ppermute | solution.py:454
  13.7 1.5 %collective-permute-start.5 = (bf16[128,1792]{1,0:T(8,128)(2,1)S(1)}, bf16[128,1792]{1,0:T(8,128)(2,1)S(1)}, u32[]{:S(2)}, u32[]{:S(2)}) collective-permute-start(bf16[128,1792]{1,0:T(8,128)(2,1)S(1)} %get-tuple-element.36), channel_id=1, source_target_pairs={{0,4},{4,0},{8,12},{12,8},{1,5},{5,1},{9,13},{13,9},{2,6},{6,2},{1... | collective-permute-start | bytes 1376264 | tf_op jit(solution)/shard_map/ppermute | solution.py:418
  15.2 1.1 %collective-permute-done.1.refs_2_ = bf16[8,3584]{1,0:T(8,128)(2,1)S(1)} collective-permute-done((bf16[8,3584]{1,0:T(8,128)(2,1)S(1)}, bf16[8,3584]{1,0:T(8,128)(2,1)S(1)}, u32[]{:S(2)}, u32[]{:S(2)}) %collective-permute-start.1) | collective-permute-done | bytes 57376 | tf_op jit(solution)/shard_map/ppermute | solution.py:418
  16.3 0.0 collective-permute-done.2.refs_3_
  16.3 0.0 collective-permute-done.refs_1_.refs_5_
  16.3 0.0 copy-done
  16.3 2.6 %gates.1.refs_4_ = f32[32,2048]{1,0:T(8,128)S(1)} custom-call(bf16[8,3584]{1,0:T(8,128)(2,1)S(1)} %get-tuple-element.27.refs_0_, bf16[8,6016]{1,0:T(8,128)(2,1)S(1)} %collective-permute-done.refs_1_.refs_5_, bf16[8,3584]{1,0:T(8,128)(2,1)S(1)} %collective-permute-done.1.refs_2_, bf16[8,3584]{1,0:T(8,128)(2,1)S(1)} %collective-permute-done.2.refs_3_, ...), custom_call_target="tpu_custom_call" | custom-call | flops 939524096 | bytes 29360128 | tf_op jit(solution)/shard_map/gates/pallas_call | solution.py:180
  18.9 0.0 collective-permute-done.4
  19.0 1.7 %collective-permute-start.6 = (bf16[2,72,896]{2,1,0:T(8,128)(2,1)S(1)}, bf16[2,72,896]{2,1,0:T(8,128)(2,1)S(1)}, u32[]{:S(2)}, u32[]{:S(2)}) collective-permute-start(bf16[2,72,896]{2,1,0:T(8,128)(2,1)S(1)} %pad_maximum_fusion.refs_9_.refs_0_), channel_id=1, source_target_pairs={{0,16},{1,3},{2,18},{3,1},{16,0},{17,19},{18,2},{19,17},{4,20},{5,... | collective-permute-start | bytes 774152 | tf_op jit(solution)/shard_map/ppermute | solution.py:458
  20.7 0.0 collective-permute-start.10
  20.7 0.0 slice-done
  20.7 0.0 slice-done.4
  20.7 0.0 slice-done.1
  20.7 0.0 slice-done.2
  20.7 0.0 slice-done.3
  20.8 0.0 slice-done.5
  20.8 0.0 slice-done.6
  20.8 0.0 slice-done.7
  20.8 0.0 copy-start.4
  20.8 0.0 copy-start.1
  20.8 0.0 copy-start.3
  20.8 5.2 %experts.1 = (bf16[8,3584]{1,0:T(8,128)(2,1)S(1)}, bf16[8,3584]{1,0:T(8,128)(2,1)S(1)}, bf16[8,6016]{1,0:T(8,128)(2,1)S(1)}, bf16[8,6016]{1,0:T(8,128)(2,1)S(1)}) custom-call(bf16[8,3584]{1,0:T(8,128)(2,1)S(1)} %get-tuple-element.27.refs_0_, bf16[8,6016]{1,0:T(8,128)(2,1)S(1)} %collective-permute-done.refs_1_.refs_5_, ...), custom_call_target="tpu_custom_call" | custom-call | flops 469762048 | bytes 14680064 | tf_op jit(solution)/shard_map/experts/pallas_call | solution.py:223
  26.0 0.0 collective-permute-done.6.refs_1_
  26.0 0.0 collective-permute-done.5.theirs_ref
  26.0 0.6 %collective-permute-start.11 = (bf16[2,72,896]{2,1,0:T(8,128)(2,1)S(1)}, bf16[2,72,896]{2,1,0:T(8,128)(2,1)S(1)}, u32[]{:S(2)}, u32[]{:S(2)}) collective-permute-start(bf16[2,72,896]{2,1,0:T(8,128)(2,1)S(1)} %collective-permute-done.6.refs_1_), channel_id=1, source_target_pairs={{0,1},{1,0},{2,3},{3,2},{4,5},{5,4},{6,7},{7,6},{8,9},{9,8},{10,11... | collective-permute-start | bytes 774152 | tf_op jit(solution)/shard_map/ppermute | solution.py:418
  26.6 0.0 copy-done.4
  26.6 3.1 %collective-permute-start.9 = (bf16[8,6016]{1,0:T(8,128)(2,1)S(1)}, bf16[8,6016]{1,0:T(8,128)(2,1)S(1)}, u32[]{:S(2)}, u32[]{:S(2)}) collective-permute-start(bf16[8,6016]{1,0:T(8,128)(2,1)S(1)} %get-tuple-element.43), channel_id=1, source_target_pairs={{0,8},{4,12},{8,0},{12,4},{1,9},{5,13},{9,1},{13,5},{2,10},{6,14},... | collective-permute-start | bytes 288776 | tf_op jit(solution)/shard_map/ppermute | solution.py:418
  29.7 1.2 %collective-permute-start.8 = (bf16[8,3584]{1,0:T(8,128)(2,1)S(1)}, bf16[8,3584]{1,0:T(8,128)(2,1)S(1)}, u32[]{:S(2)}, u32[]{:S(2)}) collective-permute-start(bf16[8,3584]{1,0:T(8,128)(2,1)S(1)} %get-tuple-element.41), channel_id=1, source_target_pairs={{0,4},{4,0},{8,12},{12,8},{1,5},{5,1},{9,13},{13,9},{2,6},{6,2},{1... | collective-permute-start | bytes 172040 | tf_op jit(solution)/shard_map/ppermute | solution.py:418
  30.9 0.3 collective-permute-start.7
  31.2 0.0 collective-permute-done.10.refs_2_
  31.2 0.0 collective-permute-done.11.refs_3_
  31.2 0.0 copy-done.1
  31.3 0.0 copy-done.3
  31.3 0.9 %project.1 = (f32[576,128]{1,0:T(8,128)S(1)}, bf16[576,128]{1,0:T(8,128)(2,1)S(1)}) custom-call(bf16[128,3584]{1,0:T(8,128)(2,1)S(1)} %copy-done.3, bf16[128,1792]{1,0:T(8,128)(2,1)S(1)} %collective-permute-done.5.theirs_ref, bf16[576,896]{1,0:T(8,128)(2,1)S(1)} %bitcast.13, bf16[2,72,896]{2,1,0:T(8,128)(2,1)S(1)} %pad_maximum_fusion.refs_9_.refs_0_, ...), custom_call_target="tpu_custom_call" | custom-call | flops 1152999936 | tf_op jit(solution)/shard_map/project/pallas_call | solution.py:352
  32.2 0.6 %collective-permute-start.12 = (bf16[576,128]{1,0:T(8,128)(2,1)S(1)}, bf16[576,128]{1,0:T(8,128)(2,1)S(1)}, u32[]{:S(2)}, u32[]{:S(2)}) collective-permute-start(bf16[576,128]{1,0:T(8,128)(2,1)S(1)} %get-tuple-element.49), channel_id=1, source_target_pairs={{0,4},{4,0},{8,12},{12,8},{1,5},{5,1},{9,13},{13,9},{2,6},{6,2},{1... | collective-permute-start | bytes 442376 | tf_op jit(solution)/shard_map/ppermute | solution.py:418
  32.8 1.3 %collective-permute-done.8.refs_2_ = bf16[8,3584]{1,0:T(8,128)(2,1)S(1)} collective-permute-done((bf16[8,3584]{1,0:T(8,128)(2,1)S(1)}, bf16[8,3584]{1,0:T(8,128)(2,1)S(1)}, u32[]{:S(2)}, u32[]{:S(2)}) %collective-permute-start.8) | collective-permute-done | bytes 57376 | tf_op jit(solution)/shard_map/ppermute | solution.py:418
  34.1 2.3 %collective-permute-done.9.refs_3_ = bf16[8,6016]{1,0:T(8,128)(2,1)S(1)} collective-permute-done((bf16[8,6016]{1,0:T(8,128)(2,1)S(1)}, bf16[8,6016]{1,0:T(8,128)(2,1)S(1)}, u32[]{:S(2)}, u32[]{:S(2)}) %collective-permute-start.9) | collective-permute-done | bytes 96288 | tf_op jit(solution)/shard_map/ppermute | solution.py:418
  36.4 1.9 %collective-permute-done.7.refs_1_ = bf16[8,6016]{1,0:T(8,128)(2,1)S(1)} collective-permute-done((bf16[8,6016]{1,0:T(8,128)(2,1)S(1)}, bf16[8,6016]{1,0:T(8,128)(2,1)S(1)}, u32[]{:S(2)}, u32[]{:S(2)}) %collective-permute-start.7) | collective-permute-done | bytes 96288 | tf_op jit(solution)/shard_map/ppermute | solution.py:418
  38.4 0.0 copy-start.2
  38.4 1.2 %combine.1 = (bf16[128,3584]{1,0:T(8,128)(2,1)}, bf16[8,9216]{1,0:T(8,128)(2,1)S(1)}) custom-call(f32[32,128]{1,0:T(8,128)S(1)} %get-tuple-element.26.mixing_ref, bf16[8,3584]{1,0:T(8,128)(2,1)S(1)} %get-tuple-element.37.refs_0_, bf16[8,6016]{1,0:T(8,128)(2,1)S(1)} %collective-permute-done.7.refs_1_, bf16[8,3584]{1,0:T(8,128)(2,1)S(1)} %collective-permute-done.8.refs_2_, ...), custom_call_target="tpu_custom_call" | custom-call | flops 11530000384 | bytes 1376256 | tf_op jit(solution)/shard_map/combine/pallas_call | solution.py:290
  39.6 0.5 %collective-permute-done.12.theirs_ref = bf16[576,128]{1,0:T(8,128)(2,1)S(1)} collective-permute-done((bf16[576,128]{1,0:T(8,128)(2,1)S(1)}, bf16[576,128]{1,0:T(8,128)(2,1)S(1)}, u32[]{:S(2)}, u32[]{:S(2)}) %collective-permute-start.12) | collective-permute-done | bytes 147488 | tf_op jit(solution)/shard_map/ppermute | solution.py:418
  40.1 0.0 copy-done.2
  40.1 0.4 finish.1
  40.5 0.7 %broadcast_select_fusion = bf16[8,9216]{1,0:T(8,128)(2,1)} fusion(bf16[8,9216]{1,0:T(8,128)(2,1)S(1)} %get-tuple-element.46.unread_ref, bf16[8,9216]{1,0:T(8,128)(2,1)S(1)} %finish.1, pred[8]{0:T(512)(128)(4,1)S(1)} %broadcast_compare_fusion), kind=kLoop, calls=%fused_computation.1 | loop fusion | flops 73728 | bytes 442376 | tf_op jit(solution)/shard_map/jit(_where)/select_n | solution.py:471
  (4 shorter events, 0.0 us)
Async XLA Ops:
  1.6 10.6 %collective-permute-start.3 = (bf16[72,896]{1,0:T(8,128)(2,1)S(1)}, bf16[72,896]{1,0:T(8,128)(2,1)S(1)}, u32[]{:S(2)}, u32[]{:S(2)}) collective-permute-start(bf16[72,896]{1,0:T(8,128)(2,1)S(1)} %dynamic-slice_bitcast_fusion), channel_id=1, source_target_pairs={{0,8},{4,12},{8,0},{12,4},{1,9},{5,13},{9,1},{13,5},{2,10},{6,14},... | collective-permute-start | bytes 387080 | tf_op jit(solution)/shard_map/ppermute | solution.py:418
  5.7 15.0 %slice-start = ((s8[14680064]{0:T(1024)(128)(4,1)}), s8[4194304]{0:T(1024)(128)(4,1)S(1)}, s32[]{:S(2)}) async-start(s8[14680064]{0:T(1024)(128)(4,1)} %bitcast.8), calls=%async_computation | async-start | bytes 8388608
  5.7 15.0 %slice-start.4 = ((s8[14680064]{0:T(1024)(128)(4,1)}), s8[4194304]{0:T(1024)(128)(4,1)S(1)}, s32[]{:S(2)}) async-start(s8[14680064]{0:T(1024)(128)(4,1)} %bitcast.10), calls=%async_computation.4 | async-start | bytes 8388608
  5.7 10.6 %copy-start = (bf16[3584,2048]{1,0:T(8,128)(2,1)S(1)}, bf16[3584,2048]{1,0:T(8,128)(2,1)}, u32[]{:S(2)}) copy-start(bf16[3584,2048]{1,0:T(8,128)(2,1)} %refs_4_.3) | copy-start | bytes 44040196
  5.7 15.0 %slice-start.1 = ((s8[14680064]{0:T(1024)(128)(4,1)}), s8[4194304]{0:T(1024)(128)(4,1)S(1)}, s32[]{:S(2)}) async-start(s8[14680064]{0:T(1024)(128)(4,1)} %bitcast.8), calls=%async_computation.1 | async-start | bytes 8388608
  5.7 15.0 %slice-start.2 = ((s8[14680064]{0:T(1024)(128)(4,1)}), s8[4194304]{0:T(1024)(128)(4,1)S(1)}, s32[]{:S(2)}) async-start(s8[14680064]{0:T(1024)(128)(4,1)} %bitcast.8), calls=%async_computation.2 | async-start | bytes 8388608
  5.7 15.0 %slice-start.3 = ((s8[14680064]{0:T(1024)(128)(4,1)}), s8[2097152]{0:T(1024)(128)(4,1)S(1)}, s32[]{:S(2)}) async-start(s8[14680064]{0:T(1024)(128)(4,1)} %bitcast.8), calls=%async_computation.3 | async-start | bytes 4194304
  5.7 15.0 %slice-start.5 = ((s8[14680064]{0:T(1024)(128)(4,1)}), s8[4194304]{0:T(1024)(128)(4,1)S(1)}, s32[]{:S(2)}) async-start(s8[14680064]{0:T(1024)(128)(4,1)} %bitcast.10), calls=%async_computation.5 | async-start | bytes 8388608
  5.7 15.0 %slice-start.6 = ((s8[14680064]{0:T(1024)(128)(4,1)}), s8[4194304]{0:T(1024)(128)(4,1)S(1)}, s32[]{:S(2)}) async-start(s8[14680064]{0:T(1024)(128)(4,1)} %bitcast.10), calls=%async_computation.6 | async-start | bytes 8388608
  5.7 15.0 %slice-start.7 = ((s8[14680064]{0:T(1024)(128)(4,1)}), s8[2097152]{0:T(1024)(128)(4,1)S(1)}, s32[]{:S(2)}) async-start(s8[14680064]{0:T(1024)(128)(4,1)} %bitcast.10), calls=%async_computation.7 | async-start | bytes 4194304
  7.8 8.5 %collective-permute-start = (bf16[8,6016]{1,0:T(8,128)(2,1)S(1)}, bf16[8,6016]{1,0:T(8,128)(2,1)S(1)}, u32[]{:S(2)}, u32[]{:S(2)}) collective-permute-start(bf16[8,6016]{1,0:T(8,128)(2,1)S(1)} %get-tuple-element.28), channel_id=1, source_target_pairs={{0,4},{4,0},{8,12},{12,8},{1,5},{5,1},{9,13},{13,9},{2,6},{6,2},{1... | collective-permute-start | bytes 288776 | tf_op jit(solution)/shard_map/ppermute | solution.py:418
  9.4 6.9 %collective-permute-start.1 = (bf16[8,3584]{1,0:T(8,128)(2,1)S(1)}, bf16[8,3584]{1,0:T(8,128)(2,1)S(1)}, u32[]{:S(2)}, u32[]{:S(2)}) collective-permute-start(bf16[8,3584]{1,0:T(8,128)(2,1)S(1)} %get-tuple-element.29), channel_id=1, source_target_pairs={{0,8},{4,12},{8,0},{12,4},{1,9},{5,13},{9,1},{13,5},{2,10},{6,14},... | collective-permute-start | bytes 172040 | tf_op jit(solution)/shard_map/ppermute | solution.py:418
  9.7 6.5 %collective-permute-start.2 = (bf16[8,3584]{1,0:T(8,128)(2,1)S(1)}, bf16[8,3584]{1,0:T(8,128)(2,1)S(1)}, u32[]{:S(2)}, u32[]{:S(2)}) collective-permute-start(bf16[8,3584]{1,0:T(8,128)(2,1)S(1)} %get-tuple-element.30), channel_id=1, source_target_pairs={{0,12},{4,8},{8,4},{12,0},{1,13},{5,9},{9,5},{13,1},{2,14},{6,10},... | collective-permute-start | bytes 172040 | tf_op jit(solution)/shard_map/ppermute | solution.py:418
  12.2 6.7 %collective-permute-start.4 = (bf16[72,896]{1,0:T(8,128)(2,1)S(1)}, bf16[72,896]{1,0:T(8,128)(2,1)S(1)}, u32[]{:S(2)}, u32[]{:S(2)}) collective-permute-start(bf16[72,896]{1,0:T(8,128)(2,1)S(1)} %collective-permute-done.3.refs_5_), channel_id=1, source_target_pairs={{0,2},{1,17},{2,0},{3,19},{16,18},{17,1},{18,16},{19,3},{4,6},{5,2... | collective-permute-start | bytes 387080 | tf_op jit(solution)/shard_map/ppermute | solution.py:454
  13.7 12.3 %collective-permute-start.5 = (bf16[128,1792]{1,0:T(8,128)(2,1)S(1)}, bf16[128,1792]{1,0:T(8,128)(2,1)S(1)}, u32[]{:S(2)}, u32[]{:S(2)}) collective-permute-start(bf16[128,1792]{1,0:T(8,128)(2,1)S(1)} %get-tuple-element.36), channel_id=1, source_target_pairs={{0,4},{4,0},{8,12},{12,8},{1,5},{5,1},{9,13},{13,9},{2,6},{6,2},{1... | collective-permute-start | bytes 1376264 | tf_op jit(solution)/shard_map/ppermute | solution.py:418
  19.0 7.0 %collective-permute-start.6 = (bf16[2,72,896]{2,1,0:T(8,128)(2,1)S(1)}, bf16[2,72,896]{2,1,0:T(8,128)(2,1)S(1)}, u32[]{:S(2)}, u32[]{:S(2)}) collective-permute-start(bf16[2,72,896]{2,1,0:T(8,128)(2,1)S(1)} %pad_maximum_fusion.refs_9_.refs_0_), channel_id=1, source_target_pairs={{0,16},{1,3},{2,18},{3,1},{16,0},{17,19},{18,2},{19,17},{4,20},{5,... | collective-permute-start | bytes 774152 | tf_op jit(solution)/shard_map/ppermute | solution.py:458
  20.7 10.5 %collective-permute-start.10 = (bf16[2,72,896]{2,1,0:T(8,128)(2,1)S(1)}, bf16[2,72,896]{2,1,0:T(8,128)(2,1)S(1)}, u32[]{:S(2)}, u32[]{:S(2)}) collective-permute-start(bf16[2,72,896]{2,1,0:T(8,128)(2,1)S(1)} %pad_maximum_fusion.refs_9_.refs_0_), channel_id=1, source_target_pairs={{0,1},{1,0},{2,3},{3,2},{4,5},{5,4},{6,7},{7,6},{8,9},{9,8},{10,11... | collective-permute-start | bytes 774152 | tf_op jit(solution)/shard_map/ppermute | solution.py:418
  20.8 5.8 %copy-start.4 = (s32[8]{0:T(128)S(1)}, s32[8]{0:T(128)}, u32[]{:S(2)}) copy-start(s32[8]{0:T(128)} %param.20) | copy-start | bytes 100
  20.8 10.4 %copy-start.1 = (bf16[896,576]{0,1:T(8,128)(2,1)S(1)}, bf16[896,576]{0,1:T(8,128)(2,1)}, u32[]{:S(2)}) copy-start(bf16[896,576]{0,1:T(8,128)(2,1)} %param.15) | copy-start | bytes 3096580
  20.8 10.4 %copy-start.3 = (bf16[128,3584]{1,0:T(8,128)(2,1)S(1)}, bf16[128,3584]{1,0:T(8,128)(2,1)}, u32[]{:S(2)}) copy-start(bf16[128,3584]{1,0:T(8,128)(2,1)} %tokens_ref.1) | copy-start | bytes 2752516
  26.0 5.2 %collective-permute-start.11 = (bf16[2,72,896]{2,1,0:T(8,128)(2,1)S(1)}, bf16[2,72,896]{2,1,0:T(8,128)(2,1)S(1)}, u32[]{:S(2)}, u32[]{:S(2)}) collective-permute-start(bf16[2,72,896]{2,1,0:T(8,128)(2,1)S(1)} %collective-permute-done.6.refs_1_), channel_id=1, source_target_pairs={{0,1},{1,0},{2,3},{3,2},{4,5},{5,4},{6,7},{7,6},{8,9},{9,8},{10,11... | collective-permute-start | bytes 774152 | tf_op jit(solution)/shard_map/ppermute | solution.py:418
  26.6 9.8 %collective-permute-start.9 = (bf16[8,6016]{1,0:T(8,128)(2,1)S(1)}, bf16[8,6016]{1,0:T(8,128)(2,1)S(1)}, u32[]{:S(2)}, u32[]{:S(2)}) collective-permute-start(bf16[8,6016]{1,0:T(8,128)(2,1)S(1)} %get-tuple-element.43), channel_id=1, source_target_pairs={{0,8},{4,12},{8,0},{12,4},{1,9},{5,13},{9,1},{13,5},{2,10},{6,14},... | collective-permute-start | bytes 288776 | tf_op jit(solution)/shard_map/ppermute | solution.py:418
  29.7 4.4 %collective-permute-start.8 = (bf16[8,3584]{1,0:T(8,128)(2,1)S(1)}, bf16[8,3584]{1,0:T(8,128)(2,1)S(1)}, u32[]{:S(2)}, u32[]{:S(2)}) collective-permute-start(bf16[8,3584]{1,0:T(8,128)(2,1)S(1)} %get-tuple-element.41), channel_id=1, source_target_pairs={{0,4},{4,0},{8,12},{12,8},{1,5},{5,1},{9,13},{13,9},{2,6},{6,2},{1... | collective-permute-start | bytes 172040 | tf_op jit(solution)/shard_map/ppermute | solution.py:418
  30.9 7.4 %collective-permute-start.7 = (bf16[8,6016]{1,0:T(8,128)(2,1)S(1)}, bf16[8,6016]{1,0:T(8,128)(2,1)S(1)}, u32[]{:S(2)}, u32[]{:S(2)}) collective-permute-start(bf16[8,6016]{1,0:T(8,128)(2,1)S(1)} %get-tuple-element.39), channel_id=1, source_target_pairs={{0,12},{4,8},{8,4},{12,0},{1,13},{5,9},{9,5},{13,1},{2,14},{6,10},... | collective-permute-start | bytes 288776 | tf_op jit(solution)/shard_map/ppermute | solution.py:418
  32.2 7.9 %collective-permute-start.12 = (bf16[576,128]{1,0:T(8,128)(2,1)S(1)}, bf16[576,128]{1,0:T(8,128)(2,1)S(1)}, u32[]{:S(2)}, u32[]{:S(2)}) collective-permute-start(bf16[576,128]{1,0:T(8,128)(2,1)S(1)} %get-tuple-element.49), channel_id=1, source_target_pairs={{0,4},{4,0},{8,12},{12,8},{1,5},{5,1},{9,13},{13,9},{2,6},{6,2},{1... | collective-permute-start | bytes 442376 | tf_op jit(solution)/shard_map/ppermute | solution.py:418
  38.4 1.7 %copy-start.2 = (f32[512]{0:T(512)S(1)}, f32[512]{0:T(512)}, u32[]{:S(2)}) copy-start(f32[512]{0:T(512)} %param.16) | copy-start | bytes 6148
